TPU v7x, 128 devices: a whole 4x4x4 slice. The times are simulated.
128 devices in a mesh: space: 32 (over z_hi, y, x), band: 4 (over z_lo, core).
Axes of the slice: x: 4, y: 4, z: 4 (z_hi: 2, z_lo: 2; z = z_hi * 2 + z_lo), core: 2. Of those that a mesh axis runs over, the one named last changes fastest.
Arguments:
- wavefunctions: float32 [256, 324000], P('band', 'space'), may hold values from -6 to 6
- stiffness: float32 [125, 125], replicated, as said below
- cell_scale: float32 [3840], P('space'), may hold values from 0.5 to 2
- cell_potential: float32 [3840], P('space'), may hold values from 0.5 to 4
- connectivity: int32 [125, 3840], P(None, 'space'), may hold values from 0 to 10124, as said below
- lower_face: int32 [64800], P('space'), may hold values from 0 to 10124, as said below
- upper_face: int32 [64800], P('space'), may hold values from 0 to 10124, as said below
Outputs:
- rotated_waves: float32 [256, 324000], P('band', 'space')
Inputs may be any that keep to these rules, and one draw needn't show every extreme that they name: `connectivity`: each column of a device's block lists the 125 distinct local nodes of one cell of a structured degree-4 hexahedral grid of 1 x 20 x 6 cells whose nodes are numbered in an arbitrary order; every local node belongs to some cell. A device's lower_face lists the 2025 distinct local nodes on its face towards the device below; the lists of one device are disjoint from each other. A device's upper_face lists the 2025 distinct local nodes on its face towards the device above, entry i being the same slab node as entry i of the next device's lower_face. `stiffness`: symmetric with a dominant diagonal.
All inputs are finite; a program needn't handle non-finite values.
Results may differ from a plain program's by a relative error of at most 0.00012.
Values sent between devices are 32-bit elements; how exact they have to be, the bound alone decides.
A program may use at most 128 MiB of HBM per device.

v0:
```python
import jax
import jax.numpy as jnp
from jax import lax
from jax.sharding import PartitionSpec as P

FILTER_DEG = 4


GLL_WEIGHTS = (0.1, 49.0 / 90.0, 32.0 / 45.0, 49.0 / 90.0, 0.1)
CENTER = 11.0
HALF_WIDTH = 9.0
HIGHEST = lax.Precision.HIGHEST


def from_behind(value, axis, steps):
    count = lax.axis_size(axis)
    initial, last = (max(0, -steps), min(count, count - steps))
    return lax.ppermute(value, axis, [(source, source + steps) for source in range(initial, last)])


def lumped_mass():
    weights = jnp.array(GLL_WEIGHTS, jnp.float32)
    return (weights[:, None, None] * weights[None, :, None] * weights[None, None, :]).reshape(-1)


def cell_apply(values, connectivity, cell_scale, cell_potential, stiffness):
    gathered = jnp.take(values, connectivity, axis=1)
    stiff_part = jnp.einsum("lm,bmc->blc", stiffness, gathered, precision=HIGHEST)
    products = stiff_part * cell_scale + lumped_mass()[:, None] * cell_potential * gathered
    return jnp.zeros_like(values).at[:, connectivity].add(products)


def inverse_factor(margin, order):
    factor = jnp.linalg.cholesky(margin)
    return lax.linalg.triangular_solve(
        factor, jnp.eye(order, dtype=margin.dtype), left_side=True, lower=True
    )


def shards(
    wavefunctions, stiffness, cell_scale, cell_potential, connectivity, lower_face, upper_face
):
    width, node_count = wavefunctions.shape
    face_count = lower_face.shape[0]
    space_count = lax.axis_size("space")
    band_count = lax.axis_size("band")
    total_bands = width * band_count
    owned_count = node_count * space_count - face_count * (space_count - 1)
    inner = lax.axis_index("space") > 0

    def operate(values):
        summed = cell_apply(values, connectivity, cell_scale, cell_potential, stiffness)
        upward = summed[:, upper_face]
        downward = summed[:, lower_face]
        from_lower = from_behind(upward, "space", 1)
        from_upper = from_behind(downward, "space", -1)
        summed = summed.at[:, lower_face].add(from_lower)
        return summed.at[:, upper_face].add(from_upper)

    owner = from_behind(wavefunctions[:, upper_face], "space", 1)
    values = wavefunctions.at[:, lower_face].set(
        jnp.where(inner, owner, wavefunctions[:, lower_face])
    )
    previous = values
    current = (operate(values) - CENTER * values) / HALF_WIDTH
    for repeat in range(FILTER_DEG - 1):
        following = 2.0 / HALF_WIDTH * (operate(current) - CENTER * current) - previous
        previous, current = (current, following)
    keeping = jnp.where(inner, 0.0, 1.0).astype(jnp.float32)
    weights = jnp.ones((node_count,), jnp.float32).at[lower_face].multiply(keeping)
    weighted = current * weights
    blocks = jnp.einsum(
        "bn,kn->bk",
        weighted,
        lax.all_gather(current, "band", axis=0, tiled=True),
        precision=HIGHEST,
    )
    row_panel = blocks
    row_panel = lax.psum(row_panel, "space")
    margin = lax.all_gather(row_panel, "band", axis=0, tiled=True) / owned_count
    inverse = inverse_factor(margin, total_bands)
    my_panel = lax.dynamic_slice_in_dim(inverse, lax.axis_index("band") * width, width, 0)
    return jnp.dot(my_panel, lax.all_gather(current, "band", axis=0, tiled=True), precision=HIGHEST)


def solution(mesh):
    placed = (
        P("band", "space"),
        P(),
        P("space"),
        P("space"),
        P(None, "space"),
        P("space"),
        P("space"),
    )
    return jax.shard_map(
        shards, mesh=mesh, in_specs=placed, out_specs=P("band", "space"), check_vma=False
    )
```

profile of v0, /device:TPU:1, one launch (start us, length us, event | category | flops | bytes accessed | tf_op | source)
XLA Modules:
  0.0 1423.2 jit_solution(9018060151078027643)
XLA Ops:
  12.5 8.1 gather_fusion
  25.6 9.8 collective-permute-done
  35.8 24.3 %scatter_custom_fusion = f32[64,10125]{0,1:T(8,128)} fusion(f32[64,10125]{0,1:T(8,128)} %copy.48, s32[2025]{0:T(1024)S(1)} %compare_select_fusion.2, f32[64,2025]{0,1:T(8,128)S(1)} %copy.47, pred[]{:T(512)S(6)} %gt.3, s32[2048]{0:T(1024)S(1)} %pad_clamp_fusion.1), kind=kCustom, calls=%fused_computation.80 | custom fusion | flops 129600 | bytes 6232577 | tf_op jit(solution)/shard_map/scatter | solution.py:61
  60.1 30.8 %gather_fusion.9 = f32[15000,64]{1,0:T(8,128)} fusion(f32[64,10125]{0,1:T(8,128)} %scatter_custom_fusion, s32[15360]{0:T(1024)S(1)} %pad_clamp_fusion), kind=kCustom, calls=%fused_computation.clone | custom fusion | bytes 7740000 | tf_op jit(solution)/shard_map/jit(_take)/gather | solution.py:27
  91.0 8.7 copy.51
  107.7 9.1 copy.90
  116.8 85.0 %scatter_custom_fusion.1 = f32[64,10125]{0,1:T(8,128)} fusion(s32[15000]{0:T(1024)S(1)} %reshape.531, f32[15000,64]{1,0:T(8,128)} %bitcast.136, f32[]{:T(128)} %constant.107.clone.1), kind=kCustom, calls=%fused_computation.68 | custom fusion | flops 960000 | bytes 2592512 | tf_op jit(solution)/shard_map/scatter-add | solution.py:30
  201.9 8.1 gather_fusion.1
  214.4 8.1 gather_fusion.2
  224.4 15.8 %scatter_fusion = f32[64,10125]{0,1:T(8,128)} fusion(f32[64,10125]{0,1:T(8,128)} %scatter_custom_fusion.1, s32[2025]{0:T(1024)S(1)} %compare_select_fusion.2, f32[2025,64]{1,0:T(8,128)S(1)} %copy.55), kind=kCustom, calls=%fused_computation.16 | custom fusion | flops 129600 | bytes 1563300 | tf_op jit(solution)/shard_map/scatter-add | solution.py:57
  240.6 15.4 %scatter_fusion.1 = f32[64,10125]{0,1:T(8,128)} fusion(f32[64,10125]{0,1:T(8,128)} %scatter_fusion, s32[2025]{0:T(1024)S(1)} %compare_select_fusion.1, f32[2025,64]{1,0:T(8,128)S(1)} %copy.57), kind=kCustom, calls=%fused_computation.17 | custom fusion | flops 129600 | bytes 1563300 | tf_op jit(solution)/shard_map/scatter-add | solution.py:58
  262.3 31.0 %gather_fusion.10 = f32[15000,64]{1,0:T(8,128)} fusion(f32[64,10125]{0,1:T(8,128)} %fusion.2, s32[15360]{0:T(1024)S(1)} %pad_clamp_fusion), kind=kCustom, calls=%fused_computation.1.clone | custom fusion | bytes 7740000 | tf_op jit(solution)/shard_map/jit(_take)/gather | solution.py:27
  293.3 8.7 copy.60
  310.0 9.1 copy.93
  319.0 85.1 %scatter_custom_fusion.4 = f32[64,10125]{0,1:T(8,128)} fusion(s32[15000]{0:T(1024)S(1)} %reshape.531, f32[15000,64]{1,0:T(8,128)} %bitcast.137, f32[]{:T(128)} %constant.107.clone.1), kind=kCustom, calls=%fused_computation.66 | custom fusion | flops 960000 | bytes 2592512 | tf_op jit(solution)/shard_map/scatter-add | solution.py:30
  404.2 8.1 gather_fusion.3
  416.6 8.1 gather_fusion.4
  426.7 15.5 %scatter_fusion.2 = f32[64,10125]{0,1:T(8,128)} fusion(f32[64,10125]{0,1:T(8,128)} %scatter_custom_fusion.4, s32[2025]{0:T(1024)S(1)} %compare_select_fusion.2, f32[2025,64]{1,0:T(8,128)S(1)} %copy.64), kind=kCustom, calls=%fused_computation.19 | custom fusion | flops 129600 | bytes 1563300 | tf_op jit(solution)/shard_map/scatter-add | solution.py:57
  442.5 15.6 %scatter_fusion.3 = f32[64,10125]{0,1:T(8,128)} fusion(f32[64,10125]{0,1:T(8,128)} %scatter_fusion.2, s32[2025]{0:T(1024)S(1)} %compare_select_fusion.1, f32[2025,64]{1,0:T(8,128)S(1)} %copy.66), kind=kCustom, calls=%fused_computation.20 | custom fusion | flops 129600 | bytes 1563300 | tf_op jit(solution)/shard_map/scatter-add | solution.py:58
  458.1 8.5 multiply_subtract_fusion.2
  466.6 31.0 %gather_fusion.11 = f32[15000,64]{1,0:T(8,128)} fusion(f32[64,10125]{0,1:T(8,128)} %multiply_subtract_fusion.2, s32[15360]{0:T(1024)S(1)} %pad_clamp_fusion), kind=kCustom, calls=%fused_computation.2.clone | custom fusion | bytes 7740000 | tf_op jit(solution)/shard_map/jit(_take)/gather | solution.py:27
  497.6 8.7 copy.69
  514.2 9.1 copy.96
  523.3 85.2 %scatter_custom_fusion.7 = f32[64,10125]{0,1:T(8,128)} fusion(s32[15000]{0:T(1024)S(1)} %reshape.531, f32[15000,64]{1,0:T(8,128)} %bitcast.138, f32[]{:T(128)} %constant.107.clone.1), kind=kCustom, calls=%fused_computation.64 | custom fusion | flops 960000 | bytes 2592512 | tf_op jit(solution)/shard_map/scatter-add | solution.py:30
  608.5 8.1 gather_fusion.5
  620.9 8.1 gather_fusion.6
  630.9 15.9 %scatter_fusion.4 = f32[64,10125]{0,1:T(8,128)} fusion(f32[64,10125]{0,1:T(8,128)} %scatter_custom_fusion.7, s32[2025]{0:T(1024)S(1)} %compare_select_fusion.2, f32[2025,64]{1,0:T(8,128)S(1)} %copy.73), kind=kCustom, calls=%fused_computation.22 | custom fusion | flops 129600 | bytes 1563300 | tf_op jit(solution)/shard_map/scatter-add | solution.py:57
  647.2 15.5 %scatter_fusion.5 = f32[64,10125]{0,1:T(8,128)} fusion(f32[64,10125]{0,1:T(8,128)} %scatter_fusion.4, s32[2025]{0:T(1024)S(1)} %compare_select_fusion.1, f32[2025,64]{1,0:T(8,128)S(1)} %copy.75), kind=kCustom, calls=%fused_computation.23 | custom fusion | flops 129600 | bytes 1563300 | tf_op jit(solution)/shard_map/scatter-add | solution.py:58
  662.7 8.4 multiply_subtract_fusion.1
  671.0 31.0 %gather_fusion.12 = f32[15000,64]{1,0:T(8,128)} fusion(f32[64,10125]{0,1:T(8,128)} %multiply_subtract_fusion.1, s32[15360]{0:T(1024)S(1)} %pad_clamp_fusion), kind=kCustom, calls=%fused_computation.3.clone | custom fusion | bytes 7740000 | tf_op jit(solution)/shard_map/jit(_take)/gather | solution.py:27
  702.0 8.7 copy.78
  718.7 9.1 copy.99
  727.7 85.2 %scatter_custom_fusion.10 = f32[64,10125]{0,1:T(8,128)} fusion(s32[15000]{0:T(1024)S(1)} %reshape.531, f32[15000,64]{1,0:T(8,128)} %bitcast.135, f32[]{:T(128)} %constant.107.clone.1), kind=kCustom, calls=%fused_computation.62 | custom fusion | flops 960000 | bytes 2592512 | tf_op jit(solution)/shard_map/scatter-add | solution.py:30
  812.9 8.1 gather_fusion.7
  826.3 8.1 gather_fusion.8
  836.5 15.5 %scatter_fusion.6 = f32[64,10125]{0,1:T(8,128)} fusion(f32[64,10125]{0,1:T(8,128)} %scatter_custom_fusion.10, s32[2025]{0:T(1024)S(1)} %compare_select_fusion.2, f32[2025,64]{1,0:T(8,128)S(1)} %copy.82), kind=kCustom, calls=%fused_computation.25 | custom fusion | flops 129600 | bytes 1563300 | tf_op jit(solution)/shard_map/scatter-add | solution.py:57
  852.4 15.5 %scatter_fusion.7 = f32[64,10125]{0,1:T(8,128)} fusion(f32[64,10125]{0,1:T(8,128)} %scatter_fusion.6, s32[2025]{0:T(1024)S(1)} %compare_select_fusion.1, f32[2025,64]{1,0:T(8,128)S(1)} %copy.84), kind=kCustom, calls=%fused_computation.26 | custom fusion | flops 129600 | bytes 1563300 | tf_op jit(solution)/shard_map/scatter-add | solution.py:58
  867.9 8.4 multiply_subtract_fusion
  881.9 11.3 scatter_custom_fusion.13
  893.2 117.3 %all-gather.2.cloned.1.call-done = f32[256,10125]{1,0:T(8,128)} async-done(((f32[64,10125]{1,0:T(8,128)}), f32[256,10125]{1,0:T(8,128)}) %all-gather.2.cloned.1.call-update) | async-done | bytes 10368016 | tf_op jit(solution)/shard_map/all_gather | solution.py:75
  1010.5 15.1 %fusion = f32[64,256]{1,0:T(8,128)} fusion(f32[256,10125]{1,0:T(8,128)} %all-gather.2.cloned.1.call-done, f32[64,10125]{0,1:T(8,128)} %multiply_subtract_fusion, f32[10125]{0:T(1024)S(1)} %scatter_custom_fusion.13), kind=kOutput, calls=%fused_computation.30 | convolution fusion | flops 1991303936 | bytes 13066036 | tf_op jit(solution)/shard_map/bn,kn->bk/dot_general | solution.py:72
  1025.6 300.8 %all-reduce.3.cloned.1.call-done = f32[64,256]{1,0:T(8,128)} async-done(((f32[64,256]{1,0:T(8,128)}), f32[64,256]{1,0:T(8,128)}) %all-reduce.3.cloned.1.call-update) | async-done | bytes 65552 | tf_op jit(solution)/shard_map/psum | solution.py:79
  1326.4 16.9 %all_gather.8 = f32[256,256]{1,0:T(8,128)S(1)} all-gather(f32[64,256]{1,0:T(8,128)} %all-reduce.3.cloned.1.call-done), channel_id=1, replica_groups=mesh['space'=32,'band'=4] {'band'}, dimensions={0}, use_global_device_ids=true | all-gather | bytes 327680 | tf_op jit(solution)/shard_map/all_gather | solution.py:80
  1343.7 11.7 cholesky.50
  1355.4 9.8 custom-call.14
  1365.7 11.7 cholesky.105
  1383.5 19.7 %custom-call.15 = f32[2,128,128]{1,2,0:T(8,128)S(1)} custom-call(f32[2,128,128]{2,1,0:T(8,128)S(1)} %get-tuple-element.13), custom_call_target="InvertDiagBlocksLowerTriangular" | custom-call | tf_op jit(solution)/shard_map/triangular_solve | solution.py:35
  1404.1 11.9 fusion.51
  (98 shorter events, 93.2 us)
Async XLA Ops:
  6.5 93.2 %copy-start = (f32[125,125]{1,0:T(8,128)S(1)}, f32[125,125]{1,0:T(8,128)}, u32[]{:S(2)}) copy-start(f32[125,125]{1,0:T(8,128)} %param.14) | copy-start | bytes 187504
  6.5 1003.9 %all-gather.2.cloned.1.call-start = ((), (), s32[]{:S(2)}) async-start(), calls=%async_computation | async-start | bytes 13107200 | tf_op jit(solution)/shard_map/all_gather | solution.py:75
  7.3 17.6 %copy-start.3 = (s32[2025]{0:T(1024)S(1)}, s32[2025]{0:T(1024)}, u32[]{:S(2)}) copy-start(s32[2025]{0:T(1024)} %param.18) | copy-start | bytes 24304
  7.3 17.7 %copy-start.1 = (s32[125,120]{0,1:T(8,128)S(1)}, s32[125,120]{0,1:T(8,128)}, u32[]{:S(2)}) copy-start(s32[125,120]{0,1:T(8,128)} %param.17) | copy-start | bytes 180004
  12.5 12.7 copy-start.4
  12.5 12.9 copy-start.5
  20.9 14.5 %collective-permute-start = (f32[64,2025]{1,0:T(8,128)S(1)}, f32[64,2025]{1,0:T(8,128)S(1)}, u32[]{:S(2)}, u32[]{:S(2)}) collective-permute-start(f32[64,2025]{1,0:T(8,128)S(1)} %copy.45), channel_id=1, source_target_pairs={{0,4},{4,8},{8,12},{12,16},{16,20},{20,24},{24,28},{28,32},{32,36}... | collective-permute-start | bytes 1555208 | tf_op jit(solution)/shard_map/ppermute | solution.py:18
  91.0 8.8 copy-start.2
  210.2 13.8 collective-permute-start.1
  222.8 17.5 %collective-permute-start.2 = (f32[64,2025]{1,0:T(8,128)S(1)}, f32[64,2025]{1,0:T(8,128)S(1)}, u32[]{:S(2)}, u32[]{:S(2)}) collective-permute-start(f32[64,2025]{1,0:T(8,128)S(1)} %copy.56), channel_id=1, source_target_pairs={{4,0},{8,4},{12,8},{16,12},{20,16},{24,20},{28,24},{32,28},{36,32}... | collective-permute-start | bytes 1555208 | tf_op jit(solution)/shard_map/ppermute | solution.py:18
  412.5 13.8 collective-permute-start.3
  425.0 17.1 %collective-permute-start.4 = (f32[64,2025]{1,0:T(8,128)S(1)}, f32[64,2025]{1,0:T(8,128)S(1)}, u32[]{:S(2)}, u32[]{:S(2)}) collective-permute-start(f32[64,2025]{1,0:T(8,128)S(1)} %copy.65), channel_id=1, source_target_pairs={{4,0},{8,4},{12,8},{16,12},{20,16},{24,20},{28,24},{32,28},{36,32}... | collective-permute-start | bytes 1555208 | tf_op jit(solution)/shard_map/ppermute | solution.py:18
  616.9 13.7 collective-permute-start.5
  629.3 17.6 %collective-permute-start.6 = (f32[64,2025]{1,0:T(8,128)S(1)}, f32[64,2025]{1,0:T(8,128)S(1)}, u32[]{:S(2)}, u32[]{:S(2)}) collective-permute-start(f32[64,2025]{1,0:T(8,128)S(1)} %copy.74), channel_id=1, source_target_pairs={{4,0},{8,4},{12,8},{16,12},{20,16},{24,20},{28,24},{32,28},{36,32}... | collective-permute-start | bytes 1555208 | tf_op jit(solution)/shard_map/ppermute | solution.py:18
  821.3 14.9 %collective-permute-start.7 = (f32[64,2025]{1,0:T(8,128)S(1)}, f32[64,2025]{1,0:T(8,128)S(1)}, u32[]{:S(2)}, u32[]{:S(2)}) collective-permute-start(f32[64,2025]{1,0:T(8,128)S(1)} %copy.81), channel_id=1, source_target_pairs={{0,4},{4,8},{8,12},{12,16},{16,20},{20,24},{24,28},{28,32},{32,36}... | collective-permute-start | bytes 1555208 | tf_op jit(solution)/shard_map/ppermute | solution.py:18
  834.7 17.3 %collective-permute-start.8 = (f32[64,2025]{1,0:T(8,128)S(1)}, f32[64,2025]{1,0:T(8,128)S(1)}, u32[]{:S(2)}, u32[]{:S(2)}) collective-permute-start(f32[64,2025]{1,0:T(8,128)S(1)} %copy.83), channel_id=1, source_target_pairs={{4,0},{8,4},{12,8},{16,12},{20,16},{24,20},{28,24},{32,28},{36,32}... | collective-permute-start | bytes 1555208 | tf_op jit(solution)/shard_map/ppermute | solution.py:18
  881.8 444.6 %all-reduce.3.cloned.1.call-start = ((), (), s32[]{:S(2)}) async-start(), calls=%async_computation.1 | async-start | bytes 131072 | tf_op jit(solution)/shard_map/psum | solution.py:79
Sparse Core Ops, SparseCore 0:
  881.9 128.5 all-gather.1
  1025.7 300.6 all-reduce.2
where the time goes:
time: 1430 us; the launch traced here: 1420 us
  other arithmetic  587 us (41%)
  waiting for transfers between devices  428 us (30%)
  local copies, waits for them, and re-layouts  288 us (20%)
  matrix products  60.4 us (4%)
  starting transfers between devices  26.6 us (2%)
  blocking collectives  16.9 us (1%)
  between operations  15.7 us (1%)
    scatter-add x4, other arithmetic, cell_apply(): return jnp.zeros_like(values).at[:, connectivity].add(products)  341 us
    psum x1, waiting for transfers between devices, shards(): row_panel = lax.psum(row_panel, 'space')  301 us
    gather x8, local copies, waits for them, and re-layouts, cell_apply(): gathered = jnp.take(values, connectivity, axis=1)  158 us
    all_gather x1, waiting for transfers between devices, shards(): lax.all_gather(current, 'band', axis=0, tiled=True)  117 us
    scatter-add x4, other arithmetic, operate(): summed = summed.at[:, lower_face].add(from_lower)  62.7 us
    scatter-add x4, other arithmetic, operate(): return summed.at[:, upper_face].add(from_upper)  62.1 us
    add x4, local copies, waits for them, and re-layouts, cell_apply(): stiff_part * cell_scale + lumped_mass()[:, None] * cell_potential * gathered  36.2 us
    another operation x6, other arithmetic, inverse_factor(): factor = jnp.linalg.cholesky(margin)  33.9 us
  transfers between devices with their start and end apart: 11, of which 3 were waited for; matrix products, arithmetic and copies ran while one was open for 8% of the time, Pallas kernels for 0%

commit v1 on v0

v1 whole, which is shorter than its diff:
```python
import functools

import jax
import jax.numpy as jnp
import numpy as np
from jax import lax
from jax.experimental import pallas as pl
from jax.experimental.pallas import tpu as pltpu
from jax.sharding import PartitionSpec as P

FILTER_DEG = 4
GLL_WEIGHTS = (0.1, 49.0 / 90.0, 32.0 / 45.0, 49.0 / 90.0, 0.1)
CENTER = 11.0
HALF_WIDTH = 9.0
HIGHEST = lax.Precision.HIGHEST
MESH = pl.DeviceIdType.MESH

CELLS_Y = 20
CELLS_Z = 6
CHUNKS = CELLS_Y // 2
TILES = CHUNKS * CELLS_Z
SLOTS = 2 * TILES
HALF = 64
LANES = 128
ROWS = 160
PLANE = 32
PACKED = 2 * TILES + CELLS_Z + CHUNKS + 1


def plane_rows():
    rows = {(0, 0): 0, (4, 0): 8, (0, 4): 16, (4, 4): 24}
    for k in (1, 2, 3):
        rows[(0, k)] = k
        rows[(4, k)] = 8 + k
        rows[(k, 0)] = 3 + k
        rows[(k, 4)] = 16 + 3 + k
    rows[(1, 1)] = 7
    for k in (1, 2, 3):
        rows[(2, k)] = 8 + 3 + k
        rows[(3, k)] = 16 + k
    rows[(1, 2)] = 24 + 1
    rows[(1, 3)] = 24 + 7
    return rows


def local_rows():
    rows = plane_rows()
    return [PLANE * a + rows[(b, c)] for a in range(5) for b in range(5) for c in range(5)]


LOCAL_ROWS = local_rows()


def row_selector():
    chosen = np.zeros((ROWS, 125), np.float32)
    chosen[LOCAL_ROWS, np.arange(125)] = 1.0
    return chosen


def row_mass():
    weights = np.array(GLL_WEIGHTS, np.float32)
    mass = (weights[:, None, None] * weights[None, :, None] * weights[None, None, :]).reshape(-1)
    spread = np.zeros((ROWS, LANES), np.float32)
    spread[LOCAL_ROWS, :] = mass[:, None]
    return spread


def local(a, b, c):
    return 25 * a + 5 * b + c


def exact_dot(x, y):
    return jnp.dot(x, y, precision=HIGHEST, preferred_element_type=jnp.float32)


def chain_counts(before, doublings):
    size = before.shape[0]
    eye = (
        lax.broadcasted_iota(jnp.int32, (size, size), 0) == lax.broadcasted_iota(jnp.int32, (size, size), 1)
    ).astype(jnp.float32)
    total, power = eye + before, before
    for _ in range(doublings):
        power = jnp.dot(power, power, preferred_element_type=jnp.float32)
        total = total + jnp.dot(total, power, preferred_element_type=jnp.float32)
    return jnp.sum(total, axis=0, keepdims=True) - 1.0


def layout_kernel(conn_ref, coef_ref, stiff_ref, select_ref, index_ref, scale_ref, potential_ref, stiffness_ref):
    conn = conn_ref[...].astype(jnp.float32)
    cells = conn.shape[1]
    on_rows = lax.broadcasted_iota(jnp.int32, (cells, cells), 0)
    on_lanes = lax.broadcasted_iota(jnp.int32, (cells, cells), 1)

    def as_column(row):
        return jnp.sum(jnp.where(on_rows == on_lanes, row, 0.0), axis=1, keepdims=True)

    def row_of(node):
        return conn[node : node + 1, :]

    after_z = (as_column(row_of(local(2, 2, 4))) == row_of(local(2, 2, 0))).astype(jnp.float32)
    after_y = (as_column(row_of(local(2, 4, 2))) == row_of(local(2, 0, 2))).astype(jnp.float32)
    at_z = chain_counts(after_z, 2)
    at_y = chain_counts(after_y, 4)
    upper_half = at_y >= CHUNKS
    tile = (at_y - jnp.where(upper_half, 1.0 * CHUNKS, 0.0)) * CELLS_Z + at_z
    slot = 2.0 * tile + jnp.where(upper_half, 1.0, 0.0)
    moved = (as_column(slot) == on_lanes.astype(jnp.float32)).astype(jnp.float32)
    index_ref[...] = (exact_dot(conn, moved) + 0.5).astype(jnp.int32)

    wanted = lax.broadcasted_iota(jnp.int32, (TILES, cells), 0).astype(jnp.float32)
    lane = lax.broadcasted_iota(jnp.int32, (TILES, LANES), 1)

    def spread(row):
        low, high = [
            jnp.sum(jnp.where(slot == 2.0 * wanted + half, row, 0.0), axis=1, keepdims=True) for half in (0.0, 1.0)
        ]
        return jnp.where(lane < HALF, low, high)

    scale_ref[...] = spread(coef_ref[0:1, :])
    potential_ref[...] = spread(coef_ref[1:2, :])

    select = select_ref[...]
    part = exact_dot(select, stiff_ref[...])
    stiff = lax.dot_general(
        part, select, (((1,), (1,)), ((), ())), precision=HIGHEST, preferred_element_type=jnp.float32
    )
    high = stiff.astype(jnp.bfloat16)
    low = (stiff - high.astype(jnp.float32)).astype(jnp.bfloat16)
    stiffness_ref[...] = jnp.concatenate([high, high, low], axis=1)


def make_layout(connectivity, coefficients, stiffness):
    cells = connectivity.shape[1]
    whole = pl.BlockSpec(memory_space=pltpu.VMEM)
    return pl.pallas_call(
        layout_kernel,
        out_shape=(
            jax.ShapeDtypeStruct((125, cells), jnp.int32),
            jax.ShapeDtypeStruct((TILES, LANES), jnp.float32),
            jax.ShapeDtypeStruct((TILES, LANES), jnp.float32),
            jax.ShapeDtypeStruct((ROWS, 3 * ROWS), jnp.bfloat16),
        ),
        in_specs=[whole] * 4,
        out_specs=(whole,) * 4,
        name="layout",
    )(connectivity, coefficients, stiffness, row_selector())


def gather_kernel(index_ref, waves_ref, cells_ref):
    low_half = lax.broadcasted_iota(jnp.int32, (1, LANES), 1) < HALF
    cells_ref[...] = jnp.zeros_like(cells_ref)

    def body(t, carry):
        for node, row in enumerate(LOCAL_ROWS):
            first = waves_ref[pl.ds(index_ref[node, 2 * t], 1), :]
            second = waves_ref[pl.ds(index_ref[node, 2 * t + 1], 1), :]
            cells_ref[t, row : row + 1, :] = jnp.where(low_half, first, second)
        return carry

    lax.fori_loop(0, TILES, body, 0)


def gather_cells(index, doubled):
    return pl.pallas_call(
        gather_kernel,
        out_shape=jax.ShapeDtypeStruct((TILES, ROWS, LANES), jnp.float32),
        in_specs=[pl.BlockSpec(memory_space=pltpu.SMEM), pl.BlockSpec(memory_space=pltpu.VMEM)],
        out_specs=pl.BlockSpec(memory_space=pltpu.VMEM),
        compiler_params=pltpu.CompilerParams(vmem_limit_bytes=40 * 2**20),
        name="gather_cells",
    )(index, doubled)


def scatter_kernel(index_ref, cells_ref, nodes_ref, rows_ref):
    lane = lax.broadcasted_iota(jnp.int32, (ROWS, LANES), 1)
    row_at = lax.broadcasted_iota(jnp.int32, (ROWS, LANES), 0)
    inner = lax.axis_index("space") > 0
    weight = jnp.where((lane >= HALF) & (row_at < PLANE) & inner, 0.0, 1.0)

    def body(t, carry):
        values = cells_ref[t]
        turned = pltpu.roll(values, HALF, 1)
        rows_ref[0] = jnp.where(lane < HALF, values, turned) * weight
        rows_ref[1] = jnp.where(lane < HALF, turned, values) * weight
        for node, row in enumerate(LOCAL_ROWS):
            nodes_ref[pl.ds(index_ref[node, 2 * t], 1), :] = rows_ref[0, row : row + 1, :]
            nodes_ref[pl.ds(index_ref[node, 2 * t + 1], 1), :] = rows_ref[1, row : row + 1, :]
        return carry

    lax.fori_loop(0, TILES, body, 0)


def scatter_nodes(index, cells, node_count):
    return pl.pallas_call(
        scatter_kernel,
        out_shape=jax.ShapeDtypeStruct((node_count, LANES), jnp.float32),
        in_specs=[pl.BlockSpec(memory_space=pltpu.SMEM), pl.BlockSpec(memory_space=pltpu.VMEM)],
        out_specs=pl.BlockSpec(memory_space=pltpu.VMEM),
        scratch_shapes=[pltpu.VMEM((2, ROWS, LANES), jnp.float32)],
        compiler_params=pltpu.CompilerParams(vmem_limit_bytes=40 * 2**20),
        name="scatter_nodes",
    )(index, cells)


def filter_kernel(
    start_ref, stiff_ref, mass_ref, scale_ref, potential_ref, out_ref,
    other, product, face, halves, sends, receives, send_sems, receive_sems,
):
    count = lax.axis_size("space")
    me = lax.axis_index("space")
    above, below = lax.rem(me + 1, count), lax.rem(me + count - 1, count)
    has_below, has_above = me > 0, me < count - 1

    barrier = pltpu.get_barrier_semaphore()
    for neighbour in (below, above):
        pl.semaphore_signal(barrier, inc=1, device_id={"space": neighbour}, device_id_type=MESH)
    pl.semaphore_wait(barrier, 2)

    sub = lax.broadcasted_iota(jnp.int32, (8, LANES), 0)
    lane = lax.broadcasted_iota(jnp.int32, (8, LANES), 1)
    corner = sub == 0
    along_y = sub <= 3
    along_z = corner | ((sub >= 4) & (sub <= 6))
    in_z_group = (sub >= 1) & (sub <= 3)
    in_y_group = (sub >= 4) & (sub <= 6)
    low_half = lane < HALF

    def copy(step, way):
        return pltpu.make_async_remote_copy(
            src_ref=sends.at[way],
            dst_ref=receives.at[step, way],
            send_sem=send_sems.at[step, way],
            recv_sem=receive_sems.at[step, way],
            device_id={"space": above if way == 0 else below},
            device_id_type=MESH,
        )

    def groups(ref, t, first):
        return [ref[t, first + 8 * g : first + 8 * g + 8, :] for g in range(4)]

    def pack(way, c, tiles):
        for z, (a, b, y, d) in enumerate(tiles):
            t = c * CELLS_Z + z
            sends[way, 2 * t] = a
            inside = jnp.where(in_z_group, y, jnp.where(in_y_group, b, d))
            sends[way, 2 * t + 1] = jnp.where(corner, pltpu.roll(d, 7, 0), inside)
        sends[way, 2 * TILES + CELLS_Z + c] = tiles[CELLS_Z - 1][2]

        @pl.when(c == CHUNKS - 1)
        def _():
            for z in range(CELLS_Z):
                sends[way, 2 * TILES + z] = tiles[z][1]
            sends[way, PACKED - 1] = tiles[CELLS_Z - 1][3]

    def unpack(step, way, c, z):
        t = c * CELLS_Z + z
        a = receives[step, way, 2 * t]
        inside = receives[step, way, 2 * t + 1]
        turned = pltpu.roll(inside, 1, 0)
        b = jnp.where(in_y_group, inside, receives[step, way, 2 * TILES + z])
        y = jnp.where(in_z_group, inside, receives[step, way, 2 * TILES + CELLS_Z + c])
        d = jnp.where(sub == 7, inside, jnp.where(sub == 1, turned, receives[step, way, PACKED - 1]))
        return [a, b, y, d]

    def fill(ref, first):
        def body(c, carry):
            nxt = lax.rem(c + 1, CHUNKS)
            last = c == CHUNKS - 1
            shared = jnp.logical_or(jnp.logical_not(last), low_half)

            def from_next(value):
                return jnp.where(last, pltpu.roll(value, HALF, 1), value)

            tiles = [groups(ref, c * CELLS_Z + z, first) for z in range(CELLS_Z)]
            b_new = []
            for z in range(CELLS_Z):
                ahead = from_next(ref[nxt * CELLS_Z + z, first : first + 8, :])
                b_new.append(jnp.where(along_y & shared, ahead, tiles[z][1]))
            for z in range(CELLS_Z):
                t = c * CELLS_Z + z
                ref[t, first + 8 : first + 16, :] = b_new[z]
                if z < CELLS_Z - 1:
                    ref[t, first + 16 : first + 24, :] = jnp.where(along_z, tiles[z + 1][0], tiles[z][2])
                    ref[t, first + 24 : first + 32, :] = jnp.where(corner, b_new[z + 1], tiles[z][3])
                else:
                    ahead = from_next(ref[nxt * CELLS_Z + z, first + 16 : first + 24, :])
                    ref[t, first + 24 : first + 32, :] = jnp.where(corner & shared, ahead, tiles[z][3])
            return carry

        lax.fori_loop(0, CHUNKS, body, 0)

    def assembled(c, first):
        prv = lax.rem(c + CHUNKS - 1, CHUNKS)
        is_first = c == 0

        def from_previous(value):
            return jnp.where(is_first, jnp.where(low_half, 0.0, pltpu.roll(value, HALF, 1)), value)

        tiles = [groups(product, c * CELLS_Z + z, first) for z in range(CELLS_Z)]
        for z in range(CELLS_Z):
            _, b, _, d = groups(product, prv * CELLS_Z + z, first)
            tiles[z][0] = tiles[z][0] + jnp.where(along_y, from_previous(b), 0.0)
            tiles[z][2] = tiles[z][2] + jnp.where(corner, from_previous(d), 0.0)
        for z in range(1, CELLS_Z):
            tiles[z][0] = tiles[z][0] + jnp.where(along_z, tiles[z - 1][2], 0.0)
            tiles[z][1] = tiles[z][1] + jnp.where(corner, tiles[z - 1][3], 0.0)
        return tiles

    def chunk_of(ref, c, rows):
        return jnp.concatenate([ref[c * CELLS_Z + z, rows, :] for z in range(CELLS_Z)], axis=1)

    def multiply(current, parts, split):
        stiff = jnp.concatenate([stiff_ref[part, :] for part in parts], axis=0)
        mass = jnp.concatenate([mass_ref[part, :] for part in parts], axis=0)

        def body(c, carry):
            if split:
                x = chunk_of(current, c, slice(0, ROWS))
                high = x.astype(jnp.bfloat16)
                low = (x - high.astype(jnp.float32)).astype(jnp.bfloat16)
                halves[c, 0:ROWS, :] = high
                halves[c, ROWS : 2 * ROWS, :] = low
            else:
                high = halves[c, 0:ROWS, :]
                low = halves[c, ROWS : 2 * ROWS, :]
            operand = jnp.concatenate([high, low, high], axis=0)
            result = jnp.dot(stiff, operand, preferred_element_type=jnp.float32)
            for z in range(CELLS_Z):
                t = c * CELLS_Z + z
                values = jnp.concatenate([current[t, part, :] for part in parts], axis=0)
                term = result[:, z * LANES : (z + 1) * LANES] * scale_ref[pl.ds(t, 1), :] + (
                    mass * potential_ref[pl.ds(t, 1), :] * values
                )
                at = 0
                for part in parts:
                    size = part.stop - part.start
                    product[t, part, :] = term[at : at + size]
                    at += size
            return carry

        lax.fori_loop(0, CHUNKS, body, 0)

    def advanced(step, current, previous, t, rows, total):
        value = total - CENTER * current[t, rows, :]
        if step == 0:
            return value * (1.0 / HALF_WIDTH)
        return value * (2.0 / HALF_WIDTH) - previous[t, rows, :]

    def advance_inner(step, current, previous, first):
        def body(c, carry):
            tiles = assembled(c, first)
            for z in range(CELLS_Z):
                t = c * CELLS_Z + z
                for g in range(4):
                    rows = slice(first + 8 * g, first + 8 * g + 8)
                    previous[t, rows, :] = advanced(step, current, previous, t, rows, tiles[z][g])
            return carry

        lax.fori_loop(0, CHUNKS, body, 0)
        fill(previous, first)

    def send_face(way, first):
        def body(c, carry):
            tiles = assembled(c, first)
            for z in range(CELLS_Z):
                for g in range(4):
                    face[way, c * CELLS_Z + z, 8 * g : 8 * g + 8, :] = tiles[z][g]
            pack(way, c, tiles)
            return carry

        lax.fori_loop(0, CHUNKS, body, 0)

    def advance_face(step, current, previous, way, first, valid):
        def body(c, carry):
            for z in range(CELLS_Z):
                t = c * CELLS_Z + z
                arrived = unpack(step + 1, way, c, z)
                for g in range(4):
                    rows = slice(first + 8 * g, first + 8 * g + 8)
                    total = face[1 - way, t, 8 * g : 8 * g + 8, :] + jnp.where(valid, arrived[g], 0.0)
                    previous[t, rows, :] = advanced(step, current, previous, t, rows, total)
            return carry

        lax.fori_loop(0, CHUNKS, body, 0)
        fill(previous, first)

    top = 4 * PLANE

    def pack_start(c, carry):
        pack(0, c, [groups(start_ref, c * CELLS_Z + z, top) for z in range(CELLS_Z)])
        return carry

    lax.fori_loop(0, CHUNKS, pack_start, 0)
    owner = copy(0, 0)
    owner.start()
    out_ref[...] = start_ref[...]
    owner.wait()

    def take_owner(c, carry):
        for z in range(CELLS_Z):
            t = c * CELLS_Z + z
            arrived = unpack(0, 0, c, z)
            for g in range(4):
                rows = slice(8 * g, 8 * g + 8)
                out_ref[t, rows, :] = jnp.where(has_below, arrived[g], out_ref[t, rows, :])
        return carry

    lax.fori_loop(0, CHUNKS, take_owner, 0)
    fill(out_ref, 0)

    for step in range(FILTER_DEG):
        current, previous = (out_ref, other) if step % 2 == 0 else (other, out_ref)
        multiply(current, [slice(0, PLANE), slice(top, ROWS)], True)
        copies = [copy(step + 1, 0), copy(step + 1, 1)]
        for way, first in ((0, top), (1, 0)):
            send_face(way, first)
            copies[way].start()
        multiply(current, [slice(PLANE, top)], False)
        for a in range(1, 4):
            advance_inner(step, current, previous, PLANE * a)
        copies[0].wait()
        advance_face(step, current, previous, 0, 0, has_below)
        copies[1].wait()
        advance_face(step, current, previous, 1, top, has_above)


def filter_cells(start, stiff, scale, potential):
    whole = pl.BlockSpec(memory_space=pltpu.VMEM)
    cells = (TILES, ROWS, LANES)
    rounds = FILTER_DEG + 1
    return pl.pallas_call(
        filter_kernel,
        out_shape=jax.ShapeDtypeStruct(cells, jnp.float32),
        in_specs=[whole] * 5,
        out_specs=whole,
        scratch_shapes=[
            pltpu.VMEM(cells, jnp.float32),
            pltpu.VMEM(cells, jnp.float32),
            pltpu.VMEM((2, TILES, PLANE, LANES), jnp.float32),
            pltpu.VMEM((CHUNKS, 2 * ROWS, CELLS_Z * LANES), jnp.bfloat16),
            pltpu.VMEM((2, PACKED, 8, LANES), jnp.float32),
            pltpu.VMEM((rounds, 2, PACKED, 8, LANES), jnp.float32),
            pltpu.SemaphoreType.DMA((rounds, 2)),
            pltpu.SemaphoreType.DMA((rounds, 2)),
        ],
        compiler_params=pltpu.CompilerParams(
            collective_id=0, has_side_effects=True, vmem_limit_bytes=56 * 2**20
        ),
        name="filter_cells",
    )(start, stiff, row_mass(), scale, potential)


def inverse_factor(margin, order):
    factor = jnp.linalg.cholesky(margin)
    return lax.linalg.triangular_solve(
        factor, jnp.eye(order, dtype=margin.dtype), left_side=True, lower=True
    )


def shards(
    wavefunctions, stiffness, cell_scale, cell_potential, connectivity, lower_face, upper_face
):
    width, node_count = wavefunctions.shape
    face_count = lower_face.shape[0]
    space_count = lax.axis_size("space")
    band_count = lax.axis_size("band")
    total_bands = width * band_count
    owned_count = node_count * space_count - face_count * (space_count - 1)

    coefficients = jnp.stack([cell_scale, cell_potential])
    index, scale, potential, stiff = make_layout(connectivity, coefficients, stiffness)
    doubled = jnp.concatenate([wavefunctions, wavefunctions], axis=0).T
    cells = gather_cells(index, doubled)
    cells = filter_cells(cells, stiff, scale, potential)
    nodes = scatter_nodes(index, cells, node_count)
    current, weighted = nodes[:, :width].T, nodes[:, width:].T

    everything = lax.all_gather(current, "band", axis=0, tiled=True)
    blocks = jnp.einsum("bn,kn->bk", weighted, everything, precision=HIGHEST)
    row_panel = lax.psum(blocks, "space")
    margin = lax.all_gather(row_panel, "band", axis=0, tiled=True) / owned_count
    inverse = inverse_factor(margin, total_bands)
    my_panel = lax.dynamic_slice_in_dim(inverse, lax.axis_index("band") * width, width, 0)
    return jnp.dot(my_panel, everything, precision=HIGHEST)


def solution(mesh):
    placed = (
        P("band", "space"),
        P(),
        P("space"),
        P("space"),
        P(None, "space"),
        P("space"),
        P("space"),
    )
    return jax.shard_map(
        shards, mesh=mesh, in_specs=placed, out_specs=P("band", "space"), check_vma=False
    )
```

time: 1430 us -> 721 us (0.50)
  other arithmetic: 587 us -> 61.6 us
  local copies, waits for them, and re-layouts: 288 us -> 29.2 us
  Pallas kernels: 0 us -> 161 us
  matrix products: 60.4 us -> 30.5 us
  waiting for transfers between devices: 428 us -> 399 us
  starting transfers between devices: 26.6 us -> 0.51 us
    scatter-add x12 -> x0, other arithmetic: 465 us -> none  [the longest x4 341 us: cell_apply(): return jnp.zeros_like(values).at[:, connectivity].add(products)]
    gather x26 -> x0, local copies, waits for them, and re-layouts: 234 us -> none  [the longest x8 158 us: cell_apply(): gathered = jnp.take(values, connectivity, axis=1)]
    pallas_call x0 -> x4, Pallas kernels: none -> 161 us  [the longest x1 112 us: filter_cells(): pl.pallas_call(filter_kernel, out_shape=jax.ShapeDtypeStruct(cells, jnp.f...]
    add x4 -> x0, local copies, waits for them, and re-layouts: 36.2 us -> none  [cell_apply(): stiff_part * cell_scale + lumped_mass()[:, None] * cell_potential * gathered]
    dot_general x6 -> x2, matrix products: 59.1 us -> 29.2 us  [the longest x1 17.3 us: shards(): blocks = jnp.einsum('bn,kn->bk', weighted, everything, precision=HIGHEST)]
    ppermute x9 -> x0, starting transfers between devices: 26.5 us -> none  [from_behind(): lax.ppermute(value, axis, [(source, source + steps) for source in range(i...]
    sub x3 -> x0, other arithmetic: 25.2 us -> none  [shards(): 2.0 / HALF_WIDTH * (operate(current) - CENTER * current) - previous]
    scatter x1 -> x0, other arithmetic: 24.3 us -> none  [shards(): wavefunctions.at[:, lower_face]]
  transfers between devices with their start and end apart: 11 -> 2, of which waited for: 3 -> 2; matrix products, arithmetic and copies ran while one was open for 8% -> 0% of each run, Pallas kernels for 0% -> 0%
where the time goes in v1:
time: 721 us; the launch traced here: 714 us
  waiting for transfers between devices  399 us (55%)
  Pallas kernels  161 us (22%)
  other arithmetic  61.6 us (9%)
  matrix products  30.5 us (4%)
  local copies, waits for them, and re-layouts  29.2 us (4%)
  blocking collectives  16.9 us (2%)
  between operations  15 us (2%)
    psum x1, waiting for transfers between devices, shards(): row_panel = lax.psum(blocks, 'space')  301 us
    pallas_call x1, Pallas kernels, filter_cells(): pl.pallas_call(filter_kernel, out_shape=jax.ShapeDtypeStruct(cells, jnp.f...  112 us
    all_gather x1, waiting for transfers between devices, shards(): everything = lax.all_gather(current, 'band', axis=0, tiled=True)  98.2 us
    another operation x6, other arithmetic, inverse_factor(): factor = jnp.linalg.cholesky(margin)  33.9 us
    pallas_call x1, Pallas kernels, scatter_nodes(): pl.pallas_call(scatter_kernel, out_shape=jax.ShapeDtypeStruct((node_count...  27.9 us
    another operation x3, other arithmetic, inverse_factor(): lax.linalg.triangular_solve(factor, jnp.eye(order, dtype=margin.dtype), l...  19.7 us
    pallas_call x1, Pallas kernels, gather_cells(): pl.pallas_call(gather_kernel, out_shape=jax.ShapeDtypeStruct((TILES, ROWS...  18.1 us
    dot_general x1, matrix products, shards(): blocks = jnp.einsum('bn,kn->bk', weighted, everything, precision=HIGHEST)  17.3 us
  transfers between devices with their start and end apart: 2, of which 2 were waited for; matrix products, arithmetic and copies ran while one was open for 0% of the time, Pallas kernels for 0%

profile of v1, /device:TPU:1, one launch (start us, length us, event | category | flops | bytes accessed | tf_op | source)
XLA Modules:
  0.0 714.4 jit_solution(18437782066310519421)
XLA Ops:
  6.5 0.0 all-gather.2.cloned.1.call-start
  6.5 1.6 copy.13.conn_ref
  8.1 5.3 copy.14
  13.4 7.3 %maximum_bitcast_fusion.waves_ref = f32[10125,128]{1,0:T(8,128)} fusion(f32[64,10125]{0,1:T(8,128)} %copy.14), kind=kLoop, calls=%fused_computation.5 | loop fusion | flops 1296000 | bytes 7776000 | tf_op jit(solution)/shard_map/transpose | solution.py:472
  20.6 0.0 copy-done.6
  20.6 0.0 copy-done.7
  20.6 0.5 pad_maximum_fusion.coef_ref
  21.2 3.3 layout.1
  24.5 2.5 copy-done.1
  26.9 0.8 copy-done.4
  27.8 18.1 %gather_cells.1.start_ref = f32[60,160,128]{2,1,0:T(8,128)S(1)} custom-call(s32[125,120]{1,0:T(8,128)S(1)} %copy-done.4, f32[10125,128]{1,0:T(8,128)S(1)} %copy-done.1), custom_call_target="tpu_custom_call" | custom-call | tf_op jit(solution)/shard_map/gather_cells/pallas_call | solution.py:164
  45.8 0.0 copy-start.2
  45.8 2.2 copy-done.2
  48.1 112.2 %filter_cells.1.cells_ref = f32[60,160,128]{2,1,0:T(8,128)} custom-call(f32[60,160,128]{2,1,0:T(8,128)} %copy-done.2, bf16[160,480]{1,0:T(8,128)(2,1)} %get-tuple-element.10.stiff_ref, f32[160,128]{1,0:T(8,128)} %constant.94.clone.mass_ref, f32[60,128]{1,0:T(8,128)} %get-tuple-element.11.scale_ref, f32[60,128]{1,0:T(8,128)} %get-tuple-element.12.potential_ref), custom_call_target="tpu_custom_call" | custom-call | tf_op jit(solution)/shard_map/filter_cells/pallas_call | solution.py:431
  160.3 0.0 copy-done.5
  160.3 0.0 copy-start.3
  160.3 2.4 copy-done.3
  162.7 27.9 %scatter_nodes.1 = f32[10125,128]{1,0:T(8,128)S(1)} custom-call(s32[125,120]{1,0:T(8,128)S(1)} %copy-done.5, f32[60,160,128]{2,1,0:T(8,128)S(1)} %copy-done.3), custom_call_target="tpu_custom_call" | custom-call | tf_op jit(solution)/shard_map/scatter_nodes/pallas_call | solution.py:194
  190.6 0.0 copy-start
  190.6 2.3 copy-done
  193.0 2.4 slice_bitcast_fusion
  195.4 5.5 copy.16
  200.9 0.0 all-gather.2.cloned.1.call-update
  200.9 0.5 all-reduce.3.cloned.1.call-start
  201.5 98.2 %all-gather.2.cloned.1.call-done = f32[256,10125]{1,0:T(8,128)} async-done(((f32[64,10125]{1,0:T(8,128)}), f32[256,10125]{1,0:T(8,128)}) %all-gather.2.cloned.1.call-update) | async-done | bytes 10368016 | tf_op jit(solution)/shard_map/all_gather | solution.py:478
  299.7 17.3 %fusion = f32[64,256]{1,0:T(8,128)} fusion(f32[256,10125]{1,0:T(8,128)} %all-gather.2.cloned.1.call-done, f32[10125,128]{1,0:T(8,128)} %copy-done), kind=kOutput, calls=%fused_computation.3 | convolution fusion | flops 1990656000 | bytes 15617536 | tf_op jit(solution)/shard_map/bn,kn->bk/dot_general | solution.py:479
  317.0 0.0 all-reduce.3.cloned.1.call-update
  317.0 300.8 %all-reduce.3.cloned.1.call-done = f32[64,256]{1,0:T(8,128)} async-done(((f32[64,256]{1,0:T(8,128)}), f32[64,256]{1,0:T(8,128)}) %all-reduce.3.cloned.1.call-update) | async-done | bytes 65552 | tf_op jit(solution)/shard_map/psum | solution.py:480
  617.8 16.9 %all_gather.7 = f32[256,256]{1,0:T(8,128)S(1)} all-gather(f32[64,256]{1,0:T(8,128)} %all-reduce.3.cloned.1.call-done), channel_id=1, replica_groups=mesh['space'=32,'band'=4] {'band'}, dimensions={0}, use_global_device_ids=true | all-gather | bytes 327680 | tf_op jit(solution)/shard_map/all_gather | solution.py:481
  634.7 0.1 copy.17
  634.9 0.1 copy.18
  635.1 11.7 %cholesky.50 = f32[128,128]{1,0:T(8,128)S(1)} custom-call(f32[128,128]{1,0:T(8,128)S(1)} %cholesky.118), custom_call_target="Cholesky" | custom-call | tf_op jit(solution)/shard_map/jit(cholesky)/cholesky | solution.py:454
  646.8 9.8 %custom-call.14 = f32[1,128,128]{1,2,0:T(8,128)S(1)} custom-call(f32[1,128,128]{2,1,0:T(8,128)S(1)} %get-tuple-element.34), custom_call_target="InvertDiagBlocksLowerTriangular" | custom-call | tf_op jit(solution)/shard_map/jit(cholesky)/cholesky | solution.py:454
  656.7 0.2 constant_dynamic-update-slice_fusion
  656.9 0.3 convolution_subtract_fusion.1
  657.1 11.7 %cholesky.105 = f32[128,128]{1,0:T(8,128)S(1)} custom-call(f32[128,128]{1,0:T(8,128)S(1)} %convolution_subtract_fusion.1), custom_call_target="Cholesky" | custom-call | tf_op jit(solution)/shard_map/jit(cholesky)/cholesky | solution.py:454
  668.9 0.6 compare_reduce_fusion
  670.8 0.1 triangular_solve.63
  670.9 4.0 while.1
  671.1 0.6 fusion.23
  671.7 1.3 bitcast_dynamic-update-slice_fusion.2
  673.0 0.6 fusion.23
  673.6 1.3 bitcast_dynamic-update-slice_fusion.2
  674.9 19.7 %custom-call.15 = f32[2,128,128]{1,2,0:T(8,128)S(1)} custom-call(f32[2,128,128]{2,1,0:T(8,128)S(1)} %get-tuple-element.20), custom_call_target="InvertDiagBlocksLowerTriangular" | custom-call | tf_op jit(solution)/shard_map/triangular_solve | solution.py:455
  694.6 0.3 fusion.3
  694.8 0.3 convolution_subtract_fusion
  695.1 0.3 fusion.9
  695.4 11.9 %fusion.6 = f32[64,10125]{1,0:T(8,128)} fusion(f32[256,10125]{1,0:T(8,128)} %all-gather.2.cloned.1.call-done, s32[]{:T(128)S(6)} %select_n.8, f32[128,256]{1,0:T(8,128)S(1)} %fusion.3, f32[128,256]{1,0:T(8,128)S(1)} %fusion.9), kind=kOutput, calls=%fused_computation.19 | convolution fusion | flops 1990672384 | bytes 13222148 | tf_op jit(solution)/shard_map/dot_general | solution.py:484
  (17 shorter events, 0.2 us)
Async XLA Ops:
  6.5 293.1 %all-gather.2.cloned.1.call-start = ((), (), s32[]{:S(2)}) async-start(), calls=%async_computation | async-start | bytes 13107200 | tf_op jit(solution)/shard_map/all_gather | solution.py:478
  13.4 7.3 %copy-start.6 = (f32[120]{0:T(128)S(1)}, f32[120]{0:T(128)}, u32[]{:S(2)}) copy-start(f32[120]{0:T(128)} %param.12) | copy-start | bytes 1444
  13.4 7.3 %copy-start.7 = (f32[120]{0:T(128)S(1)}, f32[120]{0:T(128)}, u32[]{:S(2)}) copy-start(f32[120]{0:T(128)} %param.11) | copy-start | bytes 1444
  24.5 2.5 copy-start.1
  26.9 0.8 copy-start.4
  45.8 2.2 copy-start.2
  48.1 112.2 %copy-start.5 = (s32[125,120]{1,0:T(8,128)S(1)}, s32[125,120]{1,0:T(8,128)}, u32[]{:S(2)}) copy-start(s32[125,120]{1,0:T(8,128)} %get-tuple-element.9.index_ref) | copy-start | bytes 180004
  160.3 2.4 copy-start.3
  190.6 2.4 copy-start
  200.9 416.9 %all-reduce.3.cloned.1.call-start = ((), (), s32[]{:S(2)}) async-start(), calls=%async_computation.1 | async-start | bytes 131072 | tf_op jit(solution)/shard_map/psum | solution.py:480
Sparse Core Ops, SparseCore 0:
  201.1 98.5 all-gather.1
  317.1 300.6 all-reduce.2

commit v2 on v1

--- a/solution.py
+++ b/solution.py
@@ -25,6 +25,12 @@
 ROWS = 160
 PLANE = 32
 PACKED = 2 * TILES + CELLS_Z + CHUNKS + 1
+
+NODES = 10125
+PAIRS = 5120
+BLOCK = 256
+BANDS_DEV = 64
+N_BAND = 4
 
 
 def plane_rows():
@@ -171,32 +177,49 @@
     )(index, doubled)
 
 
-def scatter_kernel(index_ref, cells_ref, nodes_ref, rows_ref):
+def scatter_kernel(index_ref, cells_ref, packed_ref, weight_ref, nodes_ref, rows_ref):
     lane = lax.broadcasted_iota(jnp.int32, (ROWS, LANES), 1)
     row_at = lax.broadcasted_iota(jnp.int32, (ROWS, LANES), 0)
     inner = lax.axis_index("space") > 0
-    weight = jnp.where((lane >= HALF) & (row_at < PLANE) & inner, 0.0, 1.0)
+    weight = jnp.where((row_at < PLANE) & inner, 0.0, 1.0)
+    nodes_ref[NODES - NODES % 8 :, :] = jnp.zeros((2 * PAIRS - NODES + NODES % 8, LANES), jnp.float32)
 
     def body(t, carry):
         values = cells_ref[t]
         turned = pltpu.roll(values, HALF, 1)
-        rows_ref[0] = jnp.where(lane < HALF, values, turned) * weight
-        rows_ref[1] = jnp.where(lane < HALF, turned, values) * weight
+        rows_ref[0] = jnp.where(lane < HALF, values, weight)
+        rows_ref[1] = jnp.where(lane < HALF, turned, weight)
         for node, row in enumerate(LOCAL_ROWS):
             nodes_ref[pl.ds(index_ref[node, 2 * t], 1), :] = rows_ref[0, row : row + 1, :]
             nodes_ref[pl.ds(index_ref[node, 2 * t + 1], 1), :] = rows_ref[1, row : row + 1, :]
         return carry
 
     lax.fori_loop(0, TILES, body, 0)
-
-
-def scatter_nodes(index, cells, node_count):
+    low_half = lax.broadcasted_iota(jnp.int32, (BLOCK, LANES), 1) < HALF
+
+    def pack(i, carry):
+        first = nodes_ref[pl.ds(pl.multiple_of(i * BLOCK, BLOCK), BLOCK), :]
+        second = nodes_ref[pl.ds(pl.multiple_of(PAIRS + i * BLOCK, BLOCK), BLOCK), :]
+        rows = pl.ds(pl.multiple_of(i * BLOCK, BLOCK), BLOCK)
+        packed_ref[rows, :] = jnp.where(low_half, first, pltpu.roll(second, HALF, 1))
+        weight_ref[rows, :] = jnp.where(low_half, pltpu.roll(first, HALF, 1), second)
+        return carry
+
+    lax.fori_loop(0, PAIRS // BLOCK, pack, 0)
+
+
+def scatter_nodes(index, cells):
+    whole = pl.BlockSpec(memory_space=pltpu.VMEM)
+    packed = jax.ShapeDtypeStruct((PAIRS, LANES), jnp.float32)
     return pl.pallas_call(
         scatter_kernel,
-        out_shape=jax.ShapeDtypeStruct((node_count, LANES), jnp.float32),
-        in_specs=[pl.BlockSpec(memory_space=pltpu.SMEM), pl.BlockSpec(memory_space=pltpu.VMEM)],
-        out_specs=pl.BlockSpec(memory_space=pltpu.VMEM),
-        scratch_shapes=[pltpu.VMEM((2, ROWS, LANES), jnp.float32)],
+        out_shape=(packed, packed),
+        in_specs=[pl.BlockSpec(memory_space=pltpu.SMEM), whole],
+        out_specs=(whole, whole),
+        scratch_shapes=[
+            pltpu.VMEM((2 * PAIRS, LANES), jnp.float32),
+            pltpu.VMEM((2, ROWS, LANES), jnp.float32),
+        ],
         compiler_params=pltpu.CompilerParams(vmem_limit_bytes=40 * 2**20),
         name="scatter_nodes",
     )(index, cells)
@@ -450,21 +473,277 @@
     )(start, stiff, row_mass(), scale, potential)
 
 
-def inverse_factor(margin, order):
-    factor = jnp.linalg.cholesky(margin)
-    return lax.linalg.triangular_solve(
-        factor, jnp.eye(order, dtype=margin.dtype), left_side=True, lower=True
+def split(x):
+    high = x.astype(jnp.bfloat16)
+    return high, (x - high.astype(jnp.float32)).astype(jnp.bfloat16)
+
+
+def exact_dot_t(x, y):
+    return lax.dot_general(
+        x, y, (((1,), (1,)), ((), ())), precision=HIGHEST, preferred_element_type=jnp.float32
     )
+
+
+def inverse_of_block(block):
+    size = BANDS_DEV
+    row_at = lax.broadcasted_iota(jnp.int32, (size, LANES), 0)
+    lane = lax.broadcasted_iota(jnp.int32, (size, LANES), 1)
+    wide = jnp.concatenate([block, jnp.zeros((size, LANES - size), jnp.float32)], axis=1)
+    wide = jnp.where(lane == row_at + size, 1.0, wide)
+    tiles = [wide[8 * g : 8 * g + 8] for g in range(size // 8)]
+    sub = lax.broadcasted_iota(jnp.int32, (8, LANES), 0)
+    for j in range(size):
+        home, at = divmod(j, 8)
+        columns = [jnp.broadcast_to(tile[:, j : j + 1], (8, LANES)) for tile in tiles[home:]]
+        row = tiles[home][at : at + 1, :]
+        ratio = row * (1.0 / columns[0][at : at + 1, :])
+        for g in range(home, size // 8):
+            factor = columns[g - home]
+            if g == home:
+                factor = jnp.where(sub > at, factor, 0.0)
+            tiles[g] = tiles[g] - factor * ratio
+    wide = jnp.concatenate(tiles, axis=0)
+    pivots = jnp.sum(jnp.where(lane == row_at, wide, 0.0), axis=1, keepdims=True)
+    return wide[:, size:] * (1.0 / jnp.sqrt(pivots))
+
+
+def finish_kernel(
+    owned, own, weight, out, partner, cross, partner_cross, sums, by_x, by_y, line, piece, by_z, reduced, everyone,
+    inverse, pair_sems, cross_sems, forward_sems, x_sems, y_sems, z_sems, y_back_sems, x_back_sems, band_sems,
+):
+    space, band = lax.axis_index("space"), lax.axis_index("band")
+    at_x = lax.rem(space, 4)
+    at_y = lax.rem(space // 4, 4)
+    core = lax.rem(band, 2)
+    chip = band // 2
+    mate = band + 1 - 2 * core
+    across = lax.rem(band + 2, N_BAND)
+    across_mate = lax.rem(mate + 2, N_BAND)
+
+    def x_peer(k):
+        return {"space": space - at_x + lax.rem(at_x + k, 4)}
+
+    def y_peer(k):
+        return {"space": space - 4 * at_y + 4 * lax.rem(at_y + k, 4)}
+
+    z_peer = {"space": lax.rem(space + 16, 32)}
+
+    peers = [x_peer(k) for k in (1, 2, 3)] + [y_peer(k) for k in (1, 2, 3)] + [z_peer]
+    peers += [{"band": lax.rem(band + k, N_BAND)} for k in (1, 2, 3)]
+    barrier = pltpu.get_barrier_semaphore()
+    for peer in peers:
+        pl.semaphore_signal(barrier, inc=1, device_id=peer, device_id_type=MESH)
+    pl.semaphore_wait(barrier, len(peers))
+
+    def send(source, target, sems, slot, peer):
+        return pltpu.make_async_remote_copy(
+            src_ref=source,
+            dst_ref=target,
+            send_sem=sems.at[0, slot],
+            recv_sem=sems.at[1, slot],
+            device_id=peer,
+            device_id_type=MESH,
+        )
+
+    half = PAIRS // 2
+    mine_first = pl.ds(pl.multiple_of(chip * half, half), half)
+    mine_second = pl.ds(pl.multiple_of((1 - chip) * half, half), half)
+    to_mate, to_across = {"band": mate}, {"band": across}
+    pair = send(own, partner, pair_sems, 0, to_mate)
+    first = send(own.at[mine_first], cross.at[mine_first], cross_sems, 0, to_across)
+    second = send(own.at[mine_second], cross.at[mine_second], cross_sems, 1, to_across)
+    forward_first = send(cross.at[mine_second], partner_cross.at[mine_second], forward_sems, 0, to_mate)
+    forward_second = send(cross.at[mine_first], partner_cross.at[mine_first], forward_sems, 1, to_mate)
+    first.start()
+    pair.start()
+    pair.wait()
+
+    def products(left, right):
+        left_high, left_low = split(left)
+        right_high, right_low = split(right)
+        return lax.dot_general(
+            jnp.concatenate([left_high, left_high, left_low], axis=0),
+            jnp.concatenate([right_high, right_low, right_high], axis=0),
+            (((0,), (0,)), ((), ())),
+            preferred_element_type=jnp.float32,
+        )
+
+    def block_rows(i):
+        return pl.ds(pl.multiple_of(i * BLOCK, BLOCK), BLOCK)
+
+    def own_terms(i, total):
+        rows = block_rows(i)
+        mine = own[rows, :]
+        return total + products(mine * weight[rows, :], jnp.concatenate([mine, partner[rows, :]], axis=1))
+
+    def cross_terms(i, total):
+        rows = block_rows(i + (1 - chip) * (half // BLOCK))
+        scale = weight[rows, :]
+        return total + products(
+            cross[rows, :], jnp.concatenate([own[rows, :] * scale, partner[rows, :] * scale], axis=1)
+        )
+
+    low_half = lax.broadcasted_iota(jnp.int32, (BANDS_DEV, LANES), 1) < HALF
+
+    def fold(total):
+        size = BANDS_DEV
+        left = total[:size, :LANES] + pltpu.roll(total[size:, :LANES], HALF, 1)
+        right = pltpu.roll(total[:size, LANES:], HALF, 1) + total[size:, LANES:]
+        return jnp.where(low_half, left, right)
+
+    zero = jnp.zeros((LANES, 2 * LANES), jnp.float32)
+    sums[0:BANDS_DEV, :] = fold(lax.fori_loop(0, PAIRS // BLOCK, own_terms, zero))
+    first.wait()
+    second.start()
+    forward_first.start()
+    sums[BANDS_DEV : 2 * BANDS_DEV, :] = fold(lax.fori_loop(0, half // BLOCK, cross_terms, zero))
+
+    def rows_of(at, size):
+        return pl.ds(pl.multiple_of(at, size), size)
+
+    to_x = [
+        send(sums.at[rows_of(32 * lax.rem(at_x + k, 4), 32)], by_x.at[k - 1], x_sems, k - 1, x_peer(k)) for k in (1, 2, 3)
+    ]
+    for step in to_x:
+        step.start()
+    for step in to_x:
+        step.wait()
+    line[...] = sums[rows_of(32 * at_x, 32), :] + by_x[0] + by_x[1] + by_x[2]
+    to_y = [
+        send(line.at[rows_of(8 * lax.rem(at_y + k, 4), 8)], by_y.at[k - 1], y_sems, k - 1, y_peer(k)) for k in (1, 2, 3)
+    ]
+    for step in to_y:
+        step.start()
+    for step in to_y:
+        step.wait()
+    piece[...] = line[rows_of(8 * at_y, 8), :] + by_y[0] + by_y[1] + by_y[2]
+    to_z = send(piece, by_z, z_sems, 0, z_peer)
+    to_z.start()
+    to_z.wait()
+    small = rows_of(32 * at_x + 8 * at_y, 8)
+    reduced[small, :] = piece[...] + by_z[...]
+    back_y = [send(reduced.at[small], reduced.at[small], y_back_sems, k - 1, y_peer(k)) for k in (1, 2, 3)]
+    for step in back_y:
+        step.start()
+    for step in back_y:
+        step.wait()
+    large = rows_of(32 * at_x, 32)
+    back_x = [send(reduced.at[large], reduced.at[large], x_back_sems, k - 1, x_peer(k)) for k in (1, 2, 3)]
+    for step in back_x:
+        step.start()
+    for step in back_x:
+        step.wait()
+    to_band = [
+        send(reduced, everyone.at[band], band_sems, k - 1, {"band": lax.rem(band + k, N_BAND)}) for k in (1, 2, 3)
+    ]
+    for step in to_band:
+        step.start()
+    everyone[band] = reduced[...]
+    for step in to_band:
+        step.wait()
+
+    def part(b, r, c):
+        size = BANDS_DEV
+        return everyone[b, r * size : (r + 1) * size, c * size : (c + 1) * size] * (1.0 / owned)
+
+    margin = {(b, b): part(b, 0, 0) for b in range(N_BAND)}
+    margin[1, 0], margin[3, 2] = part(1, 0, 1), part(3, 0, 1)
+    margin[2, 0] = part(0, 1, 0) + part(2, 1, 0).T
+    margin[2, 1] = part(0, 1, 1) + part(3, 1, 1).T
+    margin[3, 0] = part(1, 1, 1) + part(2, 1, 1).T
+    margin[3, 1] = part(1, 1, 0) + part(3, 1, 0).T
+
+    inverses, factor, whole = [], {}, {}
+    for k in range(N_BAND):
+        diagonal = inverse_of_block(margin[k, k])
+        inverses.append(diagonal)
+        for i in range(k + 1, N_BAND):
+            factor[i, k] = exact_dot_t(margin[i, k], diagonal)
+        for i in range(k + 1, N_BAND):
+            for j in range(k + 1, i + 1):
+                margin[i, j] = margin[i, j] - exact_dot_t(factor[i, k], factor[j, k])
+        whole[k, k] = diagonal
+        for j in range(k):
+            total = exact_dot(factor[k, j], whole[j, j])
+            for m in range(j + 1, k):
+                total = total + exact_dot(factor[k, m], whole[m, j])
+            whole[k, j] = -exact_dot(diagonal, total)
+        if k == 2:
+            second.wait()
+            forward_second.start()
+    padding = jnp.zeros((BANDS_DEV, LANES - BANDS_DEV), jnp.float32)
+    for i in range(N_BAND):
+        for j in range(N_BAND):
+            if j <= i:
+                inverse[i, j] = jnp.concatenate([whole[i, j], padding], axis=1)
+            else:
+                inverse[i, j] = jnp.zeros((BANDS_DEV, LANES), jnp.float32)
+    forward_first.wait()
+    forward_second.wait()
+
+    panels = [inverse[band, source] for source in (band, mate, across, across_mate)]
+    left = jnp.concatenate(
+        [
+            jnp.concatenate(panels, axis=1),
+            jnp.concatenate([pltpu.roll(panel, HALF, 1) for panel in panels], axis=1),
+        ],
+        axis=0,
+    )
+    left_high, left_low = split(left)
+    left = jnp.concatenate([left_high, left_high, left_low], axis=1)
+
+    def rotate(i, carry):
+        rows = block_rows(i)
+        right = jnp.concatenate([ref[rows, :] for ref in (own, partner, cross, partner_cross)], axis=1)
+        right_high, right_low = split(right)
+        rotated = lax.dot_general(
+            left,
+            jnp.concatenate([right_high, right_low, right_high], axis=1),
+            (((1,), (1,)), ((), ())),
+            preferred_element_type=jnp.float32,
+        )
+        out[:, rows] = rotated[:BANDS_DEV]
+        out[:, pl.ds(pl.multiple_of(PAIRS + i * BLOCK, BLOCK), BLOCK)] = rotated[BANDS_DEV:]
+        return carry
+
+    lax.fori_loop(0, PAIRS // BLOCK, rotate, 0)
+
+
+def finish(packed, weight, owned_count):
+    whole = pl.BlockSpec(memory_space=pltpu.VMEM)
+    nodes = pltpu.VMEM((PAIRS, LANES), jnp.float32)
+
+    def small(*shape):
+        return pltpu.VMEM(shape, jnp.float32)
+
+    def sems(slots):
+        return pltpu.SemaphoreType.DMA((2, slots))
+
+    return pl.pallas_call(
+        functools.partial(finish_kernel, owned_count),
+        out_shape=jax.ShapeDtypeStruct((BANDS_DEV, 2 * PAIRS), jnp.float32),
+        in_specs=[whole, whole],
+        out_specs=whole,
+        scratch_shapes=[
+            nodes, nodes, nodes,
+            small(LANES, LANES), small(3, 32, LANES), small(3, 8, LANES), small(32, LANES), small(8, LANES),
+            small(8, LANES), small(LANES, LANES), small(N_BAND, LANES, LANES),
+            small(N_BAND, N_BAND, BANDS_DEV, LANES),
+            sems(1), sems(2), sems(2), sems(3), sems(3), sems(1), sems(3), sems(3), sems(3),
+        ],
+        compiler_params=pltpu.CompilerParams(
+            collective_id=1, has_side_effects=True, vmem_limit_bytes=48 * 2**20
+        ),
+        name="finish",
+    )(packed, weight)
 
 
 def shards(
     wavefunctions, stiffness, cell_scale, cell_potential, connectivity, lower_face, upper_face
 ):
-    width, node_count = wavefunctions.shape
+    node_count = wavefunctions.shape[1]
     face_count = lower_face.shape[0]
     space_count = lax.axis_size("space")
-    band_count = lax.axis_size("band")
-    total_bands = width * band_count
     owned_count = node_count * space_count - face_count * (space_count - 1)
 
     coefficients = jnp.stack([cell_scale, cell_potential])
@@ -472,16 +751,8 @@
     doubled = jnp.concatenate([wavefunctions, wavefunctions], axis=0).T
     cells = gather_cells(index, doubled)
     cells = filter_cells(cells, stiff, scale, potential)
-    nodes = scatter_nodes(index, cells, node_count)
-    current, weighted = nodes[:, :width].T, nodes[:, width:].T
-
-    everything = lax.all_gather(current, "band", axis=0, tiled=True)
-    blocks = jnp.einsum("bn,kn->bk", weighted, everything, precision=HIGHEST)
-    row_panel = lax.psum(blocks, "space")
-    margin = lax.all_gather(row_panel, "band", axis=0, tiled=True) / owned_count
-    inverse = inverse_factor(margin, total_bands)
-    my_panel = lax.dynamic_slice_in_dim(inverse, lax.axis_index("band") * width, width, 0)
-    return jnp.dot(my_panel, everything, precision=HIGHEST)
+    packed, weight = scatter_nodes(index, cells)
+    return finish(packed, weight, owned_count)[:, :node_count]
 
 
 def solution(mesh):

time: 721 us -> 292 us (0.40)
  waiting for transfers between devices: 399 us -> 0 us
  Pallas kernels: 161 us -> 269 us
  other arithmetic: 61.6 us -> 6.99 us
  matrix products: 30.5 us -> 0 us
  blocking collectives: 16.9 us -> 0 us
  between operations: 15 us -> 0.08 us
  local copies, waits for them, and re-layouts: 29.2 us -> 14.3 us
    psum x1 -> x0, waiting for transfers between devices: 301 us -> none  [shards(): row_panel = lax.psum(blocks, 'space')]
    pallas_call x1 -> x2, Pallas kernels: 27.9 us -> 136 us  [the longest x1 108 us: finish(): pl.pallas_call(functools.partial(finish_kernel, owned_count), out_shape=j...]
    all_gather x1 -> x0, waiting for transfers between devices: 98.2 us -> none  [shards(): everything = lax.all_gather(current, 'band', axis=0, tiled=True)]
    another operation x9 -> x0, other arithmetic: 53.7 us -> none  [the longest x6 33.9 us: inverse_factor(): factor = jnp.linalg.cholesky(margin)]
    dot_general x2 -> x0, matrix products: 29.2 us -> none  [the longest x1 17.3 us: shards(): blocks = jnp.einsum('bn,kn->bk', weighted, everything, precision=HIGHEST)]
    all_gather x1 -> x0, blocking collectives: 16.9 us -> none  [shards(): margin = lax.all_gather(row_panel, 'band', axis=0, tiled=True) / owned_count]
    transpose x2 -> x0, local copies, waits for them, and re-layouts: 7.94 us -> none  [shards(): current, weighted = (nodes[:, :width].T, nodes[:, width:].T)]
    unnamed x18 -> x11, local copies, waits for them, and re-layouts: 17.1 us -> 14.3 us
  transfers between devices with their start and end apart: 2 -> 0, of which waited for: 2 -> 0; matrix products, arithmetic and copies ran while one was open for 0% -> 0% of each run, Pallas kernels for 0% -> 0%
where the time goes in v2:
time: 292 us; the launch traced here: 291 us
  Pallas kernels  269 us (92%)
  local copies, waits for them, and re-layouts  14.3 us (5%)
  other arithmetic  6.99 us (2%)
    pallas_call x1, Pallas kernels, filter_cells(): pl.pallas_call(filter_kernel, out_shape=jax.ShapeDtypeStruct(cells, jnp.f...  112 us
    pallas_call x1, Pallas kernels, finish(): pl.pallas_call(functools.partial(finish_kernel, owned_count), out_shape=j...  108 us
    pallas_call x1, Pallas kernels, scatter_nodes(): pl.pallas_call(scatter_kernel, out_shape=(packed, packed), in_specs=[pl.B...  27.4 us
    pallas_call x1, Pallas kernels, gather_cells(): pl.pallas_call(gather_kernel, out_shape=jax.ShapeDtypeStruct((TILES, ROWS...  18.1 us
    unnamed x11, local copies, waits for them, and re-layouts  14.3 us

profile of v2, /device:TPU:1, one launch (start us, length us, event | category | flops | bytes accessed | tf_op | source)
XLA Modules:
  0.0 290.8 jit_solution(16515253175628062785)
XLA Ops:
  0.0 1.3 pad_maximum_fusion.coef_ref
  1.3 1.5 copy.8.conn_ref
  2.8 3.3 %layout.1 = (s32[125,120]{1,0:T(8,128)}, f32[60,128]{1,0:T(8,128)}, f32[60,128]{1,0:T(8,128)}, bf16[160,480]{1,0:T(8,128)(2,1)}) custom-call(s32[125,120]{1,0:T(8,128)} %copy.8.conn_ref, f32[2,120]{1,0:T(2,128)} %pad_maximum_fusion.coef_ref, f32[125,125]{1,0:T(8,128)} %stiff_ref.1, f32[160,125]{1,0:T(8,128)} %constant.4.clone.select_ref), custom_call_target="tpu_custom_call" | custom-call | tf_op jit(solution)/shard_map/layout/pallas_call | solution.py:141
  6.1 5.2 %copy.9 = f32[64,10125]{0,1:T(8,128)} copy(f32[64,10125]{1,0:T(8,128)} %param.9) | data formatting | bytes 5184000 | tf_op args[0]
  11.3 0.0 copy-start.3
  11.3 5.7 %maximum_bitcast_fusion.waves_ref = f32[10125,128]{1,0:T(8,128)S(1)} fusion(f32[64,10125]{0,1:T(8,128)} %copy.9), kind=kLoop, calls=%fused_computation | loop fusion | flops 1296000 | bytes 7776000 | tf_op jit(solution)/shard_map/transpose | solution.py:751
  17.1 0.0 copy-done.3
  17.1 18.1 %gather_cells.1.start_ref = f32[60,160,128]{2,1,0:T(8,128)S(1)} custom-call(s32[125,120]{1,0:T(8,128)S(1)} %copy-done.3, f32[10125,128]{1,0:T(8,128)S(1)} %maximum_bitcast_fusion.waves_ref), custom_call_target="tpu_custom_call" | custom-call | tf_op jit(solution)/shard_map/gather_cells/pallas_call | solution.py:170
  35.1 0.0 copy-start.1
  35.1 2.2 copy-done.1
  37.3 112.3 %filter_cells.1.cells_ref = f32[60,160,128]{2,1,0:T(8,128)} custom-call(f32[60,160,128]{2,1,0:T(8,128)} %copy-done.1, bf16[160,480]{1,0:T(8,128)(2,1)} %get-tuple-element.12.stiff_ref, f32[160,128]{1,0:T(8,128)} %constant.5.clone.mass_ref, f32[60,128]{1,0:T(8,128)} %get-tuple-element.13.scale_ref, f32[60,128]{1,0:T(8,128)} %get-tuple-element.14.potential_ref), custom_call_target="tpu_custom_call" | custom-call | tf_op jit(solution)/shard_map/filter_cells/pallas_call | solution.py:454
  149.6 0.0 copy-start
  149.6 2.4 copy-done
  152.0 27.4 %scatter_nodes.1 = (f32[5120,128]{1,0:T(8,128)S(1)}, f32[5120,128]{1,0:T(8,128)S(1)}) custom-call(s32[125,120]{1,0:T(8,128)S(1)} %copy-done.3, f32[60,160,128]{2,1,0:T(8,128)S(1)} %copy-done), custom_call_target="tpu_custom_call" | custom-call | tf_op jit(solution)/shard_map/scatter_nodes/pallas_call | solution.py:214
  179.3 0.0 copy-start.2
  179.4 1.5 copy-done.2
  180.8 108.4 %finish.1 = f32[64,10240]{1,0:T(8,128)S(1)} custom-call(f32[5120,128]{1,0:T(8,128)S(1)} %get-tuple-element.15.own, f32[5120,128]{1,0:T(8,128)} %copy-done.2), custom_call_target="tpu_custom_call" | custom-call | tf_op jit(solution)/shard_map/finish/pallas_call | solution.py:722
  289.3 1.5 copy.12
Async XLA Ops:
  11.3 5.7 %copy-start.3 = (s32[125,120]{1,0:T(8,128)S(1)}, s32[125,120]{1,0:T(8,128)}, u32[]{:S(2)}) copy-start(s32[125,120]{1,0:T(8,128)} %get-tuple-element.11.index_ref) | copy-start | bytes 180004
  35.1 2.2 copy-start.1
  149.6 2.4 copy-start
  179.3 1.5 copy-start.2

commit v3 on v2

--- a/solution.py
+++ b/solution.py
@@ -22,8 +22,9 @@
 SLOTS = 2 * TILES
 HALF = 64
 LANES = 128
-ROWS = 160
-PLANE = 32
+ROWS = 128
+PLANE = 24
+CORNERS = 5 * PLANE
 PACKED = 2 * TILES + CELLS_Z + CHUNKS + 1
 
 NODES = 10125
@@ -33,28 +34,28 @@
 N_BAND = 4
 
 
-def plane_rows():
-    rows = {(0, 0): 0, (4, 0): 8, (0, 4): 16, (4, 4): 24}
+def row_of_node(a, b, c):
+    if (b, c) == (4, 4):
+        return CORNERS + a
+    rows = {(0, 0): 0, (4, 0): 8, (0, 4): 16, (1, 1): 7, (1, 2): 15, (1, 3): 23}
     for k in (1, 2, 3):
         rows[(0, k)] = k
         rows[(4, k)] = 8 + k
         rows[(k, 0)] = 3 + k
         rows[(k, 4)] = 16 + 3 + k
-    rows[(1, 1)] = 7
-    for k in (1, 2, 3):
         rows[(2, k)] = 8 + 3 + k
         rows[(3, k)] = 16 + k
-    rows[(1, 2)] = 24 + 1
-    rows[(1, 3)] = 24 + 7
-    return rows
-
-
-def local_rows():
-    rows = plane_rows()
-    return [PLANE * a + rows[(b, c)] for a in range(5) for b in range(5) for c in range(5)]
-
-
-LOCAL_ROWS = local_rows()
+    return PLANE * a + rows[(b, c)]
+
+
+def node_rows(planes, chosen):
+    return [
+        (25 * a + 5 * b + c, row_of_node(a, b, c))
+        for a in planes for b in range(5) for c in range(5) if chosen(b, c)
+    ]
+
+
+LOCAL_ROWS = [row for _, row in node_rows(range(5), lambda b, c: True)]
 
 
 def row_selector():
@@ -132,7 +133,9 @@
     )
     high = stiff.astype(jnp.bfloat16)
     low = (stiff - high.astype(jnp.float32)).astype(jnp.bfloat16)
-    stiffness_ref[...] = jnp.concatenate([high, high, low], axis=1)
+    stiffness_ref[...] = jnp.concatenate(
+        [jnp.concatenate([high, high], axis=1), jnp.concatenate([low, low], axis=1)], axis=0
+    )
 
 
 def make_layout(connectivity, coefficients, stiffness):
@@ -144,7 +147,7 @@
             jax.ShapeDtypeStruct((125, cells), jnp.int32),
             jax.ShapeDtypeStruct((TILES, LANES), jnp.float32),
             jax.ShapeDtypeStruct((TILES, LANES), jnp.float32),
-            jax.ShapeDtypeStruct((ROWS, 3 * ROWS), jnp.bfloat16),
+            jax.ShapeDtypeStruct((2 * ROWS, 2 * ROWS), jnp.bfloat16),
         ),
         in_specs=[whole] * 4,
         out_specs=(whole,) * 4,
@@ -152,49 +155,36 @@
     )(connectivity, coefficients, stiffness, row_selector())
 
 
-def gather_kernel(index_ref, waves_ref, cells_ref):
-    low_half = lax.broadcasted_iota(jnp.int32, (1, LANES), 1) < HALF
-    cells_ref[...] = jnp.zeros_like(cells_ref)
-
-    def body(t, carry):
-        for node, row in enumerate(LOCAL_ROWS):
-            first = waves_ref[pl.ds(index_ref[node, 2 * t], 1), :]
-            second = waves_ref[pl.ds(index_ref[node, 2 * t + 1], 1), :]
-            cells_ref[t, row : row + 1, :] = jnp.where(low_half, first, second)
-        return carry
-
-    lax.fori_loop(0, TILES, body, 0)
-
-
-def gather_cells(index, doubled):
-    return pl.pallas_call(
-        gather_kernel,
-        out_shape=jax.ShapeDtypeStruct((TILES, ROWS, LANES), jnp.float32),
-        in_specs=[pl.BlockSpec(memory_space=pltpu.SMEM), pl.BlockSpec(memory_space=pltpu.VMEM)],
-        out_specs=pl.BlockSpec(memory_space=pltpu.VMEM),
-        compiler_params=pltpu.CompilerParams(vmem_limit_bytes=40 * 2**20),
-        name="gather_cells",
-    )(index, doubled)
+def each_node_once(planes, visit):
+    def loop(count, tile_of, nodes):
+        def body(i, carry):
+            visit(tile_of(i), nodes)
+            return carry
+
+        lax.fori_loop(0, count, body, 0)
+
+    loop(TILES, lambda i: i, node_rows(planes, lambda b, c: b < 4 and c < 4))
+    loop(CELLS_Z, lambda i: TILES - CELLS_Z + i, node_rows(planes, lambda b, c: b == 4))
+    loop(CHUNKS, lambda i: i * CELLS_Z + CELLS_Z - 1, node_rows(planes, lambda b, c: b < 4 and c == 4))
 
 
 def scatter_kernel(index_ref, cells_ref, packed_ref, weight_ref, nodes_ref, rows_ref):
     lane = lax.broadcasted_iota(jnp.int32, (ROWS, LANES), 1)
     row_at = lax.broadcasted_iota(jnp.int32, (ROWS, LANES), 0)
     inner = lax.axis_index("space") > 0
-    weight = jnp.where((row_at < PLANE) & inner, 0.0, 1.0)
+    weight = jnp.where(((row_at < PLANE) | (row_at == CORNERS)) & inner, 0.0, 1.0)
     nodes_ref[NODES - NODES % 8 :, :] = jnp.zeros((2 * PAIRS - NODES + NODES % 8, LANES), jnp.float32)
 
-    def body(t, carry):
+    def visit(t, nodes):
         values = cells_ref[t]
         turned = pltpu.roll(values, HALF, 1)
         rows_ref[0] = jnp.where(lane < HALF, values, weight)
         rows_ref[1] = jnp.where(lane < HALF, turned, weight)
-        for node, row in enumerate(LOCAL_ROWS):
+        for node, row in nodes:
             nodes_ref[pl.ds(index_ref[node, 2 * t], 1), :] = rows_ref[0, row : row + 1, :]
             nodes_ref[pl.ds(index_ref[node, 2 * t + 1], 1), :] = rows_ref[1, row : row + 1, :]
-        return carry
-
-    lax.fori_loop(0, TILES, body, 0)
+
+    each_node_once(range(5), visit)
     low_half = lax.broadcasted_iota(jnp.int32, (BLOCK, LANES), 1) < HALF
 
     def pack(i, carry):
@@ -226,8 +216,8 @@
 
 
 def filter_kernel(
-    start_ref, stiff_ref, mass_ref, scale_ref, potential_ref, out_ref,
-    other, product, face, halves, sends, receives, send_sems, receive_sems,
+    index_ref, waves_ref, stiff_ref, mass_ref, scale_ref, potential_ref, out_ref,
+    other, product, face, doubled, sends, receives, send_sems, receive_sems,
 ):
     count = lax.axis_size("space")
     me = lax.axis_index("space")
@@ -244,9 +234,26 @@
     corner = sub == 0
     along_y = sub <= 3
     along_z = corner | ((sub >= 4) & (sub <= 6))
-    in_z_group = (sub >= 1) & (sub <= 3)
     in_y_group = (sub >= 4) & (sub <= 6)
+    in_z_group = ((sub >= 1) & (sub <= 3)) | (sub == 7)
     low_half = lane < HALF
+    corners = slice(CORNERS, CORNERS + 8)
+    last_tile = TILES - 1
+    bottom, top = 0, 4
+    inner = (1, 2, 3)
+
+    def group(a, g):
+        return slice(PLANE * a + 8 * g, PLANE * a + 8 * g + 8)
+
+    def turn(value, by):
+        return pltpu.roll(value, by % 8, 0) if by % 8 else value
+
+    def over_chunks(body):
+        def step(c, carry):
+            body(c)
+            return carry
+
+        lax.fori_loop(0, CHUNKS, step, 0)
 
     def copy(step, way):
         return pltpu.make_async_remote_copy(
@@ -258,209 +265,227 @@
             device_id_type=MESH,
         )
 
-    def groups(ref, t, first):
-        return [ref[t, first + 8 * g : first + 8 * g + 8, :] for g in range(4)]
-
     def pack(way, c, tiles):
-        for z, (a, b, y, d) in enumerate(tiles):
+        for z, (own, y, d) in enumerate(tiles):
             t = c * CELLS_Z + z
-            sends[way, 2 * t] = a
-            inside = jnp.where(in_z_group, y, jnp.where(in_y_group, b, d))
-            sends[way, 2 * t + 1] = jnp.where(corner, pltpu.roll(d, 7, 0), inside)
+            sends[way, 2 * t] = own
+            sends[way, 2 * t + 1] = jnp.where(corner, turn(y, 1), jnp.where(in_y_group, y, d))
         sends[way, 2 * TILES + CELLS_Z + c] = tiles[CELLS_Z - 1][2]
 
         @pl.when(c == CHUNKS - 1)
         def _():
             for z in range(CELLS_Z):
                 sends[way, 2 * TILES + z] = tiles[z][1]
-            sends[way, PACKED - 1] = tiles[CELLS_Z - 1][3]
 
     def unpack(step, way, c, z):
         t = c * CELLS_Z + z
-        a = receives[step, way, 2 * t]
         inside = receives[step, way, 2 * t + 1]
-        turned = pltpu.roll(inside, 1, 0)
-        b = jnp.where(in_y_group, inside, receives[step, way, 2 * TILES + z])
-        y = jnp.where(in_z_group, inside, receives[step, way, 2 * TILES + CELLS_Z + c])
-        d = jnp.where(sub == 7, inside, jnp.where(sub == 1, turned, receives[step, way, PACKED - 1]))
-        return [a, b, y, d]
-
-    def fill(ref, first):
-        def body(c, carry):
-            nxt = lax.rem(c + 1, CHUNKS)
-            last = c == CHUNKS - 1
-            shared = jnp.logical_or(jnp.logical_not(last), low_half)
-
-            def from_next(value):
-                return jnp.where(last, pltpu.roll(value, HALF, 1), value)
-
-            tiles = [groups(ref, c * CELLS_Z + z, first) for z in range(CELLS_Z)]
-            b_new = []
+        edge = receives[step, way, 2 * TILES + z]
+        y = jnp.where(in_y_group, inside, jnp.where(sub == 7, turn(inside, 7), edge))
+        d = jnp.where(in_z_group, inside, receives[step, way, 2 * TILES + CELLS_Z + c])
+        return [receives[step, way, 2 * t], y, d]
+
+    def unpack_corner(step, way):
+        return turn(receives[step, way, PACKED - 1], 4)
+
+    def fill(ref, planes):
+        end = ref[last_tile, corners, :]
+        for a in planes:
             for z in range(CELLS_Z):
-                ahead = from_next(ref[nxt * CELLS_Z + z, first : first + 8, :])
-                b_new.append(jnp.where(along_y & shared, ahead, tiles[z][1]))
+                ref[TILES + z, group(a, 0), :] = jnp.where(
+                    low_half, pltpu.roll(ref[z, group(a, 0), :], HALF, 1), ref[TILES - CELLS_Z + z, group(a, 1), :]
+                )
+            ref[TILES + CELLS_Z - 1, group(a, 2), :] = jnp.where(
+                low_half, pltpu.roll(ref[CELLS_Z - 1, group(a, 2), :], HALF, 1), turn(end, -a)
+            )
+
+        def body(c):
+            first = c * CELLS_Z
+            ends = [ref[first + z, corners, :] for z in range(CELLS_Z)]
+            for a in planes:
+                y_new = [
+                    jnp.where(along_y, ref[first + CELLS_Z + z, group(a, 0), :], ref[first + z, group(a, 1), :])
+                    for z in range(CELLS_Z)
+                ]
+                for z in range(CELLS_Z):
+                    ref[first + z, group(a, 1), :] = y_new[z]
+                    if z < CELLS_Z - 1:
+                        ref[first + z, group(a, 2), :] = jnp.where(
+                            along_z, ref[first + z + 1, group(a, 0), :], ref[first + z, group(a, 2), :]
+                        )
+                        ahead = y_new[z + 1]
+                    else:
+                        ahead = ref[first + CELLS_Z + z, group(a, 2), :]
+                    ends[z] = jnp.where(sub == a, turn(ahead, a), ends[z])
             for z in range(CELLS_Z):
-                t = c * CELLS_Z + z
-                ref[t, first + 8 : first + 16, :] = b_new[z]
-                if z < CELLS_Z - 1:
-                    ref[t, first + 16 : first + 24, :] = jnp.where(along_z, tiles[z + 1][0], tiles[z][2])
-                    ref[t, first + 24 : first + 32, :] = jnp.where(corner, b_new[z + 1], tiles[z][3])
-                else:
-                    ahead = from_next(ref[nxt * CELLS_Z + z, first + 16 : first + 24, :])
-                    ref[t, first + 24 : first + 32, :] = jnp.where(corner & shared, ahead, tiles[z][3])
-            return carry
-
-        lax.fori_loop(0, CHUNKS, body, 0)
-
-    def assembled(c, first):
-        prv = lax.rem(c + CHUNKS - 1, CHUNKS)
-        is_first = c == 0
-
-        def from_previous(value):
-            return jnp.where(is_first, jnp.where(low_half, 0.0, pltpu.roll(value, HALF, 1)), value)
-
-        tiles = [groups(product, c * CELLS_Z + z, first) for z in range(CELLS_Z)]
+                ref[first + z, corners, :] = ends[z]
+
+        over_chunks(body)
+
+    def assembled(c, a):
+        tiles, corner_terms = [], []
         for z in range(CELLS_Z):
-            _, b, _, d = groups(product, prv * CELLS_Z + z, first)
-            tiles[z][0] = tiles[z][0] + jnp.where(along_y, from_previous(b), 0.0)
-            tiles[z][2] = tiles[z][2] + jnp.where(corner, from_previous(d), 0.0)
+            t = c * CELLS_Z + z
+            own, y, d = [product[t + CELLS_Z, group(a, g), :] for g in range(3)]
+            own = own + jnp.where(along_y, product[t, group(a, 1), :], 0.0)
+            d = d + jnp.where(corner, turn(product[t, corners, :], -a), 0.0)
+            tiles.append([own, y, d])
+            corner_terms.append(turn(product[t + CELLS_Z, corners, :], -a))
         for z in range(1, CELLS_Z):
             tiles[z][0] = tiles[z][0] + jnp.where(along_z, tiles[z - 1][2], 0.0)
-            tiles[z][1] = tiles[z][1] + jnp.where(corner, tiles[z - 1][3], 0.0)
+            tiles[z][1] = tiles[z][1] + jnp.where(corner, corner_terms[z - 1], 0.0)
         return tiles
 
-    def chunk_of(ref, c, rows):
-        return jnp.concatenate([ref[c * CELLS_Z + z, rows, :] for z in range(CELLS_Z)], axis=1)
-
-    def multiply(current, parts, split):
-        stiff = jnp.concatenate([stiff_ref[part, :] for part in parts], axis=0)
-        mass = jnp.concatenate([mass_ref[part, :] for part in parts], axis=0)
-
-        def body(c, carry):
-            if split:
-                x = chunk_of(current, c, slice(0, ROWS))
-                high = x.astype(jnp.bfloat16)
-                low = (x - high.astype(jnp.float32)).astype(jnp.bfloat16)
-                halves[c, 0:ROWS, :] = high
-                halves[c, ROWS : 2 * ROWS, :] = low
-            else:
-                high = halves[c, 0:ROWS, :]
-                low = halves[c, ROWS : 2 * ROWS, :]
-            operand = jnp.concatenate([high, low, high], axis=0)
-            result = jnp.dot(stiff, operand, preferred_element_type=jnp.float32)
-            for z in range(CELLS_Z):
-                t = c * CELLS_Z + z
-                values = jnp.concatenate([current[t, part, :] for part in parts], axis=0)
-                term = result[:, z * LANES : (z + 1) * LANES] * scale_ref[pl.ds(t, 1), :] + (
-                    mass * potential_ref[pl.ds(t, 1), :] * values
+    def multiply(current):
+        mass = mass_ref[...]
+        stiff = stiff_ref[...]
+
+        def body(c):
+            for pair in range(CELLS_Z // 2):
+                t = c * CELLS_Z + 2 * pair
+                values = [current[t], current[t + 1]]
+                high, low = split(jnp.concatenate(values, axis=1))
+                result = jnp.dot(
+                    stiff, jnp.concatenate([high, low], axis=0), preferred_element_type=jnp.float32
                 )
-                at = 0
-                for part in parts:
-                    size = part.stop - part.start
-                    product[t, part, :] = term[at : at + size]
-                    at += size
-            return carry
-
-        lax.fori_loop(0, CHUNKS, body, 0)
-
-    def advanced(step, current, previous, t, rows, total):
+                result = result[:ROWS] + result[ROWS:]
+                for k in range(2):
+                    product[t + CELLS_Z + k] = result[:, k * LANES : (k + 1) * LANES] * scale_ref[
+                        pl.ds(t + k, 1), :
+                    ] + mass * potential_ref[pl.ds(t + k, 1), :] * values[k]
+
+        over_chunks(body)
+        for z in range(CELLS_Z):
+            for rows in [group(a, 1) for a in range(5)] + [corners]:
+                turned = pltpu.roll(product[TILES + z, rows, :], HALF, 1)
+                product[z, rows, :] = jnp.where(low_half, 0.0, turned)
+
+    def advance(step, current, previous, t, rows, total):
         value = total - CENTER * current[t, rows, :]
         if step == 0:
-            return value * (1.0 / HALF_WIDTH)
-        return value * (2.0 / HALF_WIDTH) - previous[t, rows, :]
-
-    def advance_inner(step, current, previous, first):
-        def body(c, carry):
-            tiles = assembled(c, first)
+            previous[t, rows, :] = value * (1.0 / HALF_WIDTH)
+        else:
+            previous[t, rows, :] = value * (2.0 / HALF_WIDTH) - previous[t, rows, :]
+
+    def advance_inner(step, current, previous):
+        def body(c):
+            for a in inner:
+                tiles = assembled(c, a)
+                for z in range(CELLS_Z):
+                    for g in range(3):
+                        advance(step, current, previous, c * CELLS_Z + z, group(a, g), tiles[z][g])
+
+        over_chunks(body)
+
+    def send_face(way, a):
+        def body(c):
+            tiles = assembled(c, a)
             for z in range(CELLS_Z):
-                t = c * CELLS_Z + z
-                for g in range(4):
-                    rows = slice(first + 8 * g, first + 8 * g + 8)
-                    previous[t, rows, :] = advanced(step, current, previous, t, rows, tiles[z][g])
-            return carry
-
-        lax.fori_loop(0, CHUNKS, body, 0)
-        fill(previous, first)
-
-    def send_face(way, first):
-        def body(c, carry):
-            tiles = assembled(c, first)
-            for z in range(CELLS_Z):
-                for g in range(4):
+                for g in range(3):
                     face[way, c * CELLS_Z + z, 8 * g : 8 * g + 8, :] = tiles[z][g]
             pack(way, c, tiles)
-            return carry
-
-        lax.fori_loop(0, CHUNKS, body, 0)
-
-    def advance_face(step, current, previous, way, first, valid):
-        def body(c, carry):
+
+        over_chunks(body)
+        sends[way, PACKED - 1] = product[TILES + CELLS_Z - 1, corners, :]
+
+    def advance_face(step, current, previous, way, a, valid):
+        def body(c):
             for z in range(CELLS_Z):
                 t = c * CELLS_Z + z
                 arrived = unpack(step + 1, way, c, z)
-                for g in range(4):
-                    rows = slice(first + 8 * g, first + 8 * g + 8)
+                for g in range(3):
                     total = face[1 - way, t, 8 * g : 8 * g + 8, :] + jnp.where(valid, arrived[g], 0.0)
-                    previous[t, rows, :] = advanced(step, current, previous, t, rows, total)
-            return carry
-
-        lax.fori_loop(0, CHUNKS, body, 0)
-        fill(previous, first)
-
-    top = 4 * PLANE
-
-    def pack_start(c, carry):
-        pack(0, c, [groups(start_ref, c * CELLS_Z + z, top) for z in range(CELLS_Z)])
+                    advance(step, current, previous, t, group(a, g), total)
+
+        over_chunks(body)
+
+    def advance_corner(step, current, previous):
+        total = product[TILES + CELLS_Z - 1, corners, :]
+        total = total + jnp.where((sub == bottom) & has_below, unpack_corner(step + 1, 0), 0.0)
+        total = total + jnp.where((sub == top) & has_above, unpack_corner(step + 1, 1), 0.0)
+        advance(step, current, previous, last_tile, corners, total)
+
+    node_count = waves_ref.shape[1]
+    whole_blocks = node_count // LANES
+
+    def transpose(i, carry):
+        at = pl.ds(pl.multiple_of(i * LANES, LANES), LANES)
+        block = waves_ref[:, at]
+        doubled[at, :] = jnp.concatenate([block, block], axis=0).T
         return carry
 
-    lax.fori_loop(0, CHUNKS, pack_start, 0)
+    lax.fori_loop(0, whole_blocks, transpose, 0)
+    rest = node_count - whole_blocks * LANES
+    block = jnp.concatenate(
+        [waves_ref[:, whole_blocks * LANES :], jnp.zeros((HALF, LANES - rest), jnp.float32)], axis=1
+    )
+    doubled[whole_blocks * LANES : (whole_blocks + 1) * LANES, :] = jnp.concatenate([block, block], axis=0).T
+
+    out_ref[...] = jnp.zeros_like(out_ref)
+    low_row = lax.broadcasted_iota(jnp.int32, (1, LANES), 1) < HALF
+
+    def gather(t, nodes):
+        for node, row in nodes:
+            first = doubled[pl.ds(index_ref[node, 2 * t], 1), :]
+            second = doubled[pl.ds(index_ref[node, 2 * t + 1], 1), :]
+            out_ref[t, row : row + 1, :] = jnp.where(low_row, first, second)
+
+    each_node_once((top,), gather)
+    over_chunks(
+        lambda c: pack(0, c, [[out_ref[c * CELLS_Z + z, group(top, g), :] for g in range(3)] for z in range(CELLS_Z)])
+    )
+    sends[0, PACKED - 1] = out_ref[last_tile, corners, :]
     owner = copy(0, 0)
     owner.start()
-    out_ref[...] = start_ref[...]
+    each_node_once((0, 1, 2, 3), gather)
     owner.wait()
 
-    def take_owner(c, carry):
+    def take_owner(c):
         for z in range(CELLS_Z):
             t = c * CELLS_Z + z
             arrived = unpack(0, 0, c, z)
-            for g in range(4):
-                rows = slice(8 * g, 8 * g + 8)
-                out_ref[t, rows, :] = jnp.where(has_below, arrived[g], out_ref[t, rows, :])
-        return carry
-
-    lax.fori_loop(0, CHUNKS, take_owner, 0)
-    fill(out_ref, 0)
+            for g in range(3):
+                out_ref[t, group(bottom, g), :] = jnp.where(has_below, arrived[g], out_ref[t, group(bottom, g), :])
+
+    over_chunks(take_owner)
+    out_ref[last_tile, corners, :] = jnp.where(
+        (sub == bottom) & has_below, unpack_corner(0, 0), out_ref[last_tile, corners, :]
+    )
+    fill(out_ref, range(5))
 
     for step in range(FILTER_DEG):
         current, previous = (out_ref, other) if step % 2 == 0 else (other, out_ref)
-        multiply(current, [slice(0, PLANE), slice(top, ROWS)], True)
+        if step == 0:
+            other[...] = jnp.zeros_like(other)
+        multiply(current)
         copies = [copy(step + 1, 0), copy(step + 1, 1)]
-        for way, first in ((0, top), (1, 0)):
-            send_face(way, first)
+        for way, a in ((0, top), (1, bottom)):
+            send_face(way, a)
             copies[way].start()
-        multiply(current, [slice(PLANE, top)], False)
-        for a in range(1, 4):
-            advance_inner(step, current, previous, PLANE * a)
+        advance_inner(step, current, previous)
         copies[0].wait()
-        advance_face(step, current, previous, 0, 0, has_below)
+        advance_face(step, current, previous, 0, bottom, has_below)
         copies[1].wait()
         advance_face(step, current, previous, 1, top, has_above)
-
-
-def filter_cells(start, stiff, scale, potential):
+        advance_corner(step, current, previous)
+        fill(previous, range(5))
+
+
+def filter_cells(index, wavefunctions, stiff, scale, potential):
     whole = pl.BlockSpec(memory_space=pltpu.VMEM)
-    cells = (TILES, ROWS, LANES)
+    cells = (TILES + CELLS_Z, ROWS, LANES)
     rounds = FILTER_DEG + 1
+    blocks = wavefunctions.shape[1] // LANES + 1
     return pl.pallas_call(
         filter_kernel,
         out_shape=jax.ShapeDtypeStruct(cells, jnp.float32),
-        in_specs=[whole] * 5,
+        in_specs=[pl.BlockSpec(memory_space=pltpu.SMEM)] + [whole] * 5,
         out_specs=whole,
         scratch_shapes=[
             pltpu.VMEM(cells, jnp.float32),
             pltpu.VMEM(cells, jnp.float32),
             pltpu.VMEM((2, TILES, PLANE, LANES), jnp.float32),
-            pltpu.VMEM((CHUNKS, 2 * ROWS, CELLS_Z * LANES), jnp.bfloat16),
+            pltpu.VMEM((blocks * LANES, LANES), jnp.float32),
             pltpu.VMEM((2, PACKED, 8, LANES), jnp.float32),
             pltpu.VMEM((rounds, 2, PACKED, 8, LANES), jnp.float32),
             pltpu.SemaphoreType.DMA((rounds, 2)),
@@ -470,7 +495,7 @@
             collective_id=0, has_side_effects=True, vmem_limit_bytes=56 * 2**20
         ),
         name="filter_cells",
-    )(start, stiff, row_mass(), scale, potential)
+    )(index, wavefunctions, stiff, row_mass(), scale, potential)
 
 
 def split(x):
@@ -492,16 +517,23 @@
     wide = jnp.where(lane == row_at + size, 1.0, wide)
     tiles = [wide[8 * g : 8 * g + 8] for g in range(size // 8)]
     sub = lax.broadcasted_iota(jnp.int32, (8, LANES), 0)
-    for j in range(size):
-        home, at = divmod(j, 8)
-        columns = [jnp.broadcast_to(tile[:, j : j + 1], (8, LANES)) for tile in tiles[home:]]
-        row = tiles[home][at : at + 1, :]
-        ratio = row * (1.0 / columns[0][at : at + 1, :])
-        for g in range(home, size // 8):
-            factor = columns[g - home]
-            if g == home:
-                factor = jnp.where(sub > at, factor, 0.0)
-            tiles[g] = tiles[g] - factor * ratio
+    for home in range(size // 8):
+        live = range(home, size // 8)
+        columns = {
+            (g, n): jnp.broadcast_to(tiles[g][:, 8 * home + n : 8 * home + n + 1], (8, LANES))
+            for g in live for n in range(8)
+        }
+        for at in range(8):
+            scale = 1.0 / columns[home, at][at : at + 1, :]
+            ratio = tiles[home][at : at + 1, :] * scale
+            ahead = {n: columns[home, n][at : at + 1, :] * scale for n in range(at + 1, 8)}
+            for g in live:
+                factor = columns[g, at]
+                if g == home:
+                    factor = jnp.where(sub > at, factor, 0.0)
+                for n in range(at + 1, 8):
+                    columns[g, n] = columns[g, n] - factor * ahead[n]
+                tiles[g] = tiles[g] - factor * ratio
     wide = jnp.concatenate(tiles, axis=0)
     pivots = jnp.sum(jnp.where(lane == row_at, wide, 0.0), axis=1, keepdims=True)
     return wide[:, size:] * (1.0 / jnp.sqrt(pivots))
@@ -748,9 +780,7 @@
 
     coefficients = jnp.stack([cell_scale, cell_potential])
     index, scale, potential, stiff = make_layout(connectivity, coefficients, stiffness)
-    doubled = jnp.concatenate([wavefunctions, wavefunctions], axis=0).T
-    cells = gather_cells(index, doubled)
-    cells = filter_cells(cells, stiff, scale, potential)
+    cells = filter_cells(index, wavefunctions, stiff, scale, potential)
     packed, weight = scatter_nodes(index, cells)
     return finish(packed, weight, owned_count)[:, :node_count]
 

time: 292 us -> 237 us (0.81)
  Pallas kernels: 269 us -> 228 us
  local copies, waits for them, and re-layouts: 14.3 us -> 6.75 us
  other arithmetic: 6.99 us -> 1.26 us
    pallas_call x1 -> x0, Pallas kernels: 18.1 us -> none  [gather_cells(): pl.pallas_call(gather_kernel, out_shape=jax.ShapeDtypeStruct((TILES, ROWS...]
    pallas_call x1, Pallas kernels: 108 us -> 93.8 us  [finish(): pl.pallas_call(functools.partial(finish_kernel, owned_count), out_shape=j...]
    unnamed x11 -> x8, local copies, waits for them, and re-layouts: 14.3 us -> 6.75 us
    pallas_call x1, Pallas kernels: 27.4 us -> 21.4 us  [scatter_nodes(): pl.pallas_call(scatter_kernel, out_shape=(packed, packed), in_specs=[pl.B...]
    transpose x1 -> x0, other arithmetic: 5.72 us -> none  [shards(): doubled = jnp.concatenate([wavefunctions, wavefunctions], axis=0).T]
where the time goes in v3:
time: 237 us; the launch traced here: 236 us
  Pallas kernels  228 us (96%)
  local copies, waits for them, and re-layouts  6.75 us (3%)
    pallas_call x1, Pallas kernels, filter_cells(): pl.pallas_call(filter_kernel, out_shape=jax.ShapeDtypeStruct(cells, jnp.f...  110 us
    pallas_call x1, Pallas kernels, finish(): pl.pallas_call(functools.partial(finish_kernel, owned_count), out_shape=j...  93.8 us
    pallas_call x1, Pallas kernels, scatter_nodes(): pl.pallas_call(scatter_kernel, out_shape=(packed, packed), in_specs=[pl.B...  21.4 us
    unnamed x8, local copies, waits for them, and re-layouts  6.75 us

profile of v3, /device:TPU:1, one launch (start us, length us, event | category | flops | bytes accessed | tf_op | source)
XLA Modules:
  0.0 236.4 jit_solution(1404651080493334913)
XLA Ops:
  0.0 1.3 pad_maximum_fusion.coef_ref
  1.3 1.6 copy.8.conn_ref
  2.8 3.0 %layout.1 = (s32[125,120]{1,0:T(8,128)}, f32[60,128]{1,0:T(8,128)}, f32[60,128]{1,0:T(8,128)}, bf16[256,256]{1,0:T(8,128)(2,1)}) custom-call(s32[125,120]{1,0:T(8,128)} %copy.8.conn_ref, f32[2,120]{1,0:T(2,128)} %pad_maximum_fusion.coef_ref, f32[125,125]{1,0:T(8,128)} %stiff_ref.1, f32[128,125]{1,0:T(8,128)} %constant.4.clone.select_ref), custom_call_target="tpu_custom_call" | custom-call | tf_op jit(solution)/shard_map/layout/pallas_call | solution.py:144
  5.8 0.0 copy-start.2
  5.9 110.2 %filter_cells.1.cells_ref = f32[66,128,128]{2,1,0:T(8,128)} custom-call(s32[125,120]{1,0:T(8,128)} %get-tuple-element.11.index_ref, f32[64,10125]{1,0:T(8,128)} %waves_ref.1, bf16[256,256]{1,0:T(8,128)(2,1)} %get-tuple-element.12.stiff_ref, f32[128,128]{1,0:T(8,128)} %constant.5.clone.mass_ref, f32[60,128]{1,0:T(8,128)} %get-tuple-element.13.scale_ref, ...), custom_call_target="tpu_custom_call" | custom-call | tf_op jit(solution)/shard_map/filter_cells/pallas_call | solution.py:479
  116.0 0.0 copy-done.2
  116.0 0.0 copy-start
  116.0 2.2 copy-done
  118.3 21.4 %scatter_nodes.1 = (f32[5120,128]{1,0:T(8,128)S(1)}, f32[5120,128]{1,0:T(8,128)S(1)}) custom-call(s32[125,120]{1,0:T(8,128)S(1)} %copy-done.2, f32[66,128,128]{2,1,0:T(8,128)S(1)} %copy-done), custom_call_target="tpu_custom_call" | custom-call | tf_op jit(solution)/shard_map/scatter_nodes/pallas_call | solution.py:204
  139.6 0.0 copy-start.1
  139.6 1.5 copy-done.1
  141.1 93.8 %finish.1 = f32[64,10240]{1,0:T(8,128)S(1)} custom-call(f32[5120,128]{1,0:T(8,128)S(1)} %get-tuple-element.15.own, f32[5120,128]{1,0:T(8,128)} %copy-done.1), custom_call_target="tpu_custom_call" | custom-call | tf_op jit(solution)/shard_map/finish/pallas_call | solution.py:754
  234.9 1.5 copy.10
Async XLA Ops:
  5.8 110.2 %copy-start.2 = (s32[125,120]{1,0:T(8,128)S(1)}, s32[125,120]{1,0:T(8,128)}, u32[]{:S(2)}) copy-start(s32[125,120]{1,0:T(8,128)} %get-tuple-element.11.index_ref) | copy-start | bytes 180004
  116.0 2.2 copy-start
  139.6 1.5 copy-start.1

commit v4 on v3

--- a/solution.py
+++ b/solution.py
@@ -25,7 +25,8 @@
 ROWS = 128
 PLANE = 24
 CORNERS = 5 * PLANE
-PACKED = 2 * TILES + CELLS_Z + CHUNKS + 1
+MESSAGE = 2 * CELLS_Z + 1
+EDGE = CELLS_Z + 1
 
 NODES = 10125
 PAIRS = 5120
@@ -156,15 +157,16 @@
 
 
 def each_node_once(planes, visit):
-    def loop(count, tile_of, nodes):
+    def loop(count, tile_of, nodes, halves=(0, 1)):
         def body(i, carry):
-            visit(tile_of(i), nodes)
+            visit(tile_of(i), nodes, halves)
             return carry
 
         lax.fori_loop(0, count, body, 0)
 
     loop(TILES, lambda i: i, node_rows(planes, lambda b, c: b < 4 and c < 4))
-    loop(CELLS_Z, lambda i: TILES - CELLS_Z + i, node_rows(planes, lambda b, c: b == 4))
+    loop(CELLS_Z, lambda i: TILES - CELLS_Z + i, node_rows(planes, lambda b, c: b == 4 and c < 4), (1,))
+    loop(1, lambda i: TILES - 1, node_rows(planes, lambda b, c: b == 4 and c == 4), (1,))
     loop(CHUNKS, lambda i: i * CELLS_Z + CELLS_Z - 1, node_rows(planes, lambda b, c: b < 4 and c == 4))
 
 
@@ -175,14 +177,14 @@
     weight = jnp.where(((row_at < PLANE) | (row_at == CORNERS)) & inner, 0.0, 1.0)
     nodes_ref[NODES - NODES % 8 :, :] = jnp.zeros((2 * PAIRS - NODES + NODES % 8, LANES), jnp.float32)
 
-    def visit(t, nodes):
+    def visit(t, nodes, halves):
         values = cells_ref[t]
         turned = pltpu.roll(values, HALF, 1)
         rows_ref[0] = jnp.where(lane < HALF, values, weight)
         rows_ref[1] = jnp.where(lane < HALF, turned, weight)
         for node, row in nodes:
-            nodes_ref[pl.ds(index_ref[node, 2 * t], 1), :] = rows_ref[0, row : row + 1, :]
-            nodes_ref[pl.ds(index_ref[node, 2 * t + 1], 1), :] = rows_ref[1, row : row + 1, :]
+            for half in halves:
+                nodes_ref[pl.ds(index_ref[node, 2 * t + half], 1), :] = rows_ref[half, row : row + 1, :]
 
     each_node_once(range(5), visit)
     low_half = lax.broadcasted_iota(jnp.int32, (BLOCK, LANES), 1) < HALF
@@ -217,7 +219,8 @@
 
 def filter_kernel(
     index_ref, waves_ref, stiff_ref, mass_ref, scale_ref, potential_ref, out_ref,
-    other, product, face, doubled, sends, receives, send_sems, receive_sems,
+    other, product, face, doubled, sends, edge_sends, receives, edge_receives,
+    send_sems, receive_sems, edge_send_sems, edge_receive_sems,
 ):
     count = lax.axis_size("space")
     me = lax.axis_index("space")
@@ -255,72 +258,95 @@
 
         lax.fori_loop(0, CHUNKS, step, 0)
 
-    def copy(step, way):
+    def message(step, way, c):
         return pltpu.make_async_remote_copy(
-            src_ref=sends.at[way],
-            dst_ref=receives.at[step, way],
-            send_sem=send_sems.at[step, way],
-            recv_sem=receive_sems.at[step, way],
+            src_ref=sends.at[way, c],
+            dst_ref=receives.at[step, way, c],
+            send_sem=send_sems.at[step, way, c],
+            recv_sem=receive_sems.at[step, way, c],
             device_id={"space": above if way == 0 else below},
             device_id_type=MESH,
         )
 
-    def pack(way, c, tiles):
+    def edge_message(step, way):
+        return pltpu.make_async_remote_copy(
+            src_ref=edge_sends.at[way],
+            dst_ref=edge_receives.at[step, way],
+            send_sem=edge_send_sems.at[step, way],
+            recv_sem=edge_receive_sems.at[step, way],
+            device_id={"space": above if way == 0 else below},
+            device_id_type=MESH,
+        )
+
+    def start(copy, way):
+        @pl.when(has_above if way == 0 else has_below)
+        def _():
+            copy.start()
+
+    def finish_copy(copy, way):
+        @pl.when(has_above if way == 0 else has_below)
+        def _():
+            copy.wait_send()
+
+        @pl.when(has_below if way == 0 else has_above)
+        def _():
+            copy.wait_recv()
+
+    def send_chunk(step, way, c, tiles, ends):
         for z, (own, y, d) in enumerate(tiles):
-            t = c * CELLS_Z + z
-            sends[way, 2 * t] = own
-            sends[way, 2 * t + 1] = jnp.where(corner, turn(y, 1), jnp.where(in_y_group, y, d))
-        sends[way, 2 * TILES + CELLS_Z + c] = tiles[CELLS_Z - 1][2]
+            sends[way, c, 2 * z] = own
+            sends[way, c, 2 * z + 1] = jnp.where(corner, turn(y, 1), jnp.where(in_y_group, y, d))
+        sends[way, c, MESSAGE - 1] = tiles[CELLS_Z - 1][2]
+        start(message(step, way, c), way)
 
         @pl.when(c == CHUNKS - 1)
         def _():
             for z in range(CELLS_Z):
-                sends[way, 2 * TILES + z] = tiles[z][1]
+                edge_sends[way, z] = tiles[z][1]
+            edge_sends[way, EDGE - 1] = ends
+            start(edge_message(step, way), way)
 
     def unpack(step, way, c, z):
-        t = c * CELLS_Z + z
-        inside = receives[step, way, 2 * t + 1]
-        edge = receives[step, way, 2 * TILES + z]
-        y = jnp.where(in_y_group, inside, jnp.where(sub == 7, turn(inside, 7), edge))
-        d = jnp.where(in_z_group, inside, receives[step, way, 2 * TILES + CELLS_Z + c])
-        return [receives[step, way, 2 * t], y, d]
+        inside = receives[step, way, c, 2 * z + 1]
+        y = jnp.where(in_y_group, inside, jnp.where(sub == 7, turn(inside, 7), 0.0))
+        d = jnp.where(in_z_group, inside, receives[step, way, c, MESSAGE - 1])
+        return [receives[step, way, c, 2 * z], y, d]
 
     def unpack_corner(step, way):
-        return turn(receives[step, way, PACKED - 1], 4)
-
-    def fill(ref, planes):
-        end = ref[last_tile, corners, :]
-        for a in planes:
+        return turn(edge_receives[step, way, EDGE - 1], 4)
+
+    def fill(ref, c):
+        @pl.when(c == CHUNKS - 1)
+        def _():
+            end = ref[last_tile, corners, :]
+            for a in range(5):
+                for z in range(CELLS_Z):
+                    ref[TILES + z, group(a, 0), :] = jnp.where(
+                        low_half, pltpu.roll(ref[z, group(a, 0), :], HALF, 1), ref[TILES - CELLS_Z + z, group(a, 1), :]
+                    )
+                ref[TILES + CELLS_Z - 1, group(a, 2), :] = jnp.where(
+                    low_half, pltpu.roll(ref[CELLS_Z - 1, group(a, 2), :], HALF, 1), turn(end, -a)
+                )
+
+        first = c * CELLS_Z
+        ends = [ref[first + z, corners, :] for z in range(CELLS_Z)]
+        for a in range(5):
+            y_new = [
+                jnp.where(along_y, ref[first + CELLS_Z + z, group(a, 0), :], ref[first + z, group(a, 1), :])
+                for z in range(CELLS_Z)
+            ]
             for z in range(CELLS_Z):
-                ref[TILES + z, group(a, 0), :] = jnp.where(
-                    low_half, pltpu.roll(ref[z, group(a, 0), :], HALF, 1), ref[TILES - CELLS_Z + z, group(a, 1), :]
-                )
-            ref[TILES + CELLS_Z - 1, group(a, 2), :] = jnp.where(
-                low_half, pltpu.roll(ref[CELLS_Z - 1, group(a, 2), :], HALF, 1), turn(end, -a)
-            )
-
-        def body(c):
-            first = c * CELLS_Z
-            ends = [ref[first + z, corners, :] for z in range(CELLS_Z)]
-            for a in planes:
-                y_new = [
-                    jnp.where(along_y, ref[first + CELLS_Z + z, group(a, 0), :], ref[first + z, group(a, 1), :])
-                    for z in range(CELLS_Z)
-                ]
-                for z in range(CELLS_Z):
-                    ref[first + z, group(a, 1), :] = y_new[z]
-                    if z < CELLS_Z - 1:
-                        ref[first + z, group(a, 2), :] = jnp.where(
-                            along_z, ref[first + z + 1, group(a, 0), :], ref[first + z, group(a, 2), :]
-                        )
-                        ahead = y_new[z + 1]
-                    else:
-                        ahead = ref[first + CELLS_Z + z, group(a, 2), :]
-                    ends[z] = jnp.where(sub == a, turn(ahead, a), ends[z])
-            for z in range(CELLS_Z):
-                ref[first + z, corners, :] = ends[z]
-
-        over_chunks(body)
+                ref[first + z, group(a, 1), :] = y_new[z]
+                if z < CELLS_Z - 1:
+                    ref[first + z, group(a, 2), :] = jnp.where(
+                        along_z, ref[first + z + 1, group(a, 0), :], ref[first + z, group(a, 2), :]
+                    )
+                    ahead = y_new[z + 1]
+                else:
+                    ahead = ref[first + CELLS_Z + z, group(a, 2), :]
+                ends[z] = jnp.where(sub == a, turn(ahead, a), ends[z])
+        for z in range(CELLS_Z):
+            ref[first + z, corners, :] = ends[z]
 
     def assembled(c, a):
         tiles, corner_terms = [], []
@@ -336,74 +362,75 @@
             tiles[z][1] = tiles[z][1] + jnp.where(corner, corner_terms[z - 1], 0.0)
         return tiles
 
-    def multiply(current):
+    def multiply(current, c):
         mass = mass_ref[...]
-        stiff = stiff_ref[...]
-
-        def body(c):
-            for pair in range(CELLS_Z // 2):
-                t = c * CELLS_Z + 2 * pair
-                values = [current[t], current[t + 1]]
-                high, low = split(jnp.concatenate(values, axis=1))
-                result = jnp.dot(
-                    stiff, jnp.concatenate([high, low], axis=0), preferred_element_type=jnp.float32
-                )
-                result = result[:ROWS] + result[ROWS:]
-                for k in range(2):
-                    product[t + CELLS_Z + k] = result[:, k * LANES : (k + 1) * LANES] * scale_ref[
-                        pl.ds(t + k, 1), :
-                    ] + mass * potential_ref[pl.ds(t + k, 1), :] * values[k]
-
-        over_chunks(body)
-        for z in range(CELLS_Z):
-            for rows in [group(a, 1) for a in range(5)] + [corners]:
-                turned = pltpu.roll(product[TILES + z, rows, :], HALF, 1)
-                product[z, rows, :] = jnp.where(low_half, 0.0, turned)
-
-    def advance(step, current, previous, t, rows, total):
-        value = total - CENTER * current[t, rows, :]
-        if step == 0:
-            previous[t, rows, :] = value * (1.0 / HALF_WIDTH)
-        else:
-            previous[t, rows, :] = value * (2.0 / HALF_WIDTH) - previous[t, rows, :]
-
-    def advance_inner(step, current, previous):
-        def body(c):
-            for a in inner:
-                tiles = assembled(c, a)
-                for z in range(CELLS_Z):
-                    for g in range(3):
-                        advance(step, current, previous, c * CELLS_Z + z, group(a, g), tiles[z][g])
-
-        over_chunks(body)
-
-    def send_face(way, a):
-        def body(c):
+        for pair in range(CELLS_Z // 2):
+            t = c * CELLS_Z + 2 * pair
+            values = [current[t], current[t + 1]]
+            high, low = split(jnp.concatenate(values, axis=1))
+            result = jnp.dot(
+                stiff_ref[...], jnp.concatenate([high, low], axis=0), preferred_element_type=jnp.float32
+            )
+            result = result[:ROWS] + result[ROWS:]
+            for k in range(2):
+                product[t + CELLS_Z + k] = result[:, k * LANES : (k + 1) * LANES] * scale_ref[
+                    pl.ds(t + k, 1), :
+                ] + mass * potential_ref[pl.ds(t + k, 1), :] * values[k]
+
+        @pl.when(c == CHUNKS - 1)
+        def _():
+            for z in range(CELLS_Z):
+                for rows in [group(a, 1) for a in range(5)] + [corners]:
+                    turned = pltpu.roll(product[TILES + z, rows, :], HALF, 1)
+                    product[z, rows, :] = jnp.where(low_half, 0.0, turned)
+
+    def buffers(step):
+        return (out_ref, other) if step % 2 == 0 else (other, out_ref)
+
+    def factor(step):
+        return (1.0 if step == 0 else 2.0) / HALF_WIDTH
+
+    def advance(step, t, rows, total):
+        current, previous = buffers(step)
+        value = (total - CENTER * current[t, rows, :]) * factor(step)
+        previous[t, rows, :] = value if step == 0 else value - previous[t, rows, :]
+
+    def assemble(step, c):
+        ends = product[TILES + CELLS_Z - 1, corners, :]
+        for way, a in ((0, top), (1, bottom)):
             tiles = assembled(c, a)
             for z in range(CELLS_Z):
                 for g in range(3):
                     face[way, c * CELLS_Z + z, 8 * g : 8 * g + 8, :] = tiles[z][g]
-            pack(way, c, tiles)
-
-        over_chunks(body)
-        sends[way, PACKED - 1] = product[TILES + CELLS_Z - 1, corners, :]
-
-    def advance_face(step, current, previous, way, a, valid):
-        def body(c):
+            send_chunk(step + 1, way, c, tiles, ends)
+        for a in inner:
+            tiles = assembled(c, a)
+            for z in range(CELLS_Z):
+                for g in range(3):
+                    advance(step, c * CELLS_Z + z, group(a, g), tiles[z][g])
+
+    def advance_faces(step, c):
+        for way, a, valid in ((0, bottom, has_below), (1, top, has_above)):
+            finish_copy(message(step + 1, way, c), way)
             for z in range(CELLS_Z):
                 t = c * CELLS_Z + z
                 arrived = unpack(step + 1, way, c, z)
                 for g in range(3):
                     total = face[1 - way, t, 8 * g : 8 * g + 8, :] + jnp.where(valid, arrived[g], 0.0)
-                    advance(step, current, previous, t, group(a, g), total)
-
-        over_chunks(body)
-
-    def advance_corner(step, current, previous):
-        total = product[TILES + CELLS_Z - 1, corners, :]
-        total = total + jnp.where((sub == bottom) & has_below, unpack_corner(step + 1, 0), 0.0)
-        total = total + jnp.where((sub == top) & has_above, unpack_corner(step + 1, 1), 0.0)
-        advance(step, current, previous, last_tile, corners, total)
+                    advance(step, t, group(a, g), total)
+
+        @pl.when(c == CHUNKS - 1)
+        def _():
+            previous = buffers(step)[1]
+            ends = product[TILES + CELLS_Z - 1, corners, :]
+            for way, a, valid in ((0, bottom, has_below), (1, top, has_above)):
+                finish_copy(edge_message(step + 1, way), way)
+                for z in range(CELLS_Z):
+                    rows = group(a, 1)
+                    edge = jnp.where(along_y & valid, edge_receives[step + 1, way, z], 0.0)
+                    previous[TILES - CELLS_Z + z, rows, :] = previous[TILES - CELLS_Z + z, rows, :] + factor(step) * edge
+                ends = ends + jnp.where((sub == a) & valid, unpack_corner(step + 1, way), 0.0)
+            advance(step, last_tile, corners, ends)
 
     node_count = waves_ref.shape[1]
     whole_blocks = node_count // LANES
@@ -424,23 +451,24 @@
     out_ref[...] = jnp.zeros_like(out_ref)
     low_row = lax.broadcasted_iota(jnp.int32, (1, LANES), 1) < HALF
 
-    def gather(t, nodes):
+    def gather(t, nodes, halves):
         for node, row in nodes:
             first = doubled[pl.ds(index_ref[node, 2 * t], 1), :]
             second = doubled[pl.ds(index_ref[node, 2 * t + 1], 1), :]
             out_ref[t, row : row + 1, :] = jnp.where(low_row, first, second)
 
     each_node_once((top,), gather)
-    over_chunks(
-        lambda c: pack(0, c, [[out_ref[c * CELLS_Z + z, group(top, g), :] for g in range(3)] for z in range(CELLS_Z)])
-    )
-    sends[0, PACKED - 1] = out_ref[last_tile, corners, :]
-    owner = copy(0, 0)
-    owner.start()
+
+    def send_owner(c):
+        tiles = [[out_ref[c * CELLS_Z + z, group(top, g), :] for g in range(3)] for z in range(CELLS_Z)]
+        send_chunk(0, 0, c, tiles, out_ref[last_tile, corners, :])
+
+    over_chunks(send_owner)
     each_node_once((0, 1, 2, 3), gather)
-    owner.wait()
+    other[...] = jnp.zeros_like(other)
 
     def take_owner(c):
+        finish_copy(message(0, 0, c), 0)
         for z in range(CELLS_Z):
             t = c * CELLS_Z + z
             arrived = unpack(0, 0, c, z)
@@ -448,27 +476,53 @@
                 out_ref[t, group(bottom, g), :] = jnp.where(has_below, arrived[g], out_ref[t, group(bottom, g), :])
 
     over_chunks(take_owner)
+    finish_copy(edge_message(0, 0), 0)
+    for z in range(CELLS_Z):
+        t = TILES - CELLS_Z + z
+        out_ref[t, group(bottom, 1), :] = jnp.where(
+            along_y & has_below, edge_receives[0, 0, z], out_ref[t, group(bottom, 1), :]
+        )
     out_ref[last_tile, corners, :] = jnp.where(
         (sub == bottom) & has_below, unpack_corner(0, 0), out_ref[last_tile, corners, :]
     )
-    fill(out_ref, range(5))
-
-    for step in range(FILTER_DEG):
-        current, previous = (out_ref, other) if step % 2 == 0 else (other, out_ref)
-        if step == 0:
-            other[...] = jnp.zeros_like(other)
-        multiply(current)
-        copies = [copy(step + 1, 0), copy(step + 1, 1)]
-        for way, a in ((0, top), (1, bottom)):
-            send_face(way, a)
-            copies[way].start()
-        advance_inner(step, current, previous)
-        copies[0].wait()
-        advance_face(step, current, previous, 0, bottom, has_below)
-        copies[1].wait()
-        advance_face(step, current, previous, 1, top, has_above)
-        advance_corner(step, current, previous)
-        fill(previous, range(5))
+    over_chunks(lambda c: fill(out_ref, c))
+
+    multiply(out_ref, CHUNKS - 1)
+
+    def first_step(c):
+        multiply(out_ref, c)
+        assemble(0, c)
+
+    lax.fori_loop(0, CHUNKS - 1, lambda c, carry: (first_step(c), carry)[1], 0)
+    assemble(0, CHUNKS - 1)
+
+    for step in range(1, FILTER_DEG):
+        base = step - 1
+        current = buffers(step)[0]
+
+        def refresh(c):
+            fill(current, c)
+            multiply(current, c)
+
+        def next_chunk(i, carry):
+            advance_faces(step - 1, lax.rem(base + i, CHUNKS))
+            c = lax.rem(base + i - 1, CHUNKS)
+            refresh(c)
+            assemble(step, c)
+            return carry
+
+        advance_faces(step - 1, base)
+        advance_faces(step - 1, base + 1)
+        refresh(base)
+        lax.fori_loop(2, CHUNKS, next_chunk, 0)
+        refresh((base + CHUNKS - 1) % CHUNKS)
+        assemble(step, (base + CHUNKS - 1) % CHUNKS)
+        assemble(step, base)
+
+    last = FILTER_DEG - 1
+    lax.fori_loop(
+        0, CHUNKS, lambda i, carry: (advance_faces(last, lax.rem(last + i, CHUNKS)), carry)[1], 0
+    )
 
 
 def filter_cells(index, wavefunctions, stiff, scale, potential):
@@ -486,8 +540,12 @@
             pltpu.VMEM(cells, jnp.float32),
             pltpu.VMEM((2, TILES, PLANE, LANES), jnp.float32),
             pltpu.VMEM((blocks * LANES, LANES), jnp.float32),
-            pltpu.VMEM((2, PACKED, 8, LANES), jnp.float32),
-            pltpu.VMEM((rounds, 2, PACKED, 8, LANES), jnp.float32),
+            pltpu.VMEM((2, CHUNKS, MESSAGE, 8, LANES), jnp.float32),
+            pltpu.VMEM((2, EDGE, 8, LANES), jnp.float32),
+            pltpu.VMEM((rounds, 2, CHUNKS, MESSAGE, 8, LANES), jnp.float32),
+            pltpu.VMEM((rounds, 2, EDGE, 8, LANES), jnp.float32),
+            pltpu.SemaphoreType.DMA((rounds, 2, CHUNKS)),
+            pltpu.SemaphoreType.DMA((rounds, 2, CHUNKS)),
             pltpu.SemaphoreType.DMA((rounds, 2)),
             pltpu.SemaphoreType.DMA((rounds, 2)),
         ],

time: 237 us -> 216 us (0.911)
  Pallas kernels: 228 us -> 208 us
    pallas_call x1, Pallas kernels: 110 us -> 88.3 us  [filter_cells(): pl.pallas_call(filter_kernel, out_shape=jax.ShapeDtypeStruct(cells, jnp.f...]
where the time goes in v4:
time: 216 us
  Pallas kernels  208 us (96%)
  local copies, waits for them, and re-layouts  6.75 us (3%)
    pallas_call x1, Pallas kernels, finish(): pl.pallas_call(functools.partial(finish_kernel, owned_count), out_shape=j...  95.5 us
    pallas_call x1, Pallas kernels, filter_cells(): pl.pallas_call(filter_kernel, out_shape=jax.ShapeDtypeStruct(cells, jnp.f...  88.3 us
    pallas_call x1, Pallas kernels, scatter_nodes(): pl.pallas_call(scatter_kernel, out_shape=(packed, packed), in_specs=[pl.B...  21.3 us
    unnamed x8, local copies, waits for them, and re-layouts  6.75 us

profile of v4, /device:TPU:1, one launch (start us, length us, event | category | flops | bytes accessed | tf_op | source)
XLA Modules:
  0.0 216.1 jit_solution(4815286598956111557)
XLA Ops:
  0.0 1.3 pad_maximum_fusion.coef_ref
  1.3 1.6 copy.8.conn_ref
  2.8 3.0 %layout.1 = (s32[125,120]{1,0:T(8,128)}, f32[60,128]{1,0:T(8,128)}, f32[60,128]{1,0:T(8,128)}, bf16[256,256]{1,0:T(8,128)(2,1)}) custom-call(s32[125,120]{1,0:T(8,128)} %copy.8.conn_ref, f32[2,120]{1,0:T(2,128)} %pad_maximum_fusion.coef_ref, f32[125,125]{1,0:T(8,128)} %stiff_ref.1, f32[128,125]{1,0:T(8,128)} %constant.4.clone.select_ref), custom_call_target="tpu_custom_call" | custom-call | tf_op jit(solution)/shard_map/layout/pallas_call | solution.py:145
  5.8 0.0 copy-start.2
  5.8 88.3 %filter_cells.1.cells_ref = f32[66,128,128]{2,1,0:T(8,128)} custom-call(s32[125,120]{1,0:T(8,128)} %get-tuple-element.11.index_ref, f32[64,10125]{1,0:T(8,128)} %waves_ref.1, bf16[256,256]{1,0:T(8,128)(2,1)} %get-tuple-element.12.stiff_ref, f32[128,128]{1,0:T(8,128)} %constant.5.clone.mass_ref, f32[60,128]{1,0:T(8,128)} %get-tuple-element.13.scale_ref, ...), custom_call_target="tpu_custom_call" | custom-call | tf_op jit(solution)/shard_map/filter_cells/pallas_call | solution.py:533
  94.1 0.0 copy-done.2
  94.1 0.0 copy-start
  94.2 2.2 %copy-done = f32[66,128,128]{2,1,0:T(8,128)S(1)} copy-done((f32[66,128,128]{2,1,0:T(8,128)S(1)}, f32[66,128,128]{2,1,0:T(8,128)}, u32[]{:S(2)}) %copy-start) | copy-done | bytes 4325400
  96.4 21.3 %scatter_nodes.1 = (f32[5120,128]{1,0:T(8,128)S(1)}, f32[5120,128]{1,0:T(8,128)S(1)}) custom-call(s32[125,120]{1,0:T(8,128)S(1)} %copy-done.2, f32[66,128,128]{2,1,0:T(8,128)S(1)} %copy-done), custom_call_target="tpu_custom_call" | custom-call | tf_op jit(solution)/shard_map/scatter_nodes/pallas_call | solution.py:206
  117.7 0.0 copy-start.1
  117.7 1.5 copy-done.1
  119.2 95.5 %finish.1 = f32[64,10240]{1,0:T(8,128)S(1)} custom-call(f32[5120,128]{1,0:T(8,128)S(1)} %get-tuple-element.15.own, f32[5120,128]{1,0:T(8,128)} %copy-done.1), custom_call_target="tpu_custom_call" | custom-call | tf_op jit(solution)/shard_map/finish/pallas_call | solution.py:812
  214.6 1.5 copy.10
Async XLA Ops:
  5.8 88.3 %copy-start.2 = (s32[125,120]{1,0:T(8,128)S(1)}, s32[125,120]{1,0:T(8,128)}, u32[]{:S(2)}) copy-start(s32[125,120]{1,0:T(8,128)} %get-tuple-element.11.index_ref) | copy-start | bytes 180004
  94.1 2.2 %copy-start = (f32[66,128,128]{2,1,0:T(8,128)S(1)}, f32[66,128,128]{2,1,0:T(8,128)}, u32[]{:S(2)}) copy-start(f32[66,128,128]{2,1,0:T(8,128)} %filter_cells.1.cells_ref) | copy-start | bytes 12976132
  117.7 1.5 copy-start.1

commit v5 on v4

--- a/solution.py
+++ b/solution.py
@@ -31,6 +31,9 @@
 NODES = 10125
 PAIRS = 5120
 BLOCK = 256
+PIECES = 5
+GROUPS = 2 * PAIRS // LANES
+PLANE_PEERS = 16
 BANDS_DEV = 64
 N_BAND = 4
 
@@ -59,6 +62,23 @@
 LOCAL_ROWS = [row for _, row in node_rows(range(5), lambda b, c: True)]
 
 
+def owners():
+    owned = np.zeros((LANES, SLOTS), np.float32)
+    for slot in range(SLOTS):
+        tile, half = divmod(slot, 2)
+        last_y = half == 1 and tile >= TILES - CELLS_Z
+        last_z = tile % CELLS_Z == CELLS_Z - 1
+        for node, _ in node_rows(range(5), lambda b, c: (b < 4 or last_y) and (c < 4 or last_z)):
+            owned[node, slot] = 1.0
+    return owned
+
+
+def place_codes():
+    codes = np.zeros((LANES, LANES), np.float32)
+    codes[:125, :] = 2.0 * np.array(LOCAL_ROWS)[:, None] + np.arange(LANES)[None, :] % 2
+    return codes
+
+
 def row_selector():
     chosen = np.zeros((ROWS, 125), np.float32)
     chosen[LOCAL_ROWS, np.arange(125)] = 1.0
@@ -93,7 +113,10 @@
     return jnp.sum(total, axis=0, keepdims=True) - 1.0
 
 
-def layout_kernel(conn_ref, coef_ref, stiff_ref, select_ref, index_ref, scale_ref, potential_ref, stiffness_ref):
+def layout_kernel(
+    conn_ref, cell_scale_ref, cell_potential_ref, stiff_ref, select_ref, owned_ref,
+    index_ref, keys_ref, scale_ref, potential_ref, stiffness_ref,
+):
     conn = conn_ref[...].astype(jnp.float32)
     cells = conn.shape[1]
     on_rows = lax.broadcasted_iota(jnp.int32, (cells, cells), 0)
@@ -113,7 +136,11 @@
     tile = (at_y - jnp.where(upper_half, 1.0 * CHUNKS, 0.0)) * CELLS_Z + at_z
     slot = 2.0 * tile + jnp.where(upper_half, 1.0, 0.0)
     moved = (as_column(slot) == on_lanes.astype(jnp.float32)).astype(jnp.float32)
-    index_ref[...] = (exact_dot(conn, moved) + 0.5).astype(jnp.int32)
+    index = (exact_dot(conn, moved) + 0.5).astype(jnp.int32)
+    index_ref[...] = index
+    index = jnp.concatenate([index, jnp.zeros((LANES - index.shape[0], cells), jnp.int32)], axis=0)
+    keys = jnp.where(owned_ref[...] > 0.5, index, -1)
+    keys_ref[...] = jnp.concatenate([keys, jnp.full((LANES, LANES - cells), -1, jnp.int32)], axis=1)
 
     wanted = lax.broadcasted_iota(jnp.int32, (TILES, cells), 0).astype(jnp.float32)
     lane = lax.broadcasted_iota(jnp.int32, (TILES, LANES), 1)
@@ -124,8 +151,8 @@
         ]
         return jnp.where(lane < HALF, low, high)
 
-    scale_ref[...] = spread(coef_ref[0:1, :])
-    potential_ref[...] = spread(coef_ref[1:2, :])
+    scale_ref[...] = spread(cell_scale_ref[...])
+    potential_ref[...] = spread(cell_potential_ref[...])
 
     select = select_ref[...]
     part = exact_dot(select, stiff_ref[...])
@@ -139,21 +166,22 @@
     )
 
 
-def make_layout(connectivity, coefficients, stiffness):
+def make_layout(connectivity, cell_scale, cell_potential, stiffness):
     cells = connectivity.shape[1]
     whole = pl.BlockSpec(memory_space=pltpu.VMEM)
     return pl.pallas_call(
         layout_kernel,
         out_shape=(
             jax.ShapeDtypeStruct((125, cells), jnp.int32),
+            jax.ShapeDtypeStruct((LANES, LANES), jnp.int32),
             jax.ShapeDtypeStruct((TILES, LANES), jnp.float32),
             jax.ShapeDtypeStruct((TILES, LANES), jnp.float32),
             jax.ShapeDtypeStruct((2 * ROWS, 2 * ROWS), jnp.bfloat16),
         ),
-        in_specs=[whole] * 4,
-        out_specs=(whole,) * 4,
+        in_specs=[whole] * 6,
+        out_specs=(whole,) * 5,
         name="layout",
-    )(connectivity, coefficients, stiffness, row_selector())
+    )(connectivity, cell_scale[None, :], cell_potential[None, :], stiffness, row_selector(), owners())
 
 
 def each_node_once(planes, visit):
@@ -170,57 +198,10 @@
     loop(CHUNKS, lambda i: i * CELLS_Z + CELLS_Z - 1, node_rows(planes, lambda b, c: b < 4 and c == 4))
 
 
-def scatter_kernel(index_ref, cells_ref, packed_ref, weight_ref, nodes_ref, rows_ref):
-    lane = lax.broadcasted_iota(jnp.int32, (ROWS, LANES), 1)
-    row_at = lax.broadcasted_iota(jnp.int32, (ROWS, LANES), 0)
-    inner = lax.axis_index("space") > 0
-    weight = jnp.where(((row_at < PLANE) | (row_at == CORNERS)) & inner, 0.0, 1.0)
-    nodes_ref[NODES - NODES % 8 :, :] = jnp.zeros((2 * PAIRS - NODES + NODES % 8, LANES), jnp.float32)
-
-    def visit(t, nodes, halves):
-        values = cells_ref[t]
-        turned = pltpu.roll(values, HALF, 1)
-        rows_ref[0] = jnp.where(lane < HALF, values, weight)
-        rows_ref[1] = jnp.where(lane < HALF, turned, weight)
-        for node, row in nodes:
-            for half in halves:
-                nodes_ref[pl.ds(index_ref[node, 2 * t + half], 1), :] = rows_ref[half, row : row + 1, :]
-
-    each_node_once(range(5), visit)
-    low_half = lax.broadcasted_iota(jnp.int32, (BLOCK, LANES), 1) < HALF
-
-    def pack(i, carry):
-        first = nodes_ref[pl.ds(pl.multiple_of(i * BLOCK, BLOCK), BLOCK), :]
-        second = nodes_ref[pl.ds(pl.multiple_of(PAIRS + i * BLOCK, BLOCK), BLOCK), :]
-        rows = pl.ds(pl.multiple_of(i * BLOCK, BLOCK), BLOCK)
-        packed_ref[rows, :] = jnp.where(low_half, first, pltpu.roll(second, HALF, 1))
-        weight_ref[rows, :] = jnp.where(low_half, pltpu.roll(first, HALF, 1), second)
-        return carry
-
-    lax.fori_loop(0, PAIRS // BLOCK, pack, 0)
-
-
-def scatter_nodes(index, cells):
-    whole = pl.BlockSpec(memory_space=pltpu.VMEM)
-    packed = jax.ShapeDtypeStruct((PAIRS, LANES), jnp.float32)
-    return pl.pallas_call(
-        scatter_kernel,
-        out_shape=(packed, packed),
-        in_specs=[pl.BlockSpec(memory_space=pltpu.SMEM), whole],
-        out_specs=(whole, whole),
-        scratch_shapes=[
-            pltpu.VMEM((2 * PAIRS, LANES), jnp.float32),
-            pltpu.VMEM((2, ROWS, LANES), jnp.float32),
-        ],
-        compiler_params=pltpu.CompilerParams(vmem_limit_bytes=40 * 2**20),
-        name="scatter_nodes",
-    )(index, cells)
-
-
 def filter_kernel(
-    index_ref, waves_ref, stiff_ref, mass_ref, scale_ref, potential_ref, out_ref,
-    other, product, face, doubled, sends, edge_sends, receives, edge_receives,
-    send_sems, receive_sems, edge_send_sems, edge_receive_sems,
+    index_vector_ref, keys_ref, codes_ref, waves_ref, stiff_ref, mass_ref, scale_ref, potential_ref, out_ref, table_ref,
+    index_ref, other, product, face, doubled, sends, edge_sends, receives, edge_receives,
+    send_sems, receive_sems, edge_send_sems, edge_receive_sems, index_sem,
 ):
     count = lax.axis_size("space")
     me = lax.axis_index("space")
@@ -432,6 +413,36 @@
                 ends = ends + jnp.where((sub == a) & valid, unpack_corner(step + 1, way), 0.0)
             advance(step, last_tile, corners, ends)
 
+    def tabulate():
+        high = lax.broadcasted_iota(jnp.int32, (GROUPS, LANES), 0)
+        low = lax.broadcasted_iota(jnp.int32, (LANES, LANES), 0)
+        tile = (lax.broadcasted_iota(jnp.int32, (1, LANES), 1) // 2).astype(jnp.float32)
+
+        def body(i, total):
+            left, right = [], []
+            for k in range(2):
+                at = pl.ds(2 * i + k, 1)
+                key = keys_ref[at, :]
+                left.append(jnp.where(high == key >> 7, 1.0, 0.0).astype(jnp.bfloat16))
+                hit = low == key & (LANES - 1)
+                values = [jnp.where(hit, tile, 0.0), jnp.where(hit, codes_ref[at, :], 0.0)]
+                right.append(jnp.concatenate(values, axis=0).astype(jnp.bfloat16))
+            return total + lax.dot_general(
+                jnp.concatenate(left, axis=1),
+                jnp.concatenate(right, axis=1),
+                (((1,), (1,)), ((), ())),
+                preferred_element_type=jnp.float32,
+            )
+
+        total = lax.fori_loop(0, LANES // 2, body, jnp.zeros((GROUPS, 2 * LANES), jnp.float32)) + 0.5
+        tiles = total[:, :LANES].astype(jnp.int32)
+        codes = total[:, LANES:].astype(jnp.int32)
+        node = high * LANES + lax.broadcasted_iota(jnp.int32, (GROUPS, LANES), 1)
+        place = (codes & 1) * (TILES * ROWS) + tiles * ROWS + (codes >> 1)
+        table_ref[...] = jnp.where(node < NODES, place, CORNERS + 5)
+
+    index_copy = pltpu.make_async_copy(index_vector_ref, index_ref, index_sem)
+    index_copy.start()
     node_count = waves_ref.shape[1]
     whole_blocks = node_count // LANES
 
@@ -457,6 +468,7 @@
             second = doubled[pl.ds(index_ref[node, 2 * t + 1], 1), :]
             out_ref[t, row : row + 1, :] = jnp.where(low_row, first, second)
 
+    index_copy.wait()
     each_node_once((top,), gather)
 
     def send_owner(c):
@@ -495,6 +507,7 @@
 
     lax.fori_loop(0, CHUNKS - 1, lambda c, carry: (first_step(c), carry)[1], 0)
     assemble(0, CHUNKS - 1)
+    tabulate()
 
     for step in range(1, FILTER_DEG):
         base = step - 1
@@ -525,17 +538,20 @@
     )
 
 
-def filter_cells(index, wavefunctions, stiff, scale, potential):
+def filter_cells(index, keys, wavefunctions, stiff, scale, potential):
     whole = pl.BlockSpec(memory_space=pltpu.VMEM)
     cells = (TILES + CELLS_Z, ROWS, LANES)
     rounds = FILTER_DEG + 1
     blocks = wavefunctions.shape[1] // LANES + 1
     return pl.pallas_call(
         filter_kernel,
-        out_shape=jax.ShapeDtypeStruct(cells, jnp.float32),
-        in_specs=[pl.BlockSpec(memory_space=pltpu.SMEM)] + [whole] * 5,
-        out_specs=whole,
+        out_shape=(
+            jax.ShapeDtypeStruct(cells, jnp.float32), jax.ShapeDtypeStruct((GROUPS, LANES), jnp.int32)
+        ),
+        in_specs=[whole] * 8,
+        out_specs=(whole, whole),
         scratch_shapes=[
+            pltpu.SMEM(index.shape, jnp.int32),
             pltpu.VMEM(cells, jnp.float32),
             pltpu.VMEM(cells, jnp.float32),
             pltpu.VMEM((2, TILES, PLANE, LANES), jnp.float32),
@@ -548,12 +564,13 @@
             pltpu.SemaphoreType.DMA((rounds, 2, CHUNKS)),
             pltpu.SemaphoreType.DMA((rounds, 2)),
             pltpu.SemaphoreType.DMA((rounds, 2)),
+            pltpu.SemaphoreType.DMA(()),
         ],
         compiler_params=pltpu.CompilerParams(
             collective_id=0, has_side_effects=True, vmem_limit_bytes=56 * 2**20
         ),
         name="filter_cells",
-    )(index, wavefunctions, stiff, row_mass(), scale, potential)
+    )(index, keys, place_codes(), wavefunctions, stiff, row_mass(), scale, potential)
 
 
 def split(x):
@@ -598,32 +615,29 @@
 
 
 def finish_kernel(
-    owned, own, weight, out, partner, cross, partner_cross, sums, by_x, by_y, line, piece, by_z, reduced, everyone,
-    inverse, pair_sems, cross_sems, forward_sems, x_sems, y_sems, z_sems, y_back_sems, x_back_sems, band_sems,
+    owned, cells, table_vector, out, table, low_rows, high_rows, own, weight, partner, cross, partner_cross,
+    sums, by_plane, piece, by_z, everyone, inverse,
+    table_sem, pair_sems, first_sems, second_sems, forward_sems, again_sems, plane_sems, z_sems, band_sems, back_sems,
 ):
+    table_copy = pltpu.make_async_copy(table_vector, table, table_sem)
+    table_copy.start()
     space, band = lax.axis_index("space"), lax.axis_index("band")
-    at_x = lax.rem(space, 4)
-    at_y = lax.rem(space // 4, 4)
+    at_plane = lax.rem(space, PLANE_PEERS)
     core = lax.rem(band, 2)
     chip = band // 2
     mate = band + 1 - 2 * core
     across = lax.rem(band + 2, N_BAND)
     across_mate = lax.rem(mate + 2, N_BAND)
 
-    def x_peer(k):
-        return {"space": space - at_x + lax.rem(at_x + k, 4)}
-
-    def y_peer(k):
-        return {"space": space - 4 * at_y + 4 * lax.rem(at_y + k, 4)}
-
-    z_peer = {"space": lax.rem(space + 16, 32)}
-
-    peers = [x_peer(k) for k in (1, 2, 3)] + [y_peer(k) for k in (1, 2, 3)] + [z_peer]
-    peers += [{"band": lax.rem(band + k, N_BAND)} for k in (1, 2, 3)]
+    def plane_peer(k):
+        return {"space": space - at_plane + lax.rem(at_plane + k, PLANE_PEERS)}
+
+    z_peer = {"space": lax.rem(space + PLANE_PEERS, 2 * PLANE_PEERS)}
+    band_peers = [{"band": lax.rem(band + k, N_BAND)} for k in (1, 2, 3)]
     barrier = pltpu.get_barrier_semaphore()
+    peers = [plane_peer(k) for k in range(1, PLANE_PEERS)] + [z_peer] + band_peers
     for peer in peers:
         pl.semaphore_signal(barrier, inc=1, device_id=peer, device_id_type=MESH)
-    pl.semaphore_wait(barrier, len(peers))
 
     def send(source, target, sems, slot, peer):
         return pltpu.make_async_remote_copy(
@@ -635,16 +649,65 @@
             device_id_type=MESH,
         )
 
+    row_at = lax.broadcasted_iota(jnp.int32, (ROWS, LANES), 0)
+    left_half = lax.broadcasted_iota(jnp.int32, (ROWS, LANES), 1) < HALF
+    shared = ((row_at < PLANE) | (row_at == CORNERS)) & (space > 0)
+    row_weight = jnp.where(shared | (row_at >= CORNERS + 5), 0.0, 1.0)
+
+    def spread(t, carry):
+        values = cells[t]
+        turned = pltpu.roll(values, HALF, 1)
+        for half, (left, right) in enumerate(((values, turned), (turned, values))):
+            rows = pl.ds(pl.multiple_of((half * TILES + t) * ROWS, ROWS), ROWS)
+            low_rows[rows, :] = jnp.where(left_half, left, row_weight)
+            high_rows[rows, :] = jnp.where(left_half, row_weight, right)
+        return carry
+
+    lax.fori_loop(0, TILES, spread, 0)
+    table_copy.wait()
+    low_lane = lax.broadcasted_iota(jnp.int32, (1, LANES), 1) < HALF
+
+    def gather(i):
+        start = pl.multiple_of(i * LANES, LANES)
+        for k in range(LANES):
+            first = low_rows[pl.ds(table[i, k], 1), :]
+            second = high_rows[pl.ds(table[i + GROUPS // 2, k], 1), :]
+            own[pl.ds(start + k, 1), :] = jnp.where(low_lane, first, second)
+            weight[pl.ds(start + k, 1), :] = jnp.where(low_lane, second, first)
+
     half = PAIRS // 2
-    mine_first = pl.ds(pl.multiple_of(chip * half, half), half)
-    mine_second = pl.ds(pl.multiple_of((1 - chip) * half, half), half)
+    size = half // PIECES
+
+    def piece_rows(side, p):
+        return pl.ds(pl.multiple_of(side * half + p * size, size), size)
+
     to_mate, to_across = {"band": mate}, {"band": across}
+    pieces = range(PIECES)
+    first = [
+        send(own.at[piece_rows(chip, p)], cross.at[piece_rows(chip, p)], first_sems, p, to_across) for p in pieces
+    ]
+    second = [
+        send(own.at[piece_rows(1 - chip, p)], cross.at[piece_rows(1 - chip, p)], second_sems, p, to_across)
+        for p in pieces
+    ]
+    forward_first = [
+        send(cross.at[piece_rows(1 - chip, p)], partner_cross.at[piece_rows(1 - chip, p)], forward_sems, p, to_mate)
+        for p in pieces
+    ]
+    forward_second = [
+        send(cross.at[piece_rows(chip, p)], partner_cross.at[piece_rows(chip, p)], again_sems, p, to_mate)
+        for p in pieces
+    ]
     pair = send(own, partner, pair_sems, 0, to_mate)
-    first = send(own.at[mine_first], cross.at[mine_first], cross_sems, 0, to_across)
-    second = send(own.at[mine_second], cross.at[mine_second], cross_sems, 1, to_across)
-    forward_first = send(cross.at[mine_second], partner_cross.at[mine_second], forward_sems, 0, to_mate)
-    forward_second = send(cross.at[mine_first], partner_cross.at[mine_first], forward_sems, 1, to_mate)
-    first.start()
+
+    groups = GROUPS // 4
+    per_piece = groups // PIECES
+    pl.semaphore_wait(barrier, len(peers))
+    for p in pieces:
+        base = chip * groups + p * per_piece
+        lax.fori_loop(0, per_piece, lambda i, carry, base=base: (gather(base + i), carry)[1], 0)
+        first[p].start()
+    lax.fori_loop(0, groups, lambda i, carry: (gather((1 - chip) * groups + i), carry)[1], 0)
     pair.start()
     pair.wait()
 
@@ -664,11 +727,12 @@
     def own_terms(i, total):
         rows = block_rows(i)
         mine = own[rows, :]
-        return total + products(mine * weight[rows, :], jnp.concatenate([mine, partner[rows, :]], axis=1))
+        scale = pltpu.roll(weight[rows, :], HALF, 1)
+        return total + products(mine * scale, jnp.concatenate([mine, partner[rows, :]], axis=1))
 
     def cross_terms(i, total):
-        rows = block_rows(i + (1 - chip) * (half // BLOCK))
-        scale = weight[rows, :]
+        rows = block_rows(i)
+        scale = pltpu.roll(weight[rows, :], HALF, 1)
         return total + products(
             cross[rows, :], jnp.concatenate([own[rows, :] * scale, partner[rows, :] * scale], axis=1)
         )
@@ -683,58 +747,60 @@
 
     zero = jnp.zeros((LANES, 2 * LANES), jnp.float32)
     sums[0:BANDS_DEV, :] = fold(lax.fori_loop(0, PAIRS // BLOCK, own_terms, zero))
-    first.wait()
-    second.start()
-    forward_first.start()
-    sums[BANDS_DEV : 2 * BANDS_DEV, :] = fold(lax.fori_loop(0, half // BLOCK, cross_terms, zero))
-
-    def rows_of(at, size):
-        return pl.ds(pl.multiple_of(at, size), size)
-
-    to_x = [
-        send(sums.at[rows_of(32 * lax.rem(at_x + k, 4), 32)], by_x.at[k - 1], x_sems, k - 1, x_peer(k)) for k in (1, 2, 3)
+    blocks = size // BLOCK
+    total = zero
+    for p in pieces:
+        first[p].wait()
+        forward_first[p].start()
+        base = (1 - chip) * (half // BLOCK) + p * blocks
+        total = lax.fori_loop(0, blocks, lambda i, total, base=base: cross_terms(base + i, total), total)
+    sums[BANDS_DEV : 2 * BANDS_DEV, :] = fold(total)
+
+    second[0].start()
+
+    def rows_of(at):
+        return pl.ds(pl.multiple_of(8 * at, 8), 8)
+
+    others = range(1, PLANE_PEERS)
+    scatter = [
+        send(sums.at[rows_of(lax.rem(at_plane + k, PLANE_PEERS))], by_plane.at[k - 1], plane_sems, k - 1, plane_peer(k))
+        for k in others
     ]
-    for step in to_x:
+    for step in scatter:
         step.start()
-    for step in to_x:
+    for step in scatter:
         step.wait()
-    line[...] = sums[rows_of(32 * at_x, 32), :] + by_x[0] + by_x[1] + by_x[2]
-    to_y = [
-        send(line.at[rows_of(8 * lax.rem(at_y + k, 4), 8)], by_y.at[k - 1], y_sems, k - 1, y_peer(k)) for k in (1, 2, 3)
-    ]
-    for step in to_y:
-        step.start()
-    for step in to_y:
-        step.wait()
-    piece[...] = line[rows_of(8 * at_y, 8), :] + by_y[0] + by_y[1] + by_y[2]
+    mine = sums[rows_of(at_plane), :]
+    for k in others:
+        mine = mine + by_plane[k - 1]
+    piece[...] = mine
     to_z = send(piece, by_z, z_sems, 0, z_peer)
     to_z.start()
     to_z.wait()
-    small = rows_of(32 * at_x + 8 * at_y, 8)
-    reduced[small, :] = piece[...] + by_z[...]
-    back_y = [send(reduced.at[small], reduced.at[small], y_back_sems, k - 1, y_peer(k)) for k in (1, 2, 3)]
-    for step in back_y:
-        step.start()
-    for step in back_y:
-        step.wait()
-    large = rows_of(32 * at_x, 32)
-    back_x = [send(reduced.at[large], reduced.at[large], x_back_sems, k - 1, x_peer(k)) for k in (1, 2, 3)]
-    for step in back_x:
-        step.start()
-    for step in back_x:
-        step.wait()
+    everyone[at_plane, band] = piece[...] + by_z[...]
     to_band = [
-        send(reduced, everyone.at[band], band_sems, k - 1, {"band": lax.rem(band + k, N_BAND)}) for k in (1, 2, 3)
+        send(everyone.at[at_plane, band], everyone.at[at_plane, band], band_sems, k, peer)
+        for k, peer in enumerate(band_peers)
     ]
     for step in to_band:
         step.start()
-    everyone[band] = reduced[...]
     for step in to_band:
         step.wait()
+    for p in pieces[1:]:
+        second[p].start()
+    back = [send(everyone.at[at_plane], everyone.at[at_plane], back_sems, k - 1, plane_peer(k)) for k in others]
+    for step in back:
+        step.start()
+    for step in back:
+        step.wait()
+
+    totals = [
+        jnp.concatenate([everyone[q, b] for q in range(PLANE_PEERS)], axis=0) * (1.0 / owned) for b in range(N_BAND)
+    ]
 
     def part(b, r, c):
         size = BANDS_DEV
-        return everyone[b, r * size : (r + 1) * size, c * size : (c + 1) * size] * (1.0 / owned)
+        return totals[b][r * size : (r + 1) * size, c * size : (c + 1) * size]
 
     margin = {(b, b): part(b, 0, 0) for b in range(N_BAND)}
     margin[1, 0], margin[3, 2] = part(1, 0, 1), part(3, 0, 1)
@@ -759,8 +825,8 @@
                 total = total + exact_dot(factor[k, m], whole[m, j])
             whole[k, j] = -exact_dot(diagonal, total)
         if k == 2:
-            second.wait()
-            forward_second.start()
+            second[0].wait()
+            forward_second[0].start()
     padding = jnp.zeros((BANDS_DEV, LANES - BANDS_DEV), jnp.float32)
     for i in range(N_BAND):
         for j in range(N_BAND):
@@ -768,8 +834,11 @@
                 inverse[i, j] = jnp.concatenate([whole[i, j], padding], axis=1)
             else:
                 inverse[i, j] = jnp.zeros((BANDS_DEV, LANES), jnp.float32)
-    forward_first.wait()
-    forward_second.wait()
+    for p in pieces[1:]:
+        second[p].wait()
+        forward_second[p].start()
+    for p in pieces:
+        forward_first[p].wait()
 
     panels = [inverse[band, source] for source in (band, mate, across, across_mate)]
     left = jnp.concatenate(
@@ -796,10 +865,15 @@
         out[:, pl.ds(pl.multiple_of(PAIRS + i * BLOCK, BLOCK), BLOCK)] = rotated[BANDS_DEV:]
         return carry
 
-    lax.fori_loop(0, PAIRS // BLOCK, rotate, 0)
-
-
-def finish(packed, weight, owned_count):
+    done = (1 - chip) * (half // BLOCK)
+    lax.fori_loop(0, half // BLOCK, lambda i, carry: rotate(done + i, carry), 0)
+    for p in pieces:
+        forward_second[p].wait()
+        base = chip * (half // BLOCK) + p * blocks
+        lax.fori_loop(0, blocks, lambda i, carry, base=base: rotate(base + i, carry), 0)
+
+
+def finish(cells, table, owned_count):
     whole = pl.BlockSpec(memory_space=pltpu.VMEM)
     nodes = pltpu.VMEM((PAIRS, LANES), jnp.float32)
 
@@ -815,17 +889,21 @@
         in_specs=[whole, whole],
         out_specs=whole,
         scratch_shapes=[
-            nodes, nodes, nodes,
-            small(LANES, LANES), small(3, 32, LANES), small(3, 8, LANES), small(32, LANES), small(8, LANES),
-            small(8, LANES), small(LANES, LANES), small(N_BAND, LANES, LANES),
+            pltpu.SMEM(table.shape, jnp.int32),
+            small(2 * TILES * ROWS, LANES), small(2 * TILES * ROWS, LANES),
+            nodes, nodes, nodes, nodes, nodes,
+            small(LANES, LANES), small(PLANE_PEERS - 1, 8, LANES), small(8, LANES), small(8, LANES),
+            small(PLANE_PEERS, N_BAND, 8, LANES),
             small(N_BAND, N_BAND, BANDS_DEV, LANES),
-            sems(1), sems(2), sems(2), sems(3), sems(3), sems(1), sems(3), sems(3), sems(3),
+            pltpu.SemaphoreType.DMA(()),
+            sems(1), sems(PIECES), sems(PIECES), sems(PIECES), sems(PIECES),
+            sems(PLANE_PEERS - 1), sems(1), sems(3), sems(PLANE_PEERS - 1),
         ],
         compiler_params=pltpu.CompilerParams(
-            collective_id=1, has_side_effects=True, vmem_limit_bytes=48 * 2**20
+            collective_id=1, has_side_effects=True, vmem_limit_bytes=56 * 2**20
         ),
         name="finish",
-    )(packed, weight)
+    )(cells, table)
 
 
 def shards(
@@ -836,11 +914,9 @@
     space_count = lax.axis_size("space")
     owned_count = node_count * space_count - face_count * (space_count - 1)
 
-    coefficients = jnp.stack([cell_scale, cell_potential])
-    index, scale, potential, stiff = make_layout(connectivity, coefficients, stiffness)
-    cells = filter_cells(index, wavefunctions, stiff, scale, potential)
-    packed, weight = scatter_nodes(index, cells)
-    return finish(packed, weight, owned_count)[:, :node_count]
+    index, keys, scale, potential, stiff = make_layout(connectivity, cell_scale, cell_potential, stiffness)
+    cells, table = filter_cells(index, keys, wavefunctions, stiff, scale, potential)
+    return finish(cells, table, owned_count)[:, :node_count]
 
 
 def solution(mesh):

time: 216 us -> 186 us (0.86)
  Pallas kernels: 208 us -> 181 us
    pallas_call x2 -> x1, Pallas kernels: 110 us -> 92.4 us  [filter_cells(): pl.pallas_call(filter_kernel, out_shape=(jax.ShapeDtypeStruct(cells, jnp....]
    pallas_call x1, Pallas kernels: 95.5 us -> 85.1 us  [finish(): pl.pallas_call(functools.partial(finish_kernel, owned_count), out_shape=j...]
    unnamed x8 -> x2, local copies, waits for them, and re-layouts: 6.75 us -> 4.97 us
where the time goes in v5:
time: 186 us
  Pallas kernels  181 us (97%)
  local copies, waits for them, and re-layouts  4.97 us (3%)
    pallas_call x1, Pallas kernels, filter_cells(): pl.pallas_call(filter_kernel, out_shape=(jax.ShapeDtypeStruct(cells, jnp....  92.4 us
    pallas_call x1, Pallas kernels, finish(): pl.pallas_call(functools.partial(finish_kernel, owned_count), out_shape=j...  85.1 us
    unnamed x2, local copies, waits for them, and re-layouts  4.97 us

profile of v5, /device:TPU:1, one launch (start us, length us, event | category | flops | bytes accessed | tf_op | source)
XLA Modules:
  0.0 185.6 jit_solution(6400161903002830087)
XLA Ops:
  0.0 1.5 copy.10.conn_ref
  1.5 3.1 %layout.1 = (s32[125,120]{1,0:T(8,128)}, s32[128,128]{1,0:T(8,128)}, f32[60,128]{1,0:T(8,128)}, f32[60,128]{1,0:T(8,128)}, bf16[256,256]{1,0:T(8,128)(2,1)}) custom-call(s32[125,120]{1,0:T(8,128)} %copy.10.conn_ref, f32[1,120]{1,0:T(1,128)} %bitcast.4, f32[1,120]{1,0:T(1,128)} %bitcast.5, f32[125,125]{1,0:T(8,128)} %stiff_ref.1, ...), custom_call_target="tpu_custom_call" | custom-call | tf_op jit(solution)/shard_map/layout/pallas_call | solution.py:172
  4.6 92.4 %filter_cells.1 = (f32[66,128,128]{2,1,0:T(8,128)}, s32[80,128]{1,0:T(8,128)}) custom-call(s32[125,120]{1,0:T(8,128)} %get-tuple-element.12.index_vector_ref, s32[128,128]{1,0:T(8,128)} %get-tuple-element.13.keys_ref, f32[128,128]{1,0:T(8,128)} %constant.10.clone.codes_ref, f32[64,10125]{1,0:T(8,128)} %waves_ref.1, ...), custom_call_target="tpu_custom_call" | custom-call | tf_op jit(solution)/shard_map/filter_cells/pallas_call | solution.py:546
  97.1 85.1 %finish.1 = f32[64,10240]{1,0:T(8,128)} custom-call(f32[66,128,128]{2,1,0:T(8,128)} %get-tuple-element.17.cells, s32[80,128]{1,0:T(8,128)} %get-tuple-element.18.table_vector), custom_call_target="tpu_custom_call" | custom-call | tf_op jit(solution)/shard_map/finish/pallas_call | solution.py:886
  182.2 3.4 %copy.12 = f32[64,10125]{1,0:T(8,128)} copy(f32[64,10125]{1,0:T(8,128)} %bitcast.3) | data formatting | bytes 5184000

commit v6 on v5

--- a/solution.py
+++ b/solution.py
@@ -32,6 +32,7 @@
 PAIRS = 5120
 BLOCK = 256
 PIECES = 5
+CELL_PARTS = 4
 GROUPS = 2 * PAIRS // LANES
 PLANE_PEERS = 16
 BANDS_DEV = 64
@@ -200,7 +201,7 @@
 
 def filter_kernel(
     index_vector_ref, keys_ref, codes_ref, waves_ref, stiff_ref, mass_ref, scale_ref, potential_ref, out_ref, table_ref,
-    index_ref, other, product, face, doubled, sends, edge_sends, receives, edge_receives,
+    index_ref, places, other, product, face, doubled, sends, edge_sends, receives, edge_receives,
     send_sems, receive_sems, edge_send_sems, edge_receive_sems, index_sem,
 ):
     count = lax.axis_size("space")
@@ -413,7 +414,7 @@
                 ends = ends + jnp.where((sub == a) & valid, unpack_corner(step + 1, way), 0.0)
             advance(step, last_tile, corners, ends)
 
-    def tabulate():
+    def tabulate(step):
         high = lax.broadcasted_iota(jnp.int32, (GROUPS, LANES), 0)
         low = lax.broadcasted_iota(jnp.int32, (LANES, LANES), 0)
         tile = (lax.broadcasted_iota(jnp.int32, (1, LANES), 1) // 2).astype(jnp.float32)
@@ -434,7 +435,13 @@
                 preferred_element_type=jnp.float32,
             )
 
-        total = lax.fori_loop(0, LANES // 2, body, jnp.zeros((GROUPS, 2 * LANES), jnp.float32)) + 0.5
+        part = LANES // 2 // FILTER_DEG
+        total = jnp.zeros((GROUPS, 2 * LANES), jnp.float32) if step == 0 else places[...]
+        total = lax.fori_loop(part * step, part * (step + 1), body, total)
+        if step < FILTER_DEG - 1:
+            places[...] = total
+            return
+        total = total + 0.5
         tiles = total[:, :LANES].astype(jnp.int32)
         codes = total[:, LANES:].astype(jnp.int32)
         node = high * LANES + lax.broadcasted_iota(jnp.int32, (GROUPS, LANES), 1)
@@ -507,7 +514,7 @@
 
     lax.fori_loop(0, CHUNKS - 1, lambda c, carry: (first_step(c), carry)[1], 0)
     assemble(0, CHUNKS - 1)
-    tabulate()
+    tabulate(0)
 
     for step in range(1, FILTER_DEG):
         base = step - 1
@@ -531,6 +538,7 @@
         refresh((base + CHUNKS - 1) % CHUNKS)
         assemble(step, (base + CHUNKS - 1) % CHUNKS)
         assemble(step, base)
+        tabulate(step)
 
     last = FILTER_DEG - 1
     lax.fori_loop(
@@ -552,6 +560,7 @@
         out_specs=(whole, whole),
         scratch_shapes=[
             pltpu.SMEM(index.shape, jnp.int32),
+            pltpu.VMEM((GROUPS, 2 * LANES), jnp.float32),
             pltpu.VMEM(cells, jnp.float32),
             pltpu.VMEM(cells, jnp.float32),
             pltpu.VMEM((2, TILES, PLANE, LANES), jnp.float32),
@@ -615,12 +624,19 @@
 
 
 def finish_kernel(
-    owned, cells, table_vector, out, table, low_rows, high_rows, own, weight, partner, cross, partner_cross,
+    owned, far_cells, table_vector, out, table, cells, wide_rows, own, weight, partner, cross, partner_cross,
     sums, by_plane, piece, by_z, everyone, inverse,
-    table_sem, pair_sems, first_sems, second_sems, forward_sems, again_sems, plane_sems, z_sems, band_sems, back_sems,
+    table_sem, cell_sems, pair_sems, first_sems, second_sems, forward_sems, again_sems, plane_sems, z_sems, band_sems, back_sems,
 ):
     table_copy = pltpu.make_async_copy(table_vector, table, table_sem)
     table_copy.start()
+    part = TILES // CELL_PARTS
+    cell_copies = [
+        pltpu.make_async_copy(far_cells.at[pl.ds(p * part, part)], cells.at[pl.ds(p * part, part)], cell_sems.at[p])
+        for p in range(CELL_PARTS)
+    ]
+    for step in cell_copies:
+        step.start()
     space, band = lax.axis_index("space"), lax.axis_index("band")
     at_plane = lax.rem(space, PLANE_PEERS)
     core = lax.rem(band, 2)
@@ -649,31 +665,38 @@
             device_id_type=MESH,
         )
 
-    row_at = lax.broadcasted_iota(jnp.int32, (ROWS, LANES), 0)
     left_half = lax.broadcasted_iota(jnp.int32, (ROWS, LANES), 1) < HALF
-    shared = ((row_at < PLANE) | (row_at == CORNERS)) & (space > 0)
-    row_weight = jnp.where(shared | (row_at >= CORNERS + 5), 0.0, 1.0)
-
-    def spread(t, carry):
+
+    def widen(t, carry):
         values = cells[t]
         turned = pltpu.roll(values, HALF, 1)
-        for half, (left, right) in enumerate(((values, turned), (turned, values))):
-            rows = pl.ds(pl.multiple_of((half * TILES + t) * ROWS, ROWS), ROWS)
-            low_rows[rows, :] = jnp.where(left_half, left, row_weight)
-            high_rows[rows, :] = jnp.where(left_half, row_weight, right)
+        for slot, (left, right) in enumerate(((values, turned), (turned, values))):
+            rows = pl.ds(pl.multiple_of((slot * TILES + t) * ROWS, ROWS), ROWS)
+            wide_rows[rows, :] = jnp.where(left_half, left, right)
         return carry
 
-    lax.fori_loop(0, TILES, spread, 0)
+    for p in range(CELL_PARTS):
+        cell_copies[p].wait()
+        lax.fori_loop(p * part, (p + 1) * part, widen, 0)
     table_copy.wait()
     low_lane = lax.broadcasted_iota(jnp.int32, (1, LANES), 1) < HALF
 
     def gather(i):
         start = pl.multiple_of(i * LANES, LANES)
         for k in range(LANES):
-            first = low_rows[pl.ds(table[i, k], 1), :]
-            second = high_rows[pl.ds(table[i + GROUPS // 2, k], 1), :]
+            first = wide_rows[pl.ds(table[i, k], 1), :]
+            second = wide_rows[pl.ds(table[i + GROUPS // 2, k], 1), :]
             own[pl.ds(start + k, 1), :] = jnp.where(low_lane, first, second)
-            weight[pl.ds(start + k, 1), :] = jnp.where(low_lane, second, first)
+
+    def weigh(i, carry):
+        def weights(at):
+            row = table_vector[pl.ds(at, 1), :] & (ROWS - 1)
+            shared = ((row < PLANE) | (row == CORNERS)) & (space > 0)
+            return jnp.broadcast_to(jnp.where(shared | (row >= CORNERS + 5), 0.0, 1.0), (HALF, LANES))
+
+        both = jnp.concatenate([weights(i), weights(i + GROUPS // 2)], axis=0)
+        weight[pl.ds(pl.multiple_of(i * LANES, LANES), LANES), :] = both.T
+        return carry
 
     half = PAIRS // 2
     size = half // PIECES
@@ -698,7 +721,8 @@
         send(cross.at[piece_rows(chip, p)], partner_cross.at[piece_rows(chip, p)], again_sems, p, to_mate)
         for p in pieces
     ]
-    pair = send(own, partner, pair_sems, 0, to_mate)
+    halves = [pl.ds(pl.multiple_of(side * half, half), half) for side in (chip, 1 - chip)]
+    pair = [send(own.at[rows], partner.at[rows], pair_sems, k, to_mate) for k, rows in enumerate(halves)]
 
     groups = GROUPS // 4
     per_piece = groups // PIECES
@@ -707,19 +731,24 @@
         base = chip * groups + p * per_piece
         lax.fori_loop(0, per_piece, lambda i, carry, base=base: (gather(base + i), carry)[1], 0)
         first[p].start()
-    lax.fori_loop(0, groups, lambda i, carry: (gather((1 - chip) * groups + i), carry)[1], 0)
-    pair.start()
-    pair.wait()
+    for p in pieces:
+        base = (1 - chip) * groups + p * per_piece
+        lax.fori_loop(0, per_piece, lambda i, carry, base=base: (gather(base + i), carry)[1], 0)
+        if p == 0:
+            second[0].start()
+            pair[0].start()
+    pair[1].start()
+    lax.fori_loop(0, GROUPS // 2, weigh, 0)
 
     def products(left, right):
-        left_high, left_low = split(left)
-        right_high, right_low = split(right)
-        return lax.dot_general(
-            jnp.concatenate([left_high, left_high, left_low], axis=0),
-            jnp.concatenate([right_high, right_low, right_high], axis=0),
+        both = lax.dot_general(
+            jnp.concatenate(split(left), axis=1),
+            jnp.concatenate(split(right), axis=1),
             (((0,), (0,)), ((), ())),
             preferred_element_type=jnp.float32,
         )
+        upper = both[:LANES, : 2 * LANES] + both[:LANES, 2 * LANES :]
+        return upper + (both[LANES:, : 2 * LANES] + both[LANES:, 2 * LANES :])
 
     def block_rows(i):
         return pl.ds(pl.multiple_of(i * BLOCK, BLOCK), BLOCK)
@@ -727,12 +756,12 @@
     def own_terms(i, total):
         rows = block_rows(i)
         mine = own[rows, :]
-        scale = pltpu.roll(weight[rows, :], HALF, 1)
+        scale = weight[rows, :]
         return total + products(mine * scale, jnp.concatenate([mine, partner[rows, :]], axis=1))
 
     def cross_terms(i, total):
         rows = block_rows(i)
-        scale = pltpu.roll(weight[rows, :], HALF, 1)
+        scale = weight[rows, :]
         return total + products(
             cross[rows, :], jnp.concatenate([own[rows, :] * scale, partner[rows, :] * scale], axis=1)
         )
@@ -746,7 +775,14 @@
         return jnp.where(low_half, left, right)
 
     zero = jnp.zeros((LANES, 2 * LANES), jnp.float32)
-    sums[0:BANDS_DEV, :] = fold(lax.fori_loop(0, PAIRS // BLOCK, own_terms, zero))
+    per_half = half // BLOCK
+    total = zero
+    for k, side in enumerate((chip, 1 - chip)):
+        pair[k].wait()
+        total = lax.fori_loop(
+            0, per_half, lambda i, total, side=side: own_terms(side * per_half + i, total), total
+        )
+    sums[0:BANDS_DEV, :] = fold(total)
     blocks = size // BLOCK
     total = zero
     for p in pieces:
@@ -756,7 +792,6 @@
         total = lax.fori_loop(0, blocks, lambda i, total, base=base: cross_terms(base + i, total), total)
     sums[BANDS_DEV : 2 * BANDS_DEV, :] = fold(total)
 
-    second[0].start()
 
     def rows_of(at):
         return pl.ds(pl.multiple_of(8 * at, 8), 8)
@@ -834,12 +869,6 @@
                 inverse[i, j] = jnp.concatenate([whole[i, j], padding], axis=1)
             else:
                 inverse[i, j] = jnp.zeros((BANDS_DEV, LANES), jnp.float32)
-    for p in pieces[1:]:
-        second[p].wait()
-        forward_second[p].start()
-    for p in pieces:
-        forward_first[p].wait()
-
     panels = [inverse[band, source] for source in (band, mate, across, across_mate)]
     left = jnp.concatenate(
         [
@@ -849,28 +878,37 @@
         axis=0,
     )
     left_high, left_low = split(left)
-    left = jnp.concatenate([left_high, left_high, left_low], axis=1)
+    left = jnp.concatenate(
+        [jnp.concatenate([left_high, left_high], axis=1), jnp.concatenate([left_low, left_low], axis=1)], axis=0
+    )
 
     def rotate(i, carry):
         rows = block_rows(i)
         right = jnp.concatenate([ref[rows, :] for ref in (own, partner, cross, partner_cross)], axis=1)
-        right_high, right_low = split(right)
-        rotated = lax.dot_general(
+        both = lax.dot_general(
             left,
-            jnp.concatenate([right_high, right_low, right_high], axis=1),
+            jnp.concatenate(split(right), axis=1),
             (((1,), (1,)), ((), ())),
             preferred_element_type=jnp.float32,
         )
+        rotated = both[: 2 * BANDS_DEV] + both[2 * BANDS_DEV :]
         out[:, rows] = rotated[:BANDS_DEV]
         out[:, pl.ds(pl.multiple_of(PAIRS + i * BLOCK, BLOCK), BLOCK)] = rotated[BANDS_DEV:]
         return carry
 
-    done = (1 - chip) * (half // BLOCK)
-    lax.fori_loop(0, half // BLOCK, lambda i, carry: rotate(done + i, carry), 0)
+    def rotate_piece(side, p):
+        base = side * per_half + p * blocks
+        lax.fori_loop(0, blocks, lambda i, carry: rotate(base + i, carry), 0)
+
+    for p in pieces:
+        forward_first[p].wait()
+        rotate_piece(1 - chip, p)
+        if p > 0:
+            second[p].wait()
+            forward_second[p].start()
     for p in pieces:
         forward_second[p].wait()
-        base = chip * (half // BLOCK) + p * blocks
-        lax.fori_loop(0, blocks, lambda i, carry, base=base: rotate(base + i, carry), 0)
+        rotate_piece(chip, p)
 
 
 def finish(cells, table, owned_count):
@@ -886,21 +924,23 @@
     return pl.pallas_call(
         functools.partial(finish_kernel, owned_count),
         out_shape=jax.ShapeDtypeStruct((BANDS_DEV, 2 * PAIRS), jnp.float32),
-        in_specs=[whole, whole],
+        in_specs=[pl.BlockSpec(memory_space=pltpu.MemorySpace.HBM), whole],
         out_specs=whole,
         scratch_shapes=[
             pltpu.SMEM(table.shape, jnp.int32),
-            small(2 * TILES * ROWS, LANES), small(2 * TILES * ROWS, LANES),
+            small(TILES, ROWS, LANES),
+            small(2 * TILES * ROWS, LANES),
             nodes, nodes, nodes, nodes, nodes,
             small(LANES, LANES), small(PLANE_PEERS - 1, 8, LANES), small(8, LANES), small(8, LANES),
             small(PLANE_PEERS, N_BAND, 8, LANES),
             small(N_BAND, N_BAND, BANDS_DEV, LANES),
             pltpu.SemaphoreType.DMA(()),
-            sems(1), sems(PIECES), sems(PIECES), sems(PIECES), sems(PIECES),
+            pltpu.SemaphoreType.DMA((CELL_PARTS,)),
+            sems(2), sems(PIECES), sems(PIECES), sems(PIECES), sems(PIECES),
             sems(PLANE_PEERS - 1), sems(1), sems(3), sems(PLANE_PEERS - 1),
         ],
         compiler_params=pltpu.CompilerParams(
-            collective_id=1, has_side_effects=True, vmem_limit_bytes=56 * 2**20
+            collective_id=1, has_side_effects=True, vmem_limit_bytes=48 * 2**20
         ),
         name="finish",
     )(cells, table)

time: 186 us -> 176 us (0.946)
  Pallas kernels: 181 us -> 172 us
    pallas_call x1, Pallas kernels: 85.1 us -> 80.3 us  [finish(): pl.pallas_call(functools.partial(finish_kernel, owned_count), out_shape=j...]
    pallas_call x1, Pallas kernels: 92.4 us -> 88.2 us  [filter_cells(): pl.pallas_call(filter_kernel, out_shape=(jax.ShapeDtypeStruct(cells, jnp....]
    unnamed x2 -> x4, local copies, waits for them, and re-layouts: 4.97 us -> 3.82 us
where the time goes in v6:
time: 176 us; the launch traced here: 175 us
  Pallas kernels  172 us (98%)
  local copies, waits for them, and re-layouts  3.82 us (2%)
    pallas_call x1, Pallas kernels, filter_cells(): pl.pallas_call(filter_kernel, out_shape=(jax.ShapeDtypeStruct(cells, jnp....  88.2 us
    pallas_call x1, Pallas kernels, finish(): pl.pallas_call(functools.partial(finish_kernel, owned_count), out_shape=j...  80.3 us
    unnamed x4, local copies, waits for them, and re-layouts  3.82 us

profile of v6, /device:TPU:1, one launch (start us, length us, event | category | flops | bytes accessed | tf_op | source)
XLA Modules:
  0.0 175.3 jit_solution(7733995307749488908)
XLA Ops:
  0.0 1.6 copy.10.conn_ref
  1.6 3.1 %layout.1 = (s32[125,120]{1,0:T(8,128)}, s32[128,128]{1,0:T(8,128)}, f32[60,128]{1,0:T(8,128)}, f32[60,128]{1,0:T(8,128)}, bf16[256,256]{1,0:T(8,128)(2,1)}) custom-call(s32[125,120]{1,0:T(8,128)} %copy.10.conn_ref, f32[1,120]{1,0:T(1,128)} %bitcast.4, f32[1,120]{1,0:T(1,128)} %bitcast.5, f32[125,125]{1,0:T(8,128)} %stiff_ref.1, ...), custom_call_target="tpu_custom_call" | custom-call | tf_op jit(solution)/shard_map/layout/pallas_call | solution.py:173
  4.7 88.2 %filter_cells.1 = (f32[66,128,128]{2,1,0:T(8,128)}, s32[80,128]{1,0:T(8,128)}) custom-call(s32[125,120]{1,0:T(8,128)} %get-tuple-element.12.index_vector_ref, s32[128,128]{1,0:T(8,128)} %get-tuple-element.13.keys_ref, f32[128,128]{1,0:T(8,128)} %constant.10.clone.codes_ref, f32[64,10125]{1,0:T(8,128)} %waves_ref.1, ...), custom_call_target="tpu_custom_call" | custom-call | tf_op jit(solution)/shard_map/filter_cells/pallas_call | solution.py:554
  92.8 0.0 copy-start
  92.8 0.8 copy-done
  93.6 80.3 %finish.1 = f32[64,10240]{1,0:T(8,128)S(1)} custom-call(f32[66,128,128]{2,1,0:T(8,128)} %get-tuple-element.17.far_cells, s32[80,128]{1,0:T(8,128)S(1)} %copy-done), custom_call_target="tpu_custom_call" | custom-call | tf_op jit(solution)/shard_map/finish/pallas_call | solution.py:924
  173.9 1.5 copy.12
Async XLA Ops:
  92.8 0.8 copy-start

commit v7 on v6

--- a/solution.py
+++ b/solution.py
@@ -466,7 +466,9 @@
     )
     doubled[whole_blocks * LANES : (whole_blocks + 1) * LANES, :] = jnp.concatenate([block, block], axis=0).T
 
-    out_ref[...] = jnp.zeros_like(out_ref)
+    unused = jnp.zeros((TILES + CELLS_Z, ROWS - CORNERS, LANES), jnp.float32)
+    out_ref[:, CORNERS:, :] = unused
+    other[:, CORNERS:, :] = unused
     low_row = lax.broadcasted_iota(jnp.int32, (1, LANES), 1) < HALF
 
     def gather(t, nodes, halves):
@@ -484,7 +486,6 @@
 
     over_chunks(send_owner)
     each_node_once((0, 1, 2, 3), gather)
-    other[...] = jnp.zeros_like(other)
 
     def take_owner(c):
         finish_copy(message(0, 0, c), 0)
@@ -494,55 +495,50 @@
             for g in range(3):
                 out_ref[t, group(bottom, g), :] = jnp.where(has_below, arrived[g], out_ref[t, group(bottom, g), :])
 
-    over_chunks(take_owner)
-    finish_copy(edge_message(0, 0), 0)
-    for z in range(CELLS_Z):
-        t = TILES - CELLS_Z + z
-        out_ref[t, group(bottom, 1), :] = jnp.where(
-            along_y & has_below, edge_receives[0, 0, z], out_ref[t, group(bottom, 1), :]
-        )
-    out_ref[last_tile, corners, :] = jnp.where(
-        (sub == bottom) & has_below, unpack_corner(0, 0), out_ref[last_tile, corners, :]
-    )
-    over_chunks(lambda c: fill(out_ref, c))
-
-    multiply(out_ref, CHUNKS - 1)
-
-    def first_step(c):
-        multiply(out_ref, c)
-        assemble(0, c)
-
-    lax.fori_loop(0, CHUNKS - 1, lambda c, carry: (first_step(c), carry)[1], 0)
-    assemble(0, CHUNKS - 1)
-    tabulate(0)
-
-    for step in range(1, FILTER_DEG):
-        base = step - 1
+        @pl.when(c == CHUNKS - 1)
+        def _():
+            finish_copy(edge_message(0, 0), 0)
+            for z in range(CELLS_Z):
+                t = TILES - CELLS_Z + z
+                out_ref[t, group(bottom, 1), :] = jnp.where(
+                    along_y & has_below, edge_receives[0, 0, z], out_ref[t, group(bottom, 1), :]
+                )
+            out_ref[last_tile, corners, :] = jnp.where(
+                (sub == bottom) & has_below, unpack_corner(0, 0), out_ref[last_tile, corners, :]
+            )
+
+    for step in range(FILTER_DEG):
         current = buffers(step)[0]
+
+        def arrive(c):
+            if step == 0:
+                take_owner(c)
+            else:
+                advance_faces(step - 1, c)
 
         def refresh(c):
             fill(current, c)
             multiply(current, c)
 
         def next_chunk(i, carry):
-            advance_faces(step - 1, lax.rem(base + i, CHUNKS))
-            c = lax.rem(base + i - 1, CHUNKS)
+            arrive(lax.rem(step + i, CHUNKS))
+            c = lax.rem(step + i - 1, CHUNKS)
             refresh(c)
             assemble(step, c)
             return carry
 
-        advance_faces(step - 1, base)
-        advance_faces(step - 1, base + 1)
-        refresh(base)
+        arrive(step)
+        arrive(step + 1)
+        refresh(step)
         lax.fori_loop(2, CHUNKS, next_chunk, 0)
-        refresh((base + CHUNKS - 1) % CHUNKS)
-        assemble(step, (base + CHUNKS - 1) % CHUNKS)
-        assemble(step, base)
+        refresh((step + CHUNKS - 1) % CHUNKS)
+        assemble(step, (step + CHUNKS - 1) % CHUNKS)
+        assemble(step, step)
         tabulate(step)
 
-    last = FILTER_DEG - 1
+    last = FILTER_DEG
     lax.fori_loop(
-        0, CHUNKS, lambda i, carry: (advance_faces(last, lax.rem(last + i, CHUNKS)), carry)[1], 0
+        0, CHUNKS, lambda i, carry: (advance_faces(last - 1, lax.rem(last + i, CHUNKS)), carry)[1], 0
     )
 
 

time: 176 us -> 171 us (0.972)
  Pallas kernels: 172 us -> 166 us
    pallas_call x1, Pallas kernels: 88.2 us -> 85.1 us  [filter_cells(): pl.pallas_call(filter_kernel, out_shape=(jax.ShapeDtypeStruct(cells, jnp....]
    pallas_call x1, Pallas kernels: 80.3 us -> 78.2 us  [finish(): pl.pallas_call(functools.partial(finish_kernel, owned_count), out_shape=j...]
where the time goes in v7:
time: 171 us; the launch traced here: 170 us
  Pallas kernels  166 us (97%)
  local copies, waits for them, and re-layouts  3.82 us (2%)
    pallas_call x1, Pallas kernels, filter_cells(): pl.pallas_call(filter_kernel, out_shape=(jax.ShapeDtypeStruct(cells, jnp....  85.1 us
    pallas_call x1, Pallas kernels, finish(): pl.pallas_call(functools.partial(finish_kernel, owned_count), out_shape=j...  78.2 us
    unnamed x4, local copies, waits for them, and re-layouts  3.82 us

profile of v7, /device:TPU:1, one launch (start us, length us, event | category | flops | bytes accessed | tf_op | source)
XLA Modules:
  0.0 170.3 jit_solution(13999133557597878801)
XLA Ops:
  0.0 1.6 copy.10.conn_ref
  1.6 3.1 %layout.1 = (s32[125,120]{1,0:T(8,128)}, s32[128,128]{1,0:T(8,128)}, f32[60,128]{1,0:T(8,128)}, f32[60,128]{1,0:T(8,128)}, bf16[256,256]{1,0:T(8,128)(2,1)}) custom-call(s32[125,120]{1,0:T(8,128)} %copy.10.conn_ref, f32[1,120]{1,0:T(1,128)} %bitcast.4, f32[1,120]{1,0:T(1,128)} %bitcast.5, f32[125,125]{1,0:T(8,128)} %stiff_ref.1, ...), custom_call_target="tpu_custom_call" | custom-call | tf_op jit(solution)/shard_map/layout/pallas_call | solution.py:173
  4.7 85.1 %filter_cells.1 = (f32[66,128,128]{2,1,0:T(8,128)}, s32[80,128]{1,0:T(8,128)}) custom-call(s32[125,120]{1,0:T(8,128)} %get-tuple-element.12.index_vector_ref, s32[128,128]{1,0:T(8,128)} %get-tuple-element.13.keys_ref, f32[128,128]{1,0:T(8,128)} %constant.10.clone.codes_ref, f32[64,10125]{1,0:T(8,128)} %waves_ref.1, ...), custom_call_target="tpu_custom_call" | custom-call | tf_op jit(solution)/shard_map/filter_cells/pallas_call | solution.py:550
  89.8 0.0 copy-start
  89.8 0.8 copy-done
  90.5 78.2 %finish.1 = f32[64,10240]{1,0:T(8,128)S(1)} custom-call(f32[66,128,128]{2,1,0:T(8,128)} %get-tuple-element.17.far_cells, s32[80,128]{1,0:T(8,128)S(1)} %copy-done), custom_call_target="tpu_custom_call" | custom-call | tf_op jit(solution)/shard_map/finish/pallas_call | solution.py:920
  168.8 1.5 copy.12
Async XLA Ops:
  89.8 0.8 copy-start

commit v8 on v7

--- a/solution.py
+++ b/solution.py
@@ -815,10 +815,10 @@
     ]
     for step in to_band:
         step.start()
+    for p in pieces[1:]:
+        second[p].start()
     for step in to_band:
         step.wait()
-    for p in pieces[1:]:
-        second[p].start()
     back = [send(everyone.at[at_plane], everyone.at[at_plane], back_sems, k - 1, plane_peer(k)) for k in others]
     for step in back:
         step.start()

time: 171 us -> 166 us (0.971)
  Pallas kernels: 166 us -> 162 us
    pallas_call x1, Pallas kernels: 78.2 us -> 73.4 us  [finish(): pl.pallas_call(functools.partial(finish_kernel, owned_count), out_shape=j...]
where the time goes in v8:
time: 166 us; the launch traced here: 165 us
  Pallas kernels  162 us (98%)
  local copies, waits for them, and re-layouts  3.82 us (2%)
    pallas_call x1, Pallas kernels, filter_cells(): pl.pallas_call(filter_kernel, out_shape=(jax.ShapeDtypeStruct(cells, jnp....  85.1 us
    pallas_call x1, Pallas kernels, finish(): pl.pallas_call(functools.partial(finish_kernel, owned_count), out_shape=j...  73.4 us
    unnamed x4, local copies, waits for them, and re-layouts  3.82 us

profile of v8, /device:TPU:1, one launch (start us, length us, event | category | flops | bytes accessed | tf_op | source)
XLA Modules:
  0.0 165.4 jit_solution(13456761463880253062)
XLA Ops:
  0.0 1.6 copy.10.conn_ref
  1.6 3.1 %layout.1 = (s32[125,120]{1,0:T(8,128)}, s32[128,128]{1,0:T(8,128)}, f32[60,128]{1,0:T(8,128)}, f32[60,128]{1,0:T(8,128)}, bf16[256,256]{1,0:T(8,128)(2,1)}) custom-call(s32[125,120]{1,0:T(8,128)} %copy.10.conn_ref, f32[1,120]{1,0:T(1,128)} %bitcast.4, f32[1,120]{1,0:T(1,128)} %bitcast.5, f32[125,125]{1,0:T(8,128)} %stiff_ref.1, ...), custom_call_target="tpu_custom_call" | custom-call | tf_op jit(solution)/shard_map/layout/pallas_call | solution.py:173
  4.7 85.1 %filter_cells.1 = (f32[66,128,128]{2,1,0:T(8,128)}, s32[80,128]{1,0:T(8,128)}) custom-call(s32[125,120]{1,0:T(8,128)} %get-tuple-element.12.index_vector_ref, s32[128,128]{1,0:T(8,128)} %get-tuple-element.13.keys_ref, f32[128,128]{1,0:T(8,128)} %constant.10.clone.codes_ref, f32[64,10125]{1,0:T(8,128)} %waves_ref.1, ...), custom_call_target="tpu_custom_call" | custom-call | tf_op jit(solution)/shard_map/filter_cells/pallas_call | solution.py:550
  89.8 0.0 copy-start
  89.8 0.8 copy-done
  90.5 73.4 %finish.1 = f32[64,10240]{1,0:T(8,128)S(1)} custom-call(f32[66,128,128]{2,1,0:T(8,128)} %get-tuple-element.17.far_cells, s32[80,128]{1,0:T(8,128)S(1)} %copy-done), custom_call_target="tpu_custom_call" | custom-call | tf_op jit(solution)/shard_map/finish/pallas_call | solution.py:920
  163.9 1.5 copy.12
Async XLA Ops:
  89.8 0.8 copy-start

commit v9 on v8

--- a/solution.py
+++ b/solution.py
@@ -734,6 +734,7 @@
             second[0].start()
             pair[0].start()
     pair[1].start()
+    second[1].start()
     lax.fori_loop(0, GROUPS // 2, weigh, 0)
 
     def products(left, right):
@@ -815,7 +816,7 @@
     ]
     for step in to_band:
         step.start()
-    for p in pieces[1:]:
+    for p in pieces[2:]:
         second[p].start()
     for step in to_band:
         step.wait()

time: 166 us -> 167 us (level)
  no operation moved by 1% of the time
where the time goes in v9:
time: 167 us
  Pallas kernels  163 us (98%)
  local copies, waits for them, and re-layouts  3.82 us (2%)
    pallas_call x1, Pallas kernels, filter_cells(): pl.pallas_call(filter_kernel, out_shape=(jax.ShapeDtypeStruct(cells, jnp....  85.1 us
    pallas_call x1, Pallas kernels, finish(): pl.pallas_call(functools.partial(finish_kernel, owned_count), out_shape=j...  74.7 us
    unnamed x4, local copies, waits for them, and re-layouts  3.82 us

profile of v9, /device:TPU:1, one launch (start us, length us, event | category | flops | bytes accessed | tf_op | source)
XLA Modules:
  0.0 166.7 jit_solution(16319257344688333409)
XLA Ops:
  0.0 1.6 copy.10.conn_ref
  1.6 3.1 %layout.1 = (s32[125,120]{1,0:T(8,128)}, s32[128,128]{1,0:T(8,128)}, f32[60,128]{1,0:T(8,128)}, f32[60,128]{1,0:T(8,128)}, bf16[256,256]{1,0:T(8,128)(2,1)}) custom-call(s32[125,120]{1,0:T(8,128)} %copy.10.conn_ref, f32[1,120]{1,0:T(1,128)} %bitcast.4, f32[1,120]{1,0:T(1,128)} %bitcast.5, f32[125,125]{1,0:T(8,128)} %stiff_ref.1, ...), custom_call_target="tpu_custom_call" | custom-call | tf_op jit(solution)/shard_map/layout/pallas_call | solution.py:173
  4.7 85.1 %filter_cells.1 = (f32[66,128,128]{2,1,0:T(8,128)}, s32[80,128]{1,0:T(8,128)}) custom-call(s32[125,120]{1,0:T(8,128)} %get-tuple-element.12.index_vector_ref, s32[128,128]{1,0:T(8,128)} %get-tuple-element.13.keys_ref, f32[128,128]{1,0:T(8,128)} %constant.10.clone.codes_ref, f32[64,10125]{1,0:T(8,128)} %waves_ref.1, ...), custom_call_target="tpu_custom_call" | custom-call | tf_op jit(solution)/shard_map/filter_cells/pallas_call | solution.py:550
  89.8 0.0 copy-start
  89.8 0.8 copy-done
  90.5 74.7 %finish.1 = f32[64,10240]{1,0:T(8,128)S(1)} custom-call(f32[66,128,128]{2,1,0:T(8,128)} %get-tuple-element.17.far_cells, s32[80,128]{1,0:T(8,128)S(1)} %copy-done), custom_call_target="tpu_custom_call" | custom-call | tf_op jit(solution)/shard_map/finish/pallas_call | solution.py:921
  165.2 1.5 copy.12
Async XLA Ops:
  89.8 0.8 copy-start
